TPU v7x, 32 devices: a whole 2x2x4 slice. The times are simulated.
32 devices in a mesh: snap: 2 (over y), pair: 4 (over z), ri: 4 (over x, core).
Axes of the slice: x: 2, y: 2, z: 4, core: 2. Of those that a mesh axis runs over, the one named last changes fastest.
Arguments:
- three_c: bfloat16 [32, 4, 64, 4096], P(('snap', 'pair'), 'ri'), parts along dimension 0, may hold values from -1.5 to 1.5
- green_occ: bfloat16 [32, 64, 64], P(('snap', 'pair')), parts along dimension 0, may hold values from -0.75 to 0.75
- green_virt: bfloat16 [32, 64, 64], P(('snap', 'pair')), parts along dimension 0, may hold values from -0.75 to 0.75
- pair_size: int32 [32], P(('snap', 'pair')), parts along dimension 0, may hold values from 16 to 64
- ri_ids: int32 [32, 4], P(('snap', 'pair')), parts along dimension 0, may hold values from 0 to 7, as said below
- coulomb: bfloat16 [1024, 512], P(('snap', 'pair', 'ri')), parts along dimension 0, may hold values from -0.25 to 0.25
Outputs:
- chi: float32 [1024, 512], P(('snap', 'pair', 'ri')), parts along dimension 0
- screen: float32 [1024, 512], P(('snap', 'pair', 'ri')), parts along dimension 0
There are 2 independent parts, one for each index of `snap`. A program takes and returns all parts, laid end to end along the dimension named above; each array names one. Nothing has to cross between parts.
Inputs may be any that keep to these rules, and one draw needn't show every extreme that they name: `ri_ids`: each row names 4 different RI blocks.
All inputs are finite; a program needn't handle non-finite values.
Results may differ from a plain program's by a relative error of at most 0.005.
Values may be sent and summed in bfloat16 or wider, within the bound.
No kernel may reach another device: no remote copies, remote signals or barrier semaphores. Data moves between devices by JAX's collectives and lax.ppermute only.
A program may use at most 128 MiB of HBM per device.

v0:
```python
import jax
import jax.numpy as jnp
from jax import lax
from jax.sharding import PartitionSpec as P


def block_products(blocks, occ, virt, sizes):
    pairs, kcount, rows, square = blocks.shape
    width = occ.shape[-1]
    shaped = blocks.reshape(pairs, kcount, rows, width, width)
    keep = (lax.broadcasted_iota(jnp.int32, (pairs, width), 1) < sizes[:, None]).astype(
        blocks.dtype
    )
    masked = shaped * keep[:, None, None, :, None]
    left = jnp.einsum("pkrmn,pnl->pkrml", masked, occ, preferred_element_type=jnp.float32).astype(
        jnp.bfloat16
    )
    right = jnp.einsum("pms,pkrsl->pkrml", virt, masked, preferred_element_type=jnp.float32).astype(
        jnp.bfloat16
    )
    return (left.reshape(pairs, kcount, rows, square), right.reshape(pairs, kcount, rows, square))


def pair_products(left, right):
    pairs, kcount, rows, square = left.shape
    flat_left = left.reshape(pairs, kcount * rows, square)
    flat_right = right.reshape(pairs, kcount * rows, square)
    pair_chi = jnp.einsum("pas,pbs->pab", flat_left, flat_right, preferred_element_type=jnp.float32)
    return pair_chi.reshape(pairs, kcount, rows, kcount, rows)


def shards(three_c, green_occ, green_virt, pair_size, ri_ids, coulomb):
    ri_count = lax.axis_size("ri")
    here = lax.axis_index("ri")
    own_pairs = three_c.shape[0] // ri_count
    first = here * own_pairs
    left_own, right_own = block_products(three_c, green_occ, green_virt, pair_size)
    left, right = (
        lax.all_to_all(left_own, "ri", split_axis=0, concat_axis=1, tiled=True),
        lax.all_to_all(right_own, "ri", split_axis=0, concat_axis=1, tiled=True),
    )
    picks = lax.dynamic_slice_in_dim(ri_ids, first, own_pairs, 0)
    kcount = picks.shape[1]
    blocks_ri = 2 * kcount
    rows = left.shape[2]
    total_rows = blocks_ri * rows
    block_ids = jnp.arange(blocks_ri, dtype=jnp.int32)
    onehot = (picks[:, :, None] == block_ids[None, None, :]).astype(jnp.float32)
    pair_chi = pair_products(left, right)
    half = jnp.einsum("pkr,pkalb->pralb", onehot, pair_chi, precision=lax.Precision.HIGHEST)
    whole = jnp.einsum("pralb,plt->ratb", half, onehot, precision=lax.Precision.HIGHEST)
    local_chi = whole.reshape(total_rows, total_rows)
    chi_rows = lax.psum_scatter(local_chi, ("pair", "ri"), scatter_dimension=0, tiled=True)
    chi_half = chi_rows.astype(jnp.bfloat16)
    screen = jnp.dot(
        chi_half,
        lax.all_gather(coulomb, ("pair", "ri"), axis=0, tiled=True),
        preferred_element_type=jnp.float32,
    )
    return (chi_rows, screen)


def solution(mesh):
    placed = (
        P(("snap", "pair"), "ri", None, None),
        P(("snap", "pair"), None, None),
        P(("snap", "pair"), None, None),
        P(("snap", "pair")),
        P(("snap", "pair"), None),
        P(("snap", "pair", "ri"), None),
    )
    return jax.shard_map(
        shards,
        mesh=mesh,
        in_specs=placed,
        out_specs=(P(("snap", "pair", "ri"), None), P(("snap", "pair", "ri"), None)),
        check_vma=False,
    )
```

profile of v0, /device:TPU:0, one launch (start us, length us, event | category | flops | bytes accessed | tf_op | source)
XLA Modules:
  0.0 167.1 jit_solution(10197483714811183885)
XLA Ops:
  7.2 0.0 copy-start
  7.2 7.0 %reshape.123 = bf16[4,64,64,64]{3,2,1,0:T(8,128)(2,1)} reshape(bf16[4,1,64,4096]{3,2,1,0:T(8,128)(2,1)} %param.6) | data formatting | bytes 4194304 | tf_op jit(solution)/shard_map/reshape | solution.py:10
  14.2 0.0 copy-start.3
  14.2 6.3 %copy.13 = bf16[4,64,64,64]{2,3,1,0:T(8,128)(2,1)} copy(bf16[4,64,64,64]{3,2,1,0:T(8,128)(2,1)} %reshape.123) | data formatting | bytes 4194304 | tf_op jit(solution)/shard_map/reshape | solution.py:10
  20.5 0.0 copy-done.3
  20.5 0.1 fusion.22
  20.6 0.0 copy-done
  20.6 5.7 %fusion.4 = bf16[4,64,64,64]{3,2,1,0:T(8,128)(2,1)} fusion(bf16[4,64,64,64]{2,3,1,0:T(8,128)(2,1)} %copy.13, bf16[4,64]{1,0:T(4,128)(2,1)S(1)} %fusion.22, bf16[4,64,64]{2,1,0:T(8,128)(2,1)S(1)} %copy-done), kind=kOutput, calls=%fused_computation.5 | convolution fusion | flops 136314880 | bytes 4227584 | tf_op jit(solution)/shard_map/pkrmn,pnl->pkrml/dot_general | solution.py:15
  26.3 0.0 copy-start.1
  26.3 6.7 %reshape.124 = bf16[4,1,64,4096]{3,2,0,1:T(8,128)(2,1)} reshape(bf16[4,64,64,64]{3,2,1,0:T(8,128)(2,1)} %fusion.4) | data formatting | bytes 4194304 | tf_op jit(solution)/shard_map/reshape | solution.py:21
  32.9 4.2 %all-to-all-start = ((bf16[4,1,64,4096]{3,2,1,0:T(8,128)(2,1)}), bf16[4,1,64,4096]{3,2,1,0:T(8,128)(2,1)S(1)}, u32[]{:S(2)}, u32[]{:S(2)}) async-start(bf16[4,1,64,4096]{3,2,1,0:T(8,128)(2,1)} %bitcast.6), calls=%async_computation | async-start | bytes 4194304 | tf_op jit(solution)/shard_map/all_to_all | solution.py:39
  37.1 0.0 copy-done.1
  37.1 5.4 %convert_bitcast_fusion = bf16[4,1,64,64,64]{3,4,2,0,1:T(8,128)(2,1)} fusion(bf16[4,64,64,64]{2,3,1,0:T(8,128)(2,1)} %copy.13, bf16[4,64]{1,0:T(4,128)(2,1)S(1)} %fusion.22, bf16[4,64,64]{2,1,0:T(8,128)(2,1)S(1)} %copy-done.1), kind=kOutput, calls=%fused_computation | convolution fusion | flops 136314880 | bytes 4227584 | tf_op jit(solution)/shard_map/pms,pkrsl->pkrml/dot_general | solution.py:18
  42.6 6.3 %copy.16 = bf16[4,1,64,64,64]{4,3,2,0,1:T(8,128)(2,1)} copy(bf16[4,1,64,64,64]{3,4,2,0,1:T(8,128)(2,1)} %convert_bitcast_fusion) | data formatting | bytes 4194304 | tf_op jit(solution)/shard_map/convert_element_type | solution.py:18
  48.9 6.6 %reshape.126 = bf16[4,1,64,4096]{3,2,0,1:T(8,128)(2,1)} reshape(bf16[4,1,64,64,64]{4,3,2,0,1:T(8,128)(2,1)} %copy.16) | data formatting | bytes 4194304 | tf_op jit(solution)/shard_map/reshape | solution.py:21
  55.5 7.4 %all-to-all-done = bf16[4,1,64,4096]{3,2,1,0:T(8,128)(2,1)S(1)} async-done(((bf16[4,1,64,4096]{3,2,1,0:T(8,128)(2,1)}), bf16[4,1,64,4096]{3,2,1,0:T(8,128)(2,1)S(1)}, u32[]{:S(2)}, u32[]{:S(2)}) %all-to-all-start) | async-done | bytes 2097184 | tf_op jit(solution)/shard_map/all_to_all | solution.py:39
  62.8 4.5 %all-to-all-start.1 = ((bf16[4,1,64,4096]{3,2,1,0:T(8,128)(2,1)}), bf16[4,1,64,4096]{3,2,1,0:T(8,128)(2,1)}, u32[]{:S(2)}, u32[]{:S(2)}) async-start(bf16[4,1,64,4096]{3,2,1,0:T(8,128)(2,1)} %bitcast.14), calls=%async_computation.1 | async-start | bytes 4194304 | tf_op jit(solution)/shard_map/all_to_all | solution.py:40
  67.3 0.0 reduce-scatter.2.cloned.1.call-start
  67.4 0.7 dynamic-slice_bitcast_fusion
  68.0 25.0 %all-to-all-done.1 = bf16[4,1,64,4096]{3,2,1,0:T(8,128)(2,1)} async-done(((bf16[4,1,64,4096]{3,2,1,0:T(8,128)(2,1)}), bf16[4,1,64,4096]{3,2,1,0:T(8,128)(2,1)}, u32[]{:S(2)}, u32[]{:S(2)}) %all-to-all-start.1) | async-done | bytes 2097184 | tf_op jit(solution)/shard_map/all_to_all | solution.py:40
  93.1 2.9 %fusion.9 = f32[4,64,4,64]{3,1,2,0:T(8,128)S(1)} fusion(bf16[4,1,64,4096]{3,2,1,0:T(8,128)(2,1)S(1)} %all-to-all-done, bf16[4,1,64,4096]{3,2,1,0:T(8,128)(2,1)} %all-to-all-done.1), kind=kOutput, calls=%fused_computation.6 | convolution fusion | flops 536870912 | bytes 4456448 | tf_op jit(solution)/shard_map/pas,pbs->pab/dot_general | solution.py:28
  95.9 0.0 copy-start.2
  95.9 1.0 fusion.15
  97.0 1.4 convolution_bitcast_fusion
  98.4 1.5 reshape.127
  99.9 0.0 reduce-scatter.2.cloned.1.call-update
  99.9 0.0 copy-done.2
  99.9 22.7 %all_gather.3 = bf16[512,512]{1,0:T(8,128)(2,1)S(1)} all-gather(bf16[32,512]{1,0:T(8,128)(2,1)S(1)} %copy-done.2), channel_id=1, replica_groups=mesh['snap'=2,'pair'=4,'ri'=4] {'pair','ri'}, dimensions={0}, use_global_device_ids=true | all-gather | bytes 557056 | tf_op jit(solution)/shard_map/all_gather | solution.py:57
  122.6 35.9 %reduce-scatter.2.cloned.1.call-done = f32[32,512]{1,0:T(8,128)} async-done(((f32[512,512]{1,0:T(8,128)}), f32[32,512]{1,0:T(8,128)}) %reduce-scatter.2.cloned.1.call-update) | async-done | bytes 65552 | tf_op jit(solution)/shard_map/reduce_scatter | solution.py:53
  158.6 1.7 fusion.19
Async XLA Ops:
  7.2 13.4 %copy-start = (bf16[4,64,64]{2,1,0:T(8,128)(2,1)S(1)}, bf16[4,64,64]{2,1,0:T(8,128)(2,1)}, u32[]{:S(2)}) copy-start(bf16[4,64,64]{2,1,0:T(8,128)(2,1)} %param.7) | copy-start | bytes 98308
  14.2 6.3 %copy-start.3 = (s32[4]{0:T(128)S(1)}, s32[4]{0:T(128)}, u32[]{:S(2)}) copy-start(s32[4]{0:T(128)} %param.9) | copy-start | bytes 52
  26.3 10.9 %copy-start.1 = (bf16[4,64,64]{2,1,0:T(8,128)(2,1)S(1)}, bf16[4,64,64]{2,1,0:T(8,128)(2,1)}, u32[]{:S(2)}) copy-start(bf16[4,64,64]{2,1,0:T(8,128)(2,1)} %param.8) | copy-start | bytes 98308
  32.9 29.9 %all-to-all-start = ((bf16[4,1,64,4096]{3,2,1,0:T(8,128)(2,1)}), bf16[4,1,64,4096]{3,2,1,0:T(8,128)(2,1)S(1)}, u32[]{:S(2)}, u32[]{:S(2)}) async-start(bf16[4,1,64,4096]{3,2,1,0:T(8,128)(2,1)} %bitcast.6), calls=%async_computation | async-start | bytes 4194304 | tf_op jit(solution)/shard_map/all_to_all | solution.py:39
  62.8 30.2 %all-to-all-start.1 = ((bf16[4,1,64,4096]{3,2,1,0:T(8,128)(2,1)}), bf16[4,1,64,4096]{3,2,1,0:T(8,128)(2,1)}, u32[]{:S(2)}, u32[]{:S(2)}) async-start(bf16[4,1,64,4096]{3,2,1,0:T(8,128)(2,1)} %bitcast.14), calls=%async_computation.1 | async-start | bytes 4194304 | tf_op jit(solution)/shard_map/all_to_all | solution.py:40
  67.3 91.3 %reduce-scatter.2.cloned.1.call-start = ((), (), s32[]{:S(2)}) async-start(), calls=%async_computation.3 | async-start | bytes 1114112 | tf_op jit(solution)/shard_map/reduce_scatter | solution.py:53
  95.9 4.0 %copy-start.2 = (bf16[32,512]{1,0:T(8,128)(2,1)S(1)}, bf16[32,512]{1,0:T(8,128)(2,1)}, u32[]{:S(2)}) copy-start(bf16[32,512]{1,0:T(8,128)(2,1)} %param.11) | copy-start | bytes 98308
Sparse Core Ops, SparseCore 0:
  100.0 58.4 reduce-scatter.1
where the time goes:
time: 168 us; the launch traced here: 167 us
  waiting for transfers between devices  68.3 us (41%)
  local copies, waits for them, and re-layouts  35 us (21%)
  blocking collectives  22.7 us (14%)
  matrix products  18.1 us (11%)
  between operations  14.1 us (8%)
  starting transfers between devices  8.7 us (5%)
    reduce_scatter x1, waiting for transfers between devices, shards(): lax.psum_scatter(local_chi, ('pair', 'ri'), scatter_dimension=0, tiled=True)  35.9 us
    all_to_all x1, waiting for transfers between devices, shards(): lax.all_to_all(right_own, 'ri', split_axis=0, concat_axis=1, tiled=True)  25 us
    all_gather x1, blocking collectives, shards(): lax.all_gather(coulomb, ('pair', 'ri'), axis=0, tiled=True)  22.7 us
    reshape x2, local copies, waits for them, and re-layouts, block_products(): shaped = blocks.reshape(pairs, kcount, rows, width, width)  13.3 us
    all_to_all x1, waiting for transfers between devices, shards(): lax.all_to_all(left_own, 'ri', split_axis=0, concat_axis=1, tiled=True)  7.37 us
    reshape x1, local copies, waits for them, and re-layouts, block_products(): left.reshape(pairs, kcount, rows, square)  6.65 us
    reshape x1, local copies, waits for them, and re-layouts, block_products(): right.reshape(pairs, kcount, rows, square)  6.61 us
    convert_element_type x1, local copies, waits for them, and re-layouts, block_products(): jnp.einsum('pms,pkrsl->pkrml', virt, masked, preferred_element_type=jnp.f...  6.3 us
  transfers between devices with their start and end apart: 3, of which 3 were waited for; matrix products, arithmetic and copies ran while one was open for 11% of the time, Pallas kernels for 0%

commit v1 on v0

v1 whole, which is shorter than its diff:
```python
import jax
import jax.numpy as jnp
from jax import lax
from jax.sharding import PartitionSpec as P


def block_products(blocks, occ, virt, size):
    kcount, rows, square = blocks.shape
    width = occ.shape[-1]
    keep = lax.broadcasted_iota(jnp.int32, (width, width), 0) < size
    keep = (keep & (lax.broadcasted_iota(jnp.int32, (width, width), 1) < size)).astype(blocks.dtype)
    shaped = blocks.reshape(kcount, rows, width, width)
    left = jnp.einsum("krmn,nl->krml", shaped, occ, preferred_element_type=jnp.float32)
    right = jnp.einsum("ms,krsl->krml", virt * keep, shaped, preferred_element_type=jnp.float32)
    left = left.astype(jnp.bfloat16).reshape(kcount * rows, square)
    right = right.astype(jnp.bfloat16).reshape(kcount * rows, square)
    return left, right


def swap(array, axes, step):
    count = lax.axis_size(axes)
    return lax.ppermute(array, axes, [(i, i ^ step) for i in range(count)])


def shards(three_c, green_occ, green_virt, pair_size, ri_ids, coulomb):
    everyone = ("pair", "ri")
    ri_count = lax.axis_size("ri")
    devices = lax.axis_size(everyone)
    here = lax.axis_index("ri")
    kcount = ri_ids.shape[1]
    rows = three_c.shape[2]
    blocks_ri = 2 * kcount
    out_rows = coulomb.shape[0]

    own = lax.dynamic_index_in_dim(three_c, here, 0, keepdims=False)
    parts = [own]
    for step in range(1, ri_count):
        part = lax.dynamic_index_in_dim(three_c, here ^ step, 0, keepdims=False)
        parts.append(swap(part, "ri", step))
    pick = lambda array: lax.dynamic_index_in_dim(array, here, 0, keepdims=False)
    occ, virt, size, ids = pick(green_occ), pick(green_virt), pick(pair_size), pick(ri_ids)
    left, right = block_products(jnp.concatenate(parts, 0), occ, virt, size)
    chi = jnp.dot(left, right.T, preferred_element_type=jnp.float32)

    order = here ^ jnp.arange(kcount, dtype=jnp.int32)
    ids = ids[order]
    block_ids = jnp.arange(blocks_ri, dtype=jnp.int32)
    onehot = (ids[:, None] == block_ids[None, :]).astype(jnp.bfloat16)
    chi = chi.astype(jnp.bfloat16).reshape(kcount, rows, kcount * rows)
    spread = jnp.einsum("kr,kac->rac", onehot, chi).reshape(devices, out_rows, kcount * rows)
    got = lax.all_to_all(spread, everyone, 0, 0, tiled=True)
    all_ids = lax.all_gather(ids, everyone)
    onehots = (all_ids[:, :, None] == block_ids[None, None, :]).astype(jnp.float32)
    got = got.astype(jnp.float32).reshape(devices, out_rows, kcount, rows)
    chi_rows = jnp.einsum("drkq,dkt->rtq", got, onehots, precision=lax.Precision.HIGHEST)
    chi_rows = chi_rows.reshape(out_rows, blocks_ri * rows)
    metric = lax.all_gather(coulomb, everyone, axis=0, tiled=True)
    screen = jnp.dot(chi_rows.astype(jnp.bfloat16), metric, preferred_element_type=jnp.float32)
    return chi_rows, screen


def solution(mesh):
    placed = (
        P(("snap", "pair"), "ri", None, None),
        P(("snap", "pair"), None, None),
        P(("snap", "pair"), None, None),
        P(("snap", "pair")),
        P(("snap", "pair"), None),
        P(("snap", "pair", "ri"), None),
    )

    def inner(three_c, *rest):
        return shards(three_c[:, 0][:, None], *rest)

    return jax.shard_map(
        inner,
        mesh=mesh,
        in_specs=placed,
        out_specs=(P(("snap", "pair", "ri"), None), P(("snap", "pair", "ri"), None)),
        check_vma=False,
    )
```

time: 168 us -> 107 us (0.64)
  waiting for transfers between devices: 68.3 us -> 13.6 us
  between operations: 14.1 us -> 1.44 us
  blocking collectives: 22.7 us -> 31.8 us
  matrix products: 18.1 us -> 14.8 us
    reduce_scatter x1 -> x0, waiting for transfers between devices: 35.9 us -> none  [shards(): lax.psum_scatter(local_chi, ('pair', 'ri'), scatter_dimension=0, tiled=True)]
    all_to_all x2 -> x1, waiting for transfers between devices: 32.4 us -> 0.01 us  [shards(): got = lax.all_to_all(spread, everyone, 0, 0, tiled=True)]
    reshape x5 -> x4, local copies, waits for them, and re-layouts: 28 us -> 12.6 us  [the longest x1 6.61 us: block_products(): right = right.astype(jnp.bfloat16).reshape(kcount * rows, square)]
    ppermute x0 -> x3, waiting for transfers between devices: none -> 13.6 us  [swap(): return lax.ppermute(array, axes, [(i, i ^ step) for i in range(count)])]
    unnamed x0 -> x1, blocking collectives: none -> 12.4 us
    concatenate x0 -> x5, local copies, waits for them, and re-layouts: none -> 6.48 us  [shards(): left, right = block_products(jnp.concatenate(parts, 0), occ, virt, size)]
    unnamed x8 -> x16, local copies, waits for them, and re-layouts: 0.02 us -> 4.04 us
    squeeze x0 -> x2, local copies, waits for them, and re-layouts: none -> 3.38 us  [the longest x1 2.69 us: shards(): part = lax.dynamic_index_in_dim(three_c, here ^ step, 0, keepdims=False)]
  transfers between devices with their start and end apart: 3 -> 4, of which waited for: 3 -> 2; matrix products, arithmetic and copies ran while one was open for 11% -> 10% of each run, Pallas kernels for 0% -> 0%
where the time goes in v1:
time: 107 us; the launch traced here: 106 us
  local copies, waits for them, and re-layouts  35 us (33%)
  blocking collectives  31.8 us (30%)
  matrix products  14.8 us (14%)
  waiting for transfers between devices  13.6 us (13%)
  starting transfers between devices  9.05 us (8%)
  between operations  1.44 us (1%)
    all_gather x1, blocking collectives, shards(): metric = lax.all_gather(coulomb, everyone, axis=0, tiled=True)  19.4 us
    ppermute x3, waiting for transfers between devices, swap(): return lax.ppermute(array, axes, [(i, i ^ step) for i in range(count)])  13.6 us
    unnamed x1, blocking collectives  12.4 us
    reshape x1, local copies, waits for them, and re-layouts, block_products(): right = right.astype(jnp.bfloat16).reshape(kcount * rows, square)  6.61 us
    concatenate x5, local copies, waits for them, and re-layouts, shards(): left, right = block_products(jnp.concatenate(parts, 0), occ, virt, size)  6.48 us
    convert_element_type x1, local copies, waits for them, and re-layouts, block_products(): right = right.astype(jnp.bfloat16).reshape(kcount * rows, square)  6.3 us
    all_to_all x1, starting transfers between devices, shards(): got = lax.all_to_all(spread, everyone, 0, 0, tiled=True)  5.96 us
    reshape x1, local copies, waits for them, and re-layouts, block_products(): left = left.astype(jnp.bfloat16).reshape(kcount * rows, square)  5.66 us
  transfers between devices with their start and end apart: 4, of which 2 were waited for; matrix products, arithmetic and copies ran while one was open for 10% of the time, Pallas kernels for 0%

profile of v1, /device:TPU:0, one launch (start us, length us, event | category | flops | bytes accessed | tf_op | source)
XLA Modules:
  0.0 106.3 jit_solution(12817918294668977035)
XLA Ops:
  0.7 2.7 %dynamic-slice_bitcast_fusion = (bf16[1,64,4096]{2,1,0:T(8,128)(2,1)}, bf16[1,64,4096]{2,1,0:T(8,128)(2,1)}, bf16[1,1,64,4096]{3,2,1,0:T(8,128)(2,1)S(1)}, bf16[1,64,4096]{2,1,0:T(8,128)(2,1)}) fusion(bf16[4,1,64,4096]{3,2,1,0:T(8,128)(2,1)} %param.6, s32[]{:T(128)S(6)} %select_n.34, s32[]{:T(128)S(6)} %select_n.32, s32[]{:T(128)S(6)} %select_n.30, ...), kind=kLoop, calls=%fused_computation.6 | loop fusion | bytes 4194320 | tf_op jit(solution)/shard_map/jit(dynamic_index_in_dim)/squeeze | solution.py:38
  3.4 0.5 collective-permute-start
  3.8 2.5 %collective-permute-start.1 = (bf16[1,64,4096]{2,1,0:T(8,128)(2,1)}, bf16[1,64,4096]{2,1,0:T(8,128)(2,1)S(1)}, u32[]{:S(2)}, u32[]{:S(2)}) collective-permute-start(bf16[1,64,4096]{2,1,0:T(8,128)(2,1)} %get-tuple-element.5), channel_id=1, source_target_pairs={{0,2},{1,3},{2,0},{3,1},{4,6},{5,7},{6,4},{7,5},{8,10},{9,11},{10,... | collective-permute-start | bytes 1572872 | tf_op jit(solution)/shard_map/ppermute | solution.py:22
  6.5 1.1 %concatenate.12 = bf16[1,64,64,64]{3,2,1,0:T(8,128)(2,1)S(1)} reshape(bf16[1,1,64,4096]{3,2,1,0:T(8,128)(2,1)S(1)} %get-tuple-element.4) | data formatting | bytes 1048576 | tf_op jit(solution)/shard_map/concatenate | solution.py:42
  7.6 0.6 dynamic_slice.34
  8.2 0.7 fusion.22
  8.9 0.6 gather_fusion
  9.5 0.7 iota_compare_fusion.2
  10.2 1.0 constant_dynamic-update-slice_fusion.3
  11.2 2.1 %concatenate.13 = bf16[1,64,64,64]{3,2,1,0:T(8,128)(2,1)S(1)} reshape(bf16[1,64,4096]{2,1,0:T(8,128)(2,1)} %collective-permute-done) | data formatting | bytes 1048576 | tf_op jit(solution)/shard_map/concatenate | solution.py:42
  13.3 6.0 %collective-permute-done.1 = bf16[1,64,4096]{2,1,0:T(8,128)(2,1)S(1)} collective-permute-done((bf16[1,64,4096]{2,1,0:T(8,128)(2,1)}, bf16[1,64,4096]{2,1,0:T(8,128)(2,1)S(1)}, u32[]{:S(2)}, u32[]{:S(2)}) %collective-permute-start.1) | collective-permute-done | bytes 524320 | tf_op jit(solution)/shard_map/ppermute | solution.py:22
  19.3 1.1 %concatenate.14 = bf16[1,64,64,64]{3,2,1,0:T(8,128)(2,1)S(1)} reshape(bf16[1,64,4096]{2,1,0:T(8,128)(2,1)S(1)} %collective-permute-done.1) | data formatting | bytes 1048576 | tf_op jit(solution)/shard_map/concatenate | solution.py:42
  20.4 1.1 %constant_dynamic-update-slice_fusion.2 = bf16[4,64,64,64]{3,2,1,0:T(8,128)(2,1)} fusion(bf16[4,64,64,64]{3,2,1,0:T(8,128)(2,1)} %constant_dynamic-update-slice_fusion.3, bf16[1,64,64,64]{3,2,1,0:T(8,128)(2,1)S(1)} %concatenate.13), kind=kLoop, calls=%fused_computation.25 | loop fusion | bytes 1572864
  21.5 1.1 constant_dynamic-update-slice_fusion.1
  22.6 7.6 %collective-permute-done.2 = bf16[1,64,4096]{2,1,0:T(8,128)(2,1)S(1)} collective-permute-done((bf16[1,64,4096]{2,1,0:T(8,128)(2,1)}, bf16[1,64,4096]{2,1,0:T(8,128)(2,1)S(1)}, u32[]{:S(2)}, u32[]{:S(2)}) %collective-permute-start.2) | collective-permute-done | bytes 524320 | tf_op jit(solution)/shard_map/ppermute | solution.py:22
  30.2 1.1 %concatenate.15 = bf16[1,64,64,64]{3,2,1,0:T(8,128)(2,1)S(1)} reshape(bf16[1,64,4096]{2,1,0:T(8,128)(2,1)S(1)} %collective-permute-done.2) | data formatting | bytes 1048576 | tf_op jit(solution)/shard_map/concatenate | solution.py:42
  31.3 1.1 constant_dynamic-update-slice_fusion
  32.4 5.4 %convolution_convert_fusion = bf16[4,64,64,64]{3,2,1,0:T(8,128)(2,1)} fusion(bf16[4,64,64,64]{3,2,1,0:T(8,128)(2,1)} %constant_dynamic-update-slice_fusion, bf16[4,64,64]{2,1,0:T(8,128)(2,1)S(1)} %copy-done, s32[]{:T(128)S(6)} %select_n.30), kind=kOutput, calls=%fused_computation.2 | convolution fusion | flops 135266304 | bytes 4210692 | tf_op jit(solution)/shard_map/krmn,nl->krml/dot_general | solution.py:13
  37.8 5.7 %reshape.46 = bf16[256,4096]{1,0:T(8,128)(2,1)S(1)} reshape(bf16[4,64,64,64]{3,2,1,0:T(8,128)(2,1)} %convolution_convert_fusion) | data formatting | bytes 4194304 | tf_op jit(solution)/shard_map/reshape | solution.py:15
  43.4 5.5 %convert_bitcast_fusion = bf16[4,64,64,64]{2,3,1,0:T(8,128)(2,1)} fusion(bf16[4,64,64,64]{3,2,1,0:T(8,128)(2,1)} %constant_dynamic-update-slice_fusion, bf16[4,64,64]{2,1,0:T(8,128)(2,1)} %param.8, s32[]{:T(128)S(6)} %select_n.30, pred[64]{0:T(512)(128)(4,1)S(1)} %iota_compare_fusion.2), kind=kOutput, calls=%fused_computation.1 | convolution fusion | flops 135274496 | bytes 6308868 | tf_op jit(solution)/shard_map/ms,krsl->krml/dot_general | solution.py:14
  48.9 6.3 %copy.13 = bf16[4,64,64,64]{3,2,1,0:T(8,128)(2,1)} copy(bf16[4,64,64,64]{2,3,1,0:T(8,128)(2,1)} %convert_bitcast_fusion) | data formatting | bytes 4194304 | tf_op jit(solution)/shard_map/convert_element_type | solution.py:16
  55.2 6.6 %reshape.47 = bf16[256,4096]{1,0:T(8,128)(2,1)} reshape(bf16[4,64,64,64]{3,2,1,0:T(8,128)(2,1)} %copy.13) | data formatting | bytes 4194304 | tf_op jit(solution)/shard_map/reshape | solution.py:16
  61.8 2.3 %convolution_convert_fusion.1 = bf16[256,256]{1,0:T(8,128)(2,1)S(1)} fusion(bf16[256,4096]{1,0:T(8,128)(2,1)S(1)} %reshape.46, bf16[256,4096]{1,0:T(8,128)(2,1)} %reshape.47), kind=kOutput, calls=%fused_computation.3 | convolution fusion | flops 536936448 | bytes 4325376 | tf_op jit(solution)/shard_map/dot_general | solution.py:43
  64.2 0.3 fusion.1
  64.5 0.7 copy.15
  65.3 6.0 %all-to-all-start = ((bf16[16,32,256]{2,1,0:T(8,128)(2,1)}), bf16[16,32,256]{2,1,0:T(8,128)(2,1)S(1)}, u32[]{:S(2)}, u32[]{:S(2)}) async-start(bf16[16,32,256]{2,1,0:T(8,128)(2,1)} %bitcast.17), calls=%async_computation | async-start | bytes 524288 | tf_op jit(solution)/shard_map/all_to_all | solution.py:51
  71.3 0.6 dynamic-slice
  72.8 12.4 %all-reduce = s32[64]{0:T(128)S(1)} all-reduce(s32[64]{0:T(128)S(1)} %dynamic-update-slice), channel_id=2, replica_groups=mesh['snap'=2,'pair'=4,'ri'=4] {'pair','ri'}, use_global_device_ids=true, to_apply=%add | all-reduce | flops 64 | bytes 512
  85.3 19.4 %all_gather.11 = bf16[512,512]{1,0:T(8,128)(2,1)S(1)} all-gather(bf16[32,512]{1,0:T(8,128)(2,1)S(1)} %copy-done.2), channel_id=1, replica_groups=mesh['snap'=2,'pair'=4,'ri'=4] {'pair','ri'}, dimensions={0}, use_global_device_ids=true | all-gather | bytes 557056 | tf_op jit(solution)/shard_map/all_gather | solution.py:57
  104.7 0.2 reshape.50
  105.0 0.4 convolution_bitcast_fusion
  105.5 0.8 fusion.3
  (20 shorter events, 0.7 us)
Async XLA Ops:
  0.6 31.7 %copy-start = (bf16[4,64,64]{2,1,0:T(8,128)(2,1)S(1)}, bf16[4,64,64]{2,1,0:T(8,128)(2,1)}, u32[]{:S(2)}) copy-start(bf16[4,64,64]{2,1,0:T(8,128)(2,1)} %param.7) | copy-start | bytes 98308
  0.6 6.9 %copy-start.3 = (s32[4]{0:T(128)S(1)}, s32[4]{0:T(128)}, u32[]{:S(2)}) copy-start(s32[4]{0:T(128)} %param.9) | copy-start | bytes 52
  3.4 7.9 %collective-permute-start = (bf16[1,64,4096]{2,1,0:T(8,128)(2,1)}, bf16[1,64,4096]{2,1,0:T(8,128)(2,1)}, u32[]{:S(2)}, u32[]{:S(2)}) collective-permute-start(bf16[1,64,4096]{2,1,0:T(8,128)(2,1)} %get-tuple-element.3), channel_id=1, source_target_pairs={{0,1},{1,0},{2,3},{3,2},{4,5},{5,4},{6,7},{7,6},{8,9},{9,8},{10,11... | collective-permute-start | bytes 1572872 | tf_op jit(solution)/shard_map/ppermute | solution.py:22
  3.8 15.5 %collective-permute-start.1 = (bf16[1,64,4096]{2,1,0:T(8,128)(2,1)}, bf16[1,64,4096]{2,1,0:T(8,128)(2,1)S(1)}, u32[]{:S(2)}, u32[]{:S(2)}) collective-permute-start(bf16[1,64,4096]{2,1,0:T(8,128)(2,1)} %get-tuple-element.5), channel_id=1, source_target_pairs={{0,2},{1,3},{2,0},{3,1},{4,6},{5,7},{6,4},{7,5},{8,10},{9,11},{10,... | collective-permute-start | bytes 1572872 | tf_op jit(solution)/shard_map/ppermute | solution.py:22
  6.3 23.9 %collective-permute-start.2 = (bf16[1,64,4096]{2,1,0:T(8,128)(2,1)}, bf16[1,64,4096]{2,1,0:T(8,128)(2,1)S(1)}, u32[]{:S(2)}, u32[]{:S(2)}) collective-permute-start(bf16[1,64,4096]{2,1,0:T(8,128)(2,1)} %get-tuple-element.2), channel_id=1, source_target_pairs={{0,3},{1,2},{2,1},{3,0},{4,7},{5,6},{6,5},{7,4},{8,11},{9,10},{10,... | collective-permute-start | bytes 1572872 | tf_op jit(solution)/shard_map/ppermute | solution.py:22
  61.8 9.4 %copy-start.4 = (u32[32]{0:T(128)S(1)}, u32[32]{0:T(128)}, u32[]{:S(2)}) copy-start(u32[32]{0:T(128)} %constant.47) | copy-start | bytes 388
  61.8 23.5 %copy-start.2 = (bf16[32,512]{1,0:T(8,128)(2,1)S(1)}, bf16[32,512]{1,0:T(8,128)(2,1)}, u32[]{:S(2)}) copy-start(bf16[32,512]{1,0:T(8,128)(2,1)} %param.11) | copy-start | bytes 98308
  65.3 39.5 %all-to-all-start = ((bf16[16,32,256]{2,1,0:T(8,128)(2,1)}), bf16[16,32,256]{2,1,0:T(8,128)(2,1)S(1)}, u32[]{:S(2)}, u32[]{:S(2)}) async-start(bf16[16,32,256]{2,1,0:T(8,128)(2,1)} %bitcast.17), calls=%async_computation | async-start | bytes 524288 | tf_op jit(solution)/shard_map/all_to_all | solution.py:51
  105.5 0.8 copy-start.1

commit v2 on v1

v2 whole, which is shorter than its diff:
```python
import functools

import jax
import jax.numpy as jnp
from jax import lax
from jax.experimental import pallas as pl
from jax.experimental.pallas import tpu as pltpu
from jax.sharding import PartitionSpec as P

LANES = 128
VMEM_LIMIT = 48 * 1024 * 1024


def iota(shape, dim):
    return lax.broadcasted_iota(jnp.int32, shape, dim)


def dot(a, b):
    return jnp.dot(a, b, preferred_element_type=jnp.float32)


def dot_nt(a, b):
    return lax.dot_general(a, b, (((1,), (1,)), ((), ())), preferred_element_type=jnp.float32)


def prep_kernel(scalars, occ, virt, occ_out, virt_out):
    size = scalars[1]
    width = occ.shape[1]
    half = width // 2
    full = occ_out.shape[0]
    one = lambda hit: jnp.where(hit, 1.0, 0.0)
    spread = one(iota((full, width), 0) % width == iota((full, width), 1)).astype(jnp.bfloat16)
    tiled = dot_nt(dot(spread, occ[0]).astype(jnp.bfloat16), spread)
    same = iota((full, full), 0) // width == iota((full, full), 1) // width
    occ_out[...] = jnp.where(same, tiled, 0.0).astype(jnp.bfloat16)

    keep = (iota((width, width), 0) < size) & (iota((width, width), 1) < size)
    kept = jnp.where(keep, virt[0].astype(jnp.float32), 0.0).astype(jnp.bfloat16)
    group = full // 2
    copies_row = iota((group, full), 0) // half
    copies_col = iota((group, full), 1) % group // half
    for parity in range(2):
        wanted = 2 * (iota((group, width), 0) % half) + parity
        picked_rows = one(wanted == iota((group, width), 1)).astype(jnp.bfloat16)
        column = iota((full, width), 0)
        side = column // group
        wanted = 2 * (column % half) + (side + parity) % 2
        picked_columns = one(wanted == iota((full, width), 1)).astype(jnp.bfloat16)
        part = dot_nt(dot(picked_rows, kept).astype(jnp.bfloat16), picked_columns)
        part = jnp.where(copies_row == copies_col, part, 0.0)
        virt_out[parity * group : (parity + 1) * group, :] = part.astype(jnp.bfloat16)


def prep(scalars, occ, virt):
    width = occ.shape[-1]
    full = 4 * width
    pick = pl.BlockSpec((1, width, width), lambda i, s: (s[0], 0, 0))
    whole = pl.BlockSpec((full, full), lambda i, s: (0, 0))
    return pl.pallas_call(
        prep_kernel,
        grid_spec=pltpu.PrefetchScalarGridSpec(
            num_scalar_prefetch=1, grid=(1,), in_specs=[pick, pick], out_specs=[whole, whole]
        ),
        out_shape=[jax.ShapeDtypeStruct((full, full), jnp.bfloat16)] * 2,
        name="prep",
    )(scalars, occ, virt)


def transform(block, occ, virt, left, right, spread, mixed):
    rows, square = block.shape
    full = occ.shape[0]
    group = full // 2
    chunks = square // LANES
    for c in range(square // full):
        at = slice(c * full, (c + 1) * full)
        left[:, at] = dot(block[:, at], occ[...]).astype(jnp.bfloat16)
    for c in range(chunks):
        piece = block[:, c * LANES : (c + 1) * LANES].astype(jnp.float32)
        spread[pl.ds(c, rows, stride=chunks), :] = piece
    low = iota((group, full), 1) % LANES < LANES // 2
    for g in range(0, rows * chunks, 2 * group):
        one, two = spread[g : g + group, :], spread[g + group : g + 2 * group, :]
        plain = jnp.concatenate([one, two], 1).astype(jnp.bfloat16)
        turned = jnp.concatenate(
            [pltpu.roll(one, LANES // 2, 1), pltpu.roll(two, LANES // 2, 1)], 1
        ).astype(jnp.bfloat16)
        out = dot(virt[...], jnp.concatenate([plain, turned], 0))
        out = jnp.where(low, out[:group], out[group:])
        mixed[g : g + group, :] = out[:, :LANES]
        mixed[g + group : g + 2 * group, :] = out[:, LANES:]
    for c in range(chunks):
        piece = mixed[pl.ds(c, rows, stride=chunks), :]
        right[:, c * LANES : (c + 1) * LANES] = piece.astype(jnp.bfloat16)


def transform_kernel(scalars, block, occ, virt, left, right, spread, mixed):
    transform(block.at[0], occ, virt, left, right, spread, mixed)


def transformed(scalars, blocks, occ, virt, picked):
    _, rows, square = blocks.shape
    full = occ.shape[0]
    where = (lambda i, s: (s[0], 0, 0)) if picked else (lambda i, s: (0, 0, 0))
    whole = pl.BlockSpec((full, full), lambda i, s: (0, 0))
    out = pl.BlockSpec((rows, square), lambda i, s: (0, 0))
    scratch = pltpu.VMEM((rows * (square // LANES), LANES), jnp.float32)
    return pl.pallas_call(
        transform_kernel,
        grid_spec=pltpu.PrefetchScalarGridSpec(
            num_scalar_prefetch=1,
            grid=(1,),
            in_specs=[pl.BlockSpec((1, rows, square), where), whole, whole],
            out_specs=[out, out],
            scratch_shapes=[scratch, scratch],
        ),
        out_shape=[jax.ShapeDtypeStruct((rows, square), jnp.bfloat16)] * 2,
        compiler_params=pltpu.CompilerParams(vmem_limit_bytes=VMEM_LIMIT),
        cost_estimate=pl.CostEstimate(
            flops=4 * rows * square * full, bytes_accessed=6 * rows * square, transcendentals=0
        ),
        name="transform",
    )(scalars, blocks, occ, virt)


def chi_kernel(count, ids, *refs):
    lefts, rights, out = refs[:count], refs[count : 2 * count], refs[2 * count]
    rows = lefts[0].shape[0]
    out[...] = jnp.zeros_like(out)
    for k in range(count):
        for half in range(0, count, 2):
            pair = [dot_nt(lefts[k][...], rights[half + i][...]) for i in range(2)]
            at = slice(half * rows, (half + 2) * rows)
            out[ids[k], :, at] = jnp.concatenate(pair, 1).astype(jnp.bfloat16)


def chi_pieces(ids, lefts, rights):
    count = len(lefts)
    rows, square = lefts[0].shape
    return pl.pallas_call(
        functools.partial(chi_kernel, count),
        in_specs=[pl.BlockSpec(memory_space=pltpu.SMEM)]
        + [pl.BlockSpec(memory_space=pltpu.VMEM)] * (2 * count),
        out_specs=pl.BlockSpec(memory_space=pltpu.VMEM),
        out_shape=jax.ShapeDtypeStruct((2 * count, rows, count * rows), jnp.bfloat16),
        compiler_params=pltpu.CompilerParams(vmem_limit_bytes=VMEM_LIMIT),
        name="pair_chi",
    )(ids, *lefts, *rights)


def finish_kernel(ri_count, ids, got, metric, chi, screen, even, odd):
    sources, rows, columns = got.shape
    kcount = ids.shape[1]
    width = columns // kcount
    even[...] = jnp.zeros_like(even)
    odd[...] = jnp.zeros_like(odd)

    def add(source_group, carry):
        for ri in range(ri_count):
            source = source_group * ri_count + ri
            for j in range(0, kcount, 2):
                piece = got[source, :, j * width : (j + 2) * width].astype(jnp.float32)
                even[ids[source, ri ^ j]] += piece
                odd[ids[source, ri ^ (j + 1)]] += piece
        return carry

    lax.fori_loop(0, sources // ri_count, add, 0)
    low = iota((rows, LANES), 1) < width
    for t in range(0, 2 * kcount, 2):
        first = even[t] + pltpu.roll(odd[t], width, 1)
        second = odd[t + 1] + pltpu.roll(even[t + 1], width, 1)
        chi[:, t * width : (t + 2) * width] = jnp.where(low, first, second)
    screen[...] = dot(chi[...].astype(jnp.bfloat16), metric[...])


def finish(ids, got, metric, ri_count):
    sources, rows, columns = got.shape
    total = metric.shape[0]
    blocks = 2 * ids.shape[1]
    scratch = pltpu.VMEM((blocks, rows, LANES), jnp.float32)
    vmem = pl.BlockSpec(memory_space=pltpu.VMEM)
    return pl.pallas_call(
        functools.partial(finish_kernel, ri_count),
        in_specs=[pl.BlockSpec(memory_space=pltpu.SMEM), vmem, vmem],
        out_specs=[vmem, vmem],
        out_shape=[jax.ShapeDtypeStruct((rows, total), jnp.float32)] * 2,
        scratch_shapes=[scratch, scratch],
        compiler_params=pltpu.CompilerParams(vmem_limit_bytes=VMEM_LIMIT),
        name="finish",
    )(ids, got, metric)


def swap(array, axes, step):
    count = lax.axis_size(axes)
    return lax.ppermute(array, axes, [(i, i ^ step) for i in range(count)])


def gathered(array, axis, step):
    other = swap(array, axis, step)
    upper = (lax.axis_index(axis) & step) != 0
    return jnp.where(upper, jnp.stack([other, array]), jnp.stack([array, other]))


def gather_metric(coulomb, ids):
    rows, total = coulomb.shape
    ri_count, pair_count = lax.axis_size("ri"), lax.axis_size("pair")
    out = coulomb[None]
    step = 2
    while step < ri_count:
        out = gathered(out, "ri", step).reshape(-1, rows, total)
        step *= 2
    step = 1
    all_ids = ids[None].astype(jnp.float32)
    while step < pair_count:
        out = gathered(out, "pair", step)
        out = out.reshape((-1,) + out.shape[2:])
        all_ids = gathered(all_ids, "pair", step).reshape((-1,) + all_ids.shape[1:])
        step *= 2
    out = gathered(out, "ri", 1)
    out = out.reshape(2, -1, rows, total).swapaxes(0, 1).reshape(-1, total)
    return out, all_ids.astype(jnp.int32).reshape(-1, ids.shape[-1])


def shards(three_c, green_occ, green_virt, pair_size, ri_ids, coulomb):
    everyone = ("pair", "ri")
    ri_count = lax.axis_size("ri")
    devices = lax.axis_size(everyone)
    here = lax.axis_index("ri")
    kcount = ri_ids.shape[1]
    pairs, _, rows, square = three_c.shape
    three_c = three_c.reshape(pairs, rows, square)

    parts = {}
    for step in list(range(2, ri_count)) + [1]:
        part = lax.dynamic_slice_in_dim(three_c, here ^ step, 1, 0)
        parts[step] = swap(part, "ri", step)
    metric, all_ids = gather_metric(coulomb, ri_ids)

    pick = lambda array: lax.dynamic_index_in_dim(array, here, 0, keepdims=False)
    scalars = jnp.stack([here, pick(pair_size)]).astype(jnp.int32)
    occ, virt = prep(scalars, green_occ, green_virt)
    lefts, rights = [], []
    for step in range(ri_count):
        left, right = transformed(scalars, parts.get(step, three_c), occ, virt, step == 0)
        lefts.append(left)
        rights.append(right)
    ids = pick(ri_ids)[here ^ jnp.arange(kcount, dtype=jnp.int32)]
    pieces = chi_pieces(ids, lefts, rights)
    pieces = pieces.reshape(devices, -1, kcount * rows)
    got = lax.all_to_all(pieces, everyone, 0, 0, tiled=True)
    return tuple(finish(all_ids, got, metric, ri_count))


def solution(mesh):
    placed = (
        P(("snap", "pair"), "ri", None, None),
        P(("snap", "pair"), None, None),
        P(("snap", "pair"), None, None),
        P(("snap", "pair")),
        P(("snap", "pair"), None),
        P(("snap", "pair", "ri"), None),
    )
    return jax.shard_map(
        shards,
        mesh=mesh,
        in_specs=placed,
        out_specs=(P(("snap", "pair", "ri"), None), P(("snap", "pair", "ri"), None)),
        check_vma=False,
    )
```

time: 107 us -> 75.9 us (0.71)
  blocking collectives: 31.8 us -> 0 us
  local copies, waits for them, and re-layouts: 35 us -> 6.38 us
  Pallas kernels: 0 us -> 18.7 us
  waiting for transfers between devices: 13.6 us -> 29.9 us
  matrix products: 14.8 us -> 0 us
  starting transfers between devices: 9.05 us -> 18.2 us
    all_gather x1 -> x0, blocking collectives: 19.4 us -> none  [shards(): metric = lax.all_gather(coulomb, everyone, axis=0, tiled=True)]
    pallas_call x0 -> x7, Pallas kernels: none -> 18.7 us  [the longest x4 10.8 us: transformed(): pl.pallas_call(transform_kernel, grid_spec=pltpu.PrefetchScalarGridSpec(n...]
    ppermute x3 -> x9, waiting for transfers between devices: 13.6 us -> 29.7 us  [swap(): return lax.ppermute(array, axes, [(i, i ^ step) for i in range(count)])]
    dot_general x6 -> x0, matrix products: 14.8 us -> none  [the longest x1 5.5 us: block_products(): jnp.einsum('ms,krsl->krml', virt * keep, shaped, preferred_element_type=j...]
    reshape x4 -> x0, local copies, waits for them, and re-layouts: 12.6 us -> none  [the longest x1 6.61 us: block_products(): right = right.astype(jnp.bfloat16).reshape(kcount * rows, square)]
    unnamed x1 -> x0, blocking collectives: 12.4 us -> none
    ppermute x3 -> x9, starting transfers between devices: 3.09 us -> 14.3 us  [swap(): return lax.ppermute(array, axes, [(i, i ^ step) for i in range(count)])]
    concatenate x5 -> x0, local copies, waits for them, and re-layouts: 6.48 us -> none  [shards(): left, right = block_products(jnp.concatenate(parts, 0), occ, virt, size)]
  transfers between devices with their start and end apart: 4 -> 10, of which waited for: 2 -> 4; matrix products, arithmetic and copies ran while one was open for 10% -> 3% of each run, Pallas kernels for 0% -> 23%
where the time goes in v2:
time: 75.9 us; the launch traced here: 75.4 us
  waiting for transfers between devices  29.9 us (39%)
  Pallas kernels  18.7 us (25%)
  starting transfers between devices  18.2 us (24%)
  local copies, waits for them, and re-layouts  6.38 us (8%)
  other arithmetic  1.38 us (2%)
  between operations  0.82 us (1%)
    ppermute x9, waiting for transfers between devices, swap(): return lax.ppermute(array, axes, [(i, i ^ step) for i in range(count)])  29.7 us
    ppermute x9, starting transfers between devices, swap(): return lax.ppermute(array, axes, [(i, i ^ step) for i in range(count)])  14.3 us
    pallas_call x4, Pallas kernels, transformed(): pl.pallas_call(transform_kernel, grid_spec=pltpu.PrefetchScalarGridSpec(n...  10.8 us
    all_to_all x1, starting transfers between devices, shards(): got = lax.all_to_all(pieces, everyone, 0, 0, tiled=True)  3.88 us
    pallas_call x1, Pallas kernels, chi_pieces(): pl.pallas_call(functools.partial(chi_kernel, count), in_specs=[pl.BlockSp...  3.64 us
    dynamic_slice x1, local copies, waits for them, and re-layouts, shards(): part = lax.dynamic_slice_in_dim(three_c, here ^ step, 1, 0)  2.71 us
    pallas_call x1, Pallas kernels, prep(): pl.pallas_call(prep_kernel, grid_spec=pltpu.PrefetchScalarGridSpec(num_sc...  2.51 us
    unnamed x14, local copies, waits for them, and re-layouts  2.43 us
  transfers between devices with their start and end apart: 10, of which 4 were waited for; matrix products, arithmetic and copies ran while one was open for 3% of the time, Pallas kernels for 23%

profile of v2, /device:TPU:0, one launch (start us, length us, event | category | flops | bytes accessed | tf_op | source)
XLA Modules:
  0.0 75.4 jit_solution(3619849699166313175)
XLA Ops:
  0.7 2.7 %dynamic-slice_bitcast_fusion = (bf16[1,64,4096]{2,1,0:T(8,128)(2,1)}, bf16[1,64,4096]{2,1,0:T(8,128)(2,1)}, bf16[1,64,4096]{2,1,0:T(8,128)(2,1)}) fusion(bf16[4,1,64,4096]{3,2,1,0:T(8,128)(2,1)} %param.6, s32[]{:T(128)S(6)} %select_n.142, s32[]{:T(128)S(6)} %select_n.140, s32[]{:T(128)S(6)} %select_n.141), kind=kLoop, calls=%fused_computation.2 | loop fusion | bytes 3145740 | tf_op jit(solution)/shard_map/dynamic_slice | solution.py:234
  3.4 0.5 collective-permute-start.2
  3.9 2.5 %collective-permute-start.3 = (bf16[1,64,4096]{2,1,0:T(8,128)(2,1)}, bf16[1,64,4096]{2,1,0:T(8,128)(2,1)S(1)}, u32[]{:S(2)}, u32[]{:S(2)}) collective-permute-start(bf16[1,64,4096]{2,1,0:T(8,128)(2,1)} %get-tuple-element.24), channel_id=1, source_target_pairs={{0,2},{1,3},{2,0},{3,1},{4,6},{5,7},{6,4},{7,5},{8,10},{9,11},{10,... | collective-permute-start | bytes 1572872 | tf_op jit(solution)/shard_map/ppermute | solution.py:194
  6.3 0.1 collective-permute-start.4
  6.5 1.7 %collective-permute-start.5 = (bf16[1,32,512]{2,1,0:T(8,128)(2,1)S(1)}, bf16[1,32,512]{2,1,0:T(8,128)(2,1)S(1)}, u32[]{:S(2)}, u32[]{:S(2)}) collective-permute-start(bf16[1,32,512]{2,1,0:T(8,128)(2,1)S(1)} %bitcast.42), channel_id=1, source_target_pairs={{0,2},{1,3},{2,0},{3,1},{4,6},{5,7},{6,4},{7,5},{8,10},{9,11},{10,... | collective-permute-start | bytes 98312 | tf_op jit(solution)/shard_map/ppermute | solution.py:194
  8.2 1.6 %collective-permute-start = (f32[1,4,4]{2,1,0:T(4,128)S(1)}, f32[1,4,4]{2,1,0:T(4,128)S(1)}, u32[]{:S(2)}, u32[]{:S(2)}) collective-permute-start(f32[1,4,4]{2,1,0:T(4,128)S(1)} %get-tuple-element.25), channel_id=1, source_target_pairs={{0,4},{4,0},{8,12},{12,8},{1,5},{5,1},{9,13},{13,9},{2,6},{6,2},{1... | collective-permute-start | bytes 200 | tf_op jit(solution)/shard_map/ppermute | solution.py:194
  9.8 0.6 dynamic_slice.24
  10.4 20.7 %collective-permute-done.5 = bf16[1,32,512]{2,1,0:T(8,128)(2,1)S(1)} collective-permute-done((bf16[1,32,512]{2,1,0:T(8,128)(2,1)S(1)}, bf16[1,32,512]{2,1,0:T(8,128)(2,1)S(1)}, u32[]{:S(2)}, u32[]{:S(2)}) %collective-permute-start.5) | collective-permute-done | bytes 32800 | tf_op jit(solution)/shard_map/ppermute | solution.py:194
  31.1 1.9 %collective-permute-start.6 = (bf16[2,32,512]{2,1,0:T(8,128)(2,1)S(1)}, bf16[2,32,512]{2,1,0:T(8,128)(2,1)S(1)}, u32[]{:S(2)}, u32[]{:S(2)}) collective-permute-start(bf16[2,32,512]{2,1,0:T(8,128)(2,1)S(1)} %maximum_select_fusion.3), channel_id=1, source_target_pairs={{0,4},{4,0},{8,12},{12,8},{1,5},{5,1},{9,13},{13,9},{2,6},{6,2},{1... | collective-permute-start | bytes 196616 | tf_op jit(solution)/shard_map/ppermute | solution.py:194
  33.0 2.4 %collective-permute-done.6 = bf16[2,32,512]{2,1,0:T(8,128)(2,1)S(1)} collective-permute-done((bf16[2,32,512]{2,1,0:T(8,128)(2,1)S(1)}, bf16[2,32,512]{2,1,0:T(8,128)(2,1)S(1)}, u32[]{:S(2)}, u32[]{:S(2)}) %collective-permute-start.6) | collective-permute-done | bytes 65568 | tf_op jit(solution)/shard_map/ppermute | solution.py:194
  35.4 2.9 %collective-permute-start.7 = (bf16[4,32,512]{2,1,0:T(8,128)(2,1)S(1)}, bf16[4,32,512]{2,1,0:T(8,128)(2,1)S(1)}, u32[]{:S(2)}, u32[]{:S(2)}) collective-permute-start(bf16[4,32,512]{2,1,0:T(8,128)(2,1)S(1)} %bitcast.38), channel_id=1, source_target_pairs={{0,8},{4,12},{8,0},{12,4},{1,9},{5,13},{9,1},{13,5},{2,10},{6,14},... | collective-permute-start | bytes 393224 | tf_op jit(solution)/shard_map/ppermute | solution.py:194
  38.4 1.2 %pad_add_fusion.scalars = s32[2]{0:T(128)} fusion(s32[1]{0:T(128)} %dynamic_slice.24, s32[1]{0:T(128)} %bitcast.7), kind=kLoop, calls=%fused_computation.20 | loop fusion | flops 2 | bytes 16 | tf_op jit(solution)/shard_map/stack | solution.py:239
  39.6 0.6 gather_fusion
  40.2 2.5 %prep.1 = (bf16[256,256]{1,0:T(8,128)(2,1)}, bf16[256,256]{1,0:T(8,128)(2,1)}) custom-call(s32[2]{0:T(128)} %pad_add_fusion.scalars, bf16[4,64,64]{2,1,0:T(8,128)(2,1)} %occ.1, bf16[4,64,64]{2,1,0:T(8,128)(2,1)} %virt.1), custom_call_target="tpu_custom_call" | custom-call | tf_op jit(solution)/shard_map/prep/pallas_call | solution.py:59
  42.7 0.9 %copy-done.1 = bf16[256,256]{1,0:T(8,128)(2,1)S(1)} copy-done((bf16[256,256]{1,0:T(8,128)(2,1)S(1)}, bf16[256,256]{1,0:T(8,128)(2,1)}, u32[]{:S(2)}) %copy-start.1) | copy-done | bytes 131096
  43.7 0.9 %copy-done.2 = bf16[256,256]{1,0:T(8,128)(2,1)S(1)} copy-done((bf16[256,256]{1,0:T(8,128)(2,1)S(1)}, bf16[256,256]{1,0:T(8,128)(2,1)}, u32[]{:S(2)}) %copy-start.2) | copy-done | bytes 131096
  44.6 0.6 copy-done.3
  45.2 2.4 %transform.4 = (bf16[64,4096]{1,0:T(8,128)(2,1)S(1)}, bf16[64,4096]{1,0:T(8,128)(2,1)S(1)}) custom-call(s32[2]{0:T(128)S(1)} %copy-done.3, bf16[4,64,4096]{2,1,0:T(8,128)(2,1)S(1)} %bitcast.33, bf16[256,256]{1,0:T(8,128)(2,1)S(1)} %copy-done.1, bf16[256,256]{1,0:T(8,128)(2,1)S(1)} %copy-done.2), custom_call_target="tpu_custom_call" | custom-call | flops 268435456 | bytes 1572864 | tf_op jit(solution)/shard_map/transform/pallas_call | solution.py:107
  47.6 3.5 %transform.5 = (bf16[64,4096]{1,0:T(8,128)(2,1)S(1)}, bf16[64,4096]{1,0:T(8,128)(2,1)S(1)}) custom-call(s32[2]{0:T(128)S(1)} %copy-done.3, bf16[1,64,4096]{2,1,0:T(8,128)(2,1)} %collective-permute-done.2.block, bf16[256,256]{1,0:T(8,128)(2,1)S(1)} %copy-done.1, bf16[256,256]{1,0:T(8,128)(2,1)S(1)} %copy-done.2), custom_call_target="tpu_custom_call" | custom-call | flops 268435456 | bytes 1572864 | tf_op jit(solution)/shard_map/transform/pallas_call | solution.py:107
  51.1 2.4 %transform.6 = (bf16[64,4096]{1,0:T(8,128)(2,1)S(1)}, bf16[64,4096]{1,0:T(8,128)(2,1)S(1)}) custom-call(s32[2]{0:T(128)S(1)} %copy-done.3, bf16[1,64,4096]{2,1,0:T(8,128)(2,1)S(1)} %collective-permute-done.3.block, bf16[256,256]{1,0:T(8,128)(2,1)S(1)} %copy-done.1, bf16[256,256]{1,0:T(8,128)(2,1)S(1)} %copy-done.2), custom_call_target="tpu_custom_call" | custom-call | flops 268435456 | bytes 1572864 | tf_op jit(solution)/shard_map/transform/pallas_call | solution.py:107
  53.6 0.0 collective-permute-done.4.block
  53.6 2.4 %transform.7 = (bf16[64,4096]{1,0:T(8,128)(2,1)S(1)}, bf16[64,4096]{1,0:T(8,128)(2,1)S(1)}) custom-call(s32[2]{0:T(128)S(1)} %copy-done.3, bf16[1,64,4096]{2,1,0:T(8,128)(2,1)S(1)} %collective-permute-done.4.block, bf16[256,256]{1,0:T(8,128)(2,1)S(1)} %copy-done.1, bf16[256,256]{1,0:T(8,128)(2,1)S(1)} %copy-done.2), custom_call_target="tpu_custom_call" | custom-call | flops 268435456 | bytes 1572864 | tf_op jit(solution)/shard_map/transform/pallas_call | solution.py:107
  56.0 3.6 %pair_chi.1 = bf16[8,64,256]{2,1,0:T(8,128)(2,1)} custom-call(s32[4]{0:T(128)S(1)} %gather_fusion, bf16[64,4096]{1,0:T(8,128)(2,1)S(1)} %get-tuple-element.14.refs_0_, bf16[64,4096]{1,0:T(8,128)(2,1)S(1)} %get-tuple-element.15.refs_1_, bf16[64,4096]{1,0:T(8,128)(2,1)S(1)} %get-tuple-element.16.refs_2_, bf16[64,4096]{1,0:T(8,128)(2,1)S(1)} %get-tuple-element.17.refs_3_, ...), custom_call_target="tpu_custom_call" | custom-call | tf_op jit(solution)/shard_map/pair_chi/pallas_call | solution.py:139
  59.7 3.9 %all-to-all-start = ((bf16[16,32,256]{2,1,0:T(8,128)(2,1)}), bf16[16,32,256]{2,1,0:T(8,128)(2,1)S(1)}, u32[]{:S(2)}, u32[]{:S(2)}) async-start(bf16[16,32,256]{2,1,0:T(8,128)(2,1)} %bitcast.12), calls=%async_computation | async-start | bytes 524288 | tf_op jit(solution)/shard_map/all_to_all | solution.py:249
  63.6 0.0 collective-permute-done.7
  63.6 0.5 collective-permute-start.8
  64.1 0.0 collective-permute-done
  64.1 2.6 %collective-permute-start.1 = (f32[2,4,4]{2,1,0:T(4,128)S(1)}, f32[2,4,4]{2,1,0:T(4,128)S(1)}, u32[]{:S(2)}, u32[]{:S(2)}) collective-permute-start(f32[2,4,4]{2,1,0:T(4,128)S(1)} %maximum_select_fusion.6), channel_id=1, source_target_pairs={{0,8},{4,12},{8,0},{12,4},{1,9},{5,13},{9,1},{13,5},{2,10},{6,14},... | collective-permute-start | bytes 392 | tf_op jit(solution)/shard_map/ppermute | solution.py:194
  66.8 6.6 %collective-permute-done.1 = f32[2,4,4]{2,1,0:T(4,128)S(1)} collective-permute-done((f32[2,4,4]{2,1,0:T(4,128)S(1)}, f32[2,4,4]{2,1,0:T(4,128)S(1)}, u32[]{:S(2)}, u32[]{:S(2)}) %collective-permute-start.1) | collective-permute-done | bytes 160 | tf_op jit(solution)/shard_map/ppermute | solution.py:194
  73.4 0.1 maximum_select_fusion
  73.5 0.2 all-to-all-done.got
  73.7 1.7 %finish.1 = (f32[32,512]{1,0:T(8,128)}, f32[32,512]{1,0:T(8,128)}) custom-call(s32[16,4]{1,0:T(8,128)S(1)} %bitcast.35, bf16[16,32,256]{2,1,0:T(8,128)(2,1)S(1)} %all-to-all-done.got, bf16[512,512]{1,0:T(8,128)(2,1)S(1)} %bitcast.34), custom_call_target="tpu_custom_call" | custom-call | tf_op jit(solution)/shard_map/finish/pallas_call | solution.py:181
  (25 shorter events, 0.1 us)
Async XLA Ops:
  0.6 5.9 %copy-start.4 = (bf16[32,512]{1,0:T(8,128)(2,1)S(1)}, bf16[32,512]{1,0:T(8,128)(2,1)}, u32[]{:S(2)}) copy-start(bf16[32,512]{1,0:T(8,128)(2,1)} %param.11) | copy-start | bytes 98308
  0.6 7.6 %copy-start.5 = (s32[4,4]{1,0:T(4,128)S(1)}, s32[4,4]{1,0:T(4,128)}, u32[]{:S(2)}) copy-start(s32[4,4]{1,0:T(4,128)} %param.10) | copy-start | bytes 196
  0.7 9.2 %copy-start.6 = (s32[4]{0:T(128)S(1)}, s32[4]{0:T(128)}, u32[]{:S(2)}) copy-start(s32[4]{0:T(128)} %param.9) | copy-start | bytes 52
  0.7 42.1 %copy-start = (bf16[4,1,64,4096]{3,2,1,0:T(8,128)(2,1)S(1)}, bf16[4,1,64,4096]{3,2,1,0:T(8,128)(2,1)}, u32[]{:S(2)}) copy-start(bf16[4,1,64,4096]{3,2,1,0:T(8,128)(2,1)} %param.6) | copy-start | bytes 6291460
  3.4 44.2 %collective-permute-start.2 = (bf16[1,64,4096]{2,1,0:T(8,128)(2,1)}, bf16[1,64,4096]{2,1,0:T(8,128)(2,1)}, u32[]{:S(2)}, u32[]{:S(2)}) collective-permute-start(bf16[1,64,4096]{2,1,0:T(8,128)(2,1)} %get-tuple-element.23), channel_id=1, source_target_pairs={{0,1},{1,0},{2,3},{3,2},{4,5},{5,4},{6,7},{7,6},{8,9},{9,8},{10,11... | collective-permute-start | bytes 1572872 | tf_op jit(solution)/shard_map/ppermute | solution.py:194
  3.9 47.3 %collective-permute-start.3 = (bf16[1,64,4096]{2,1,0:T(8,128)(2,1)}, bf16[1,64,4096]{2,1,0:T(8,128)(2,1)S(1)}, u32[]{:S(2)}, u32[]{:S(2)}) collective-permute-start(bf16[1,64,4096]{2,1,0:T(8,128)(2,1)} %get-tuple-element.24), channel_id=1, source_target_pairs={{0,2},{1,3},{2,0},{3,1},{4,6},{5,7},{6,4},{7,5},{8,10},{9,11},{10,... | collective-permute-start | bytes 1572872 | tf_op jit(solution)/shard_map/ppermute | solution.py:194
  6.3 47.2 %collective-permute-start.4 = (bf16[1,64,4096]{2,1,0:T(8,128)(2,1)}, bf16[1,64,4096]{2,1,0:T(8,128)(2,1)S(1)}, u32[]{:S(2)}, u32[]{:S(2)}) collective-permute-start(bf16[1,64,4096]{2,1,0:T(8,128)(2,1)} %get-tuple-element.22), channel_id=1, source_target_pairs={{0,3},{1,2},{2,1},{3,0},{4,7},{5,6},{6,5},{7,4},{8,11},{9,10},{10,... | collective-permute-start | bytes 1572872 | tf_op jit(solution)/shard_map/ppermute | solution.py:194
  6.5 24.6 %collective-permute-start.5 = (bf16[1,32,512]{2,1,0:T(8,128)(2,1)S(1)}, bf16[1,32,512]{2,1,0:T(8,128)(2,1)S(1)}, u32[]{:S(2)}, u32[]{:S(2)}) collective-permute-start(bf16[1,32,512]{2,1,0:T(8,128)(2,1)S(1)} %bitcast.42), channel_id=1, source_target_pairs={{0,2},{1,3},{2,0},{3,1},{4,6},{5,7},{6,4},{7,5},{8,10},{9,11},{10,... | collective-permute-start | bytes 98312 | tf_op jit(solution)/shard_map/ppermute | solution.py:194
  8.2 55.9 %collective-permute-start = (f32[1,4,4]{2,1,0:T(4,128)S(1)}, f32[1,4,4]{2,1,0:T(4,128)S(1)}, u32[]{:S(2)}, u32[]{:S(2)}) collective-permute-start(f32[1,4,4]{2,1,0:T(4,128)S(1)} %get-tuple-element.25), channel_id=1, source_target_pairs={{0,4},{4,0},{8,12},{12,8},{1,5},{5,1},{9,13},{13,9},{2,6},{6,2},{1... | collective-permute-start | bytes 200 | tf_op jit(solution)/shard_map/ppermute | solution.py:194
  31.1 4.3 %collective-permute-start.6 = (bf16[2,32,512]{2,1,0:T(8,128)(2,1)S(1)}, bf16[2,32,512]{2,1,0:T(8,128)(2,1)S(1)}, u32[]{:S(2)}, u32[]{:S(2)}) collective-permute-start(bf16[2,32,512]{2,1,0:T(8,128)(2,1)S(1)} %maximum_select_fusion.3), channel_id=1, source_target_pairs={{0,4},{4,0},{8,12},{12,8},{1,5},{5,1},{9,13},{13,9},{2,6},{6,2},{1... | collective-permute-start | bytes 196616 | tf_op jit(solution)/shard_map/ppermute | solution.py:194
  35.4 28.1 %collective-permute-start.7 = (bf16[4,32,512]{2,1,0:T(8,128)(2,1)S(1)}, bf16[4,32,512]{2,1,0:T(8,128)(2,1)S(1)}, u32[]{:S(2)}, u32[]{:S(2)}) collective-permute-start(bf16[4,32,512]{2,1,0:T(8,128)(2,1)S(1)} %bitcast.38), channel_id=1, source_target_pairs={{0,8},{4,12},{8,0},{12,4},{1,9},{5,13},{9,1},{13,5},{2,10},{6,14},... | collective-permute-start | bytes 393224 | tf_op jit(solution)/shard_map/ppermute | solution.py:194
  42.7 0.9 %copy-start.1 = (bf16[256,256]{1,0:T(8,128)(2,1)S(1)}, bf16[256,256]{1,0:T(8,128)(2,1)}, u32[]{:S(2)}) copy-start(bf16[256,256]{1,0:T(8,128)(2,1)} %get-tuple-element.12.occ) | copy-start | bytes 393220
  43.6 0.9 %copy-start.2 = (bf16[256,256]{1,0:T(8,128)(2,1)S(1)}, bf16[256,256]{1,0:T(8,128)(2,1)}, u32[]{:S(2)}) copy-start(bf16[256,256]{1,0:T(8,128)(2,1)} %get-tuple-element.13.virt) | copy-start | bytes 393220
  44.6 0.6 copy-start.3
  59.7 14.0 %all-to-all-start = ((bf16[16,32,256]{2,1,0:T(8,128)(2,1)}), bf16[16,32,256]{2,1,0:T(8,128)(2,1)S(1)}, u32[]{:S(2)}, u32[]{:S(2)}) async-start(bf16[16,32,256]{2,1,0:T(8,128)(2,1)} %bitcast.12), calls=%async_computation | async-start | bytes 524288 | tf_op jit(solution)/shard_map/all_to_all | solution.py:249
  63.6 9.8 %collective-permute-start.8 = (bf16[8,32,512]{2,1,0:T(8,128)(2,1)S(1)}, bf16[8,32,512]{2,1,0:T(8,128)(2,1)S(1)}, u32[]{:S(2)}, u32[]{:S(2)}) collective-permute-start(bf16[8,32,512]{2,1,0:T(8,128)(2,1)S(1)} %bitcast.36), channel_id=1, source_target_pairs={{0,1},{1,0},{2,3},{3,2},{4,5},{5,4},{6,7},{7,6},{8,9},{9,8},{10,11... | collective-permute-start | bytes 786440 | tf_op jit(solution)/shard_map/ppermute | solution.py:194
  64.1 9.3 %collective-permute-start.1 = (f32[2,4,4]{2,1,0:T(4,128)S(1)}, f32[2,4,4]{2,1,0:T(4,128)S(1)}, u32[]{:S(2)}, u32[]{:S(2)}) collective-permute-start(f32[2,4,4]{2,1,0:T(4,128)S(1)} %maximum_select_fusion.6), channel_id=1, source_target_pairs={{0,8},{4,12},{8,0},{12,4},{1,9},{5,13},{9,1},{13,5},{2,10},{6,14},... | collective-permute-start | bytes 392 | tf_op jit(solution)/shard_map/ppermute | solution.py:194

commit v3 on v2

v3 whole, which is shorter than its diff:
```python
import functools

import jax
import jax.numpy as jnp
from jax import lax
from jax.experimental import pallas as pl
from jax.experimental.pallas import tpu as pltpu
from jax.sharding import PartitionSpec as P

LANES = 128
SUB = 8
VMEM_LIMIT = 48 * 1024 * 1024


def iota(shape, dim):
    return lax.broadcasted_iota(jnp.int32, shape, dim)


def dot(a, b):
    return jnp.dot(a, b, preferred_element_type=jnp.float32)


def dot_nt(a, b):
    return lax.dot_general(a, b, (((1,), (1,)), ((), ())), preferred_element_type=jnp.float32)


def prepared(size, occ, virt, occ_out, virt_out):
    width = occ.shape[0]
    full = occ_out.shape[0]
    one = lambda hit: jnp.where(hit, 1.0, 0.0).astype(jnp.bfloat16)
    spread = one(iota((full, width), 0) % width == iota((full, width), 1))
    tiled = dot_nt(dot(spread, occ).astype(jnp.bfloat16), spread)
    same = iota((full, full), 0) // width == iota((full, full), 1) // width
    occ_out[...] = jnp.where(same, tiled, 0.0).astype(jnp.bfloat16)

    keep = (iota((width, width), 0) < size) & (iota((width, width), 1) < size)
    kept = jnp.where(keep, virt.astype(jnp.float32), 0.0).astype(jnp.bfloat16)
    half = virt_out.shape[0] // 2
    same = iota((half, 2 * half), 0) % SUB == iota((half, 2 * half), 1) % SUB
    for parity in range(2):
        wanted = 2 * (iota((half, width), 0) // SUB) + parity
        picked_rows = one(wanted == iota((half, width), 1))
        column = iota((2 * half, width), 0)
        wanted = 2 * (column % half // SUB) + (column // half + parity) % 2
        picked_columns = one(wanted == iota((2 * half, width), 1))
        part = dot_nt(dot(picked_rows, kept).astype(jnp.bfloat16), picked_columns)
        part = jnp.where(same, part, 0.0).astype(jnp.bfloat16)
        virt_out[parity * half : (parity + 1) * half, :] = part


def transform(block, occ, virt, left, right):
    rows, square = right.shape
    full = occ.shape[0]
    chunks = square // LANES
    half = chunks * SUB
    for c in range(square // full):
        at = slice(c * full, (c + 1) * full)
        left[:, at] = dot(block[:, at], occ[...]).astype(jnp.bfloat16)
    low = iota((half, 2 * LANES), 1) % LANES < LANES // 2
    for row in range(0, rows, 2 * SUB):
        tile = block[row : row + 2 * SUB, :square].astype(jnp.float32)
        plain, turned = [], []
        for i in range(2):
            part = tile[i * SUB : (i + 1) * SUB]
            stacked = jnp.concatenate(
                [part[:, c * LANES : (c + 1) * LANES] for c in range(chunks)], 0
            )
            plain.append(stacked)
            turned.append(pltpu.roll(stacked, LANES // 2, 1))
        operand = jnp.concatenate(
            [jnp.concatenate(plain, 1), jnp.concatenate(turned, 1)], 0
        ).astype(jnp.bfloat16)
        out = dot(virt[...], operand)
        out = jnp.where(low, out[:half], out[half:])
        for c in range(chunks):
            piece = out[c * SUB : (c + 1) * SUB]
            piece = jnp.concatenate([piece[:, :LANES], piece[:, LANES:]], 0)
            right[row : row + 2 * SUB, c * LANES : (c + 1) * LANES] = piece.astype(jnp.bfloat16)


def first_kernel(scalars, own, other, occ, virt, occ_out, virt_out, left, right):
    prepared(scalars[1], occ[0], virt[0], occ_out, virt_out)
    rows = own.shape[1]
    for i, block in enumerate((own, other)):
        at = slice(i * rows, (i + 1) * rows)
        transform(block.at[0], occ_out, virt_out, left.at[at], right.at[at])


def first_blocks(scalars, three_c, other, occ, virt):
    _, rows, square = three_c.shape
    width = occ.shape[-1]
    pick = lambda shape: pl.BlockSpec((1,) + shape, lambda i, s: (s[0], 0, 0))
    whole = lambda *shape: pl.BlockSpec(shape, lambda i, s: (0,) * len(shape))
    shapes = [(4 * width, 4 * width), (SUB * width, SUB * width), (2 * rows, square), (2 * rows, square)]
    return pl.pallas_call(
        first_kernel,
        grid_spec=pltpu.PrefetchScalarGridSpec(
            num_scalar_prefetch=1,
            grid=(1,),
            in_specs=[pick((rows, square)), whole(1, rows, square), pick((width, width)), pick((width, width))],
            out_specs=[whole(*shape) for shape in shapes],
        ),
        out_shape=[jax.ShapeDtypeStruct(shape, jnp.bfloat16) for shape in shapes],
        compiler_params=pltpu.CompilerParams(vmem_limit_bytes=VMEM_LIMIT),
        name="first_blocks",
    )(scalars, three_c, other, occ, virt)


def next_kernel(block, occ, virt, left, right):
    transform(block.at[0], occ, virt, left, right)


def next_block(block, occ, virt, square):
    rows = block.shape[1]
    vmem = pl.BlockSpec(memory_space=pltpu.VMEM)
    return pl.pallas_call(
        next_kernel,
        in_specs=[vmem] * 3,
        out_specs=[vmem] * 2,
        out_shape=[jax.ShapeDtypeStruct((rows, square), jnp.bfloat16)] * 2,
        compiler_params=pltpu.CompilerParams(vmem_limit_bytes=VMEM_LIMIT),
        name="next_block",
    )(block, occ, virt)


def last_kernel(count, ids, block, occ, virt, *refs):
    lefts, rights = list(refs[:count]), list(refs[count : 2 * count])
    out, left, right = refs[2 * count :]
    transform(block.at[0], occ, virt, left, right)
    lefts.append(left)
    rights.append(right)
    rows, square = left.shape
    step = 512
    total = None
    for c in range(0, square, step):
        a = jnp.concatenate([ref[:, c : c + step] for ref in lefts], 0)
        b = jnp.concatenate([ref[:, c : c + step] for ref in rights], 0)
        part = dot_nt(a, b)
        total = part if total is None else total + part
    out[...] = jnp.zeros_like(out)
    for k in range(total.shape[0] // rows):
        out[ids[k]] = total[k * rows : (k + 1) * rows].astype(jnp.bfloat16)


def last_block(ids, block, occ, virt, lefts, rights):
    count = ids.shape[0]
    _, rows, square = block.shape
    vmem = pl.BlockSpec(memory_space=pltpu.VMEM)
    scratch = pltpu.VMEM((rows, square), jnp.bfloat16)
    return pl.pallas_call(
        functools.partial(last_kernel, len(lefts)),
        in_specs=[pl.BlockSpec(memory_space=pltpu.SMEM)] + [vmem] * (3 + 2 * len(lefts)),
        out_specs=vmem,
        out_shape=jax.ShapeDtypeStruct((2 * count, rows, count * rows), jnp.bfloat16),
        scratch_shapes=[scratch, scratch],
        compiler_params=pltpu.CompilerParams(vmem_limit_bytes=VMEM_LIMIT),
        name="last_block",
    )(ids, block, occ, virt, *lefts, *rights)


def finish_kernel(ri_count, ids, got, metric, chi, screen, even, odd):
    sources, rows, columns = got.shape
    kcount = ids.shape[1]
    width = columns // kcount
    even[...] = jnp.zeros_like(even)
    odd[...] = jnp.zeros_like(odd)

    def add(source_group, carry):
        for ri in range(ri_count):
            source = source_group * ri_count + ri
            for j in range(0, kcount, 2):
                piece = got[source, :, j * width : (j + 2) * width].astype(jnp.float32)
                even[ids[source, ri ^ j]] += piece
                odd[ids[source, ri ^ (j + 1)]] += piece
        return carry

    lax.fori_loop(0, sources // ri_count, add, 0)
    low = iota((rows, LANES), 1) < width
    for t in range(0, 2 * kcount, 2):
        first = even[t] + pltpu.roll(odd[t], width, 1)
        second = odd[t + 1] + pltpu.roll(even[t + 1], width, 1)
        chi[:, t * width : (t + 2) * width] = jnp.where(low, first, second)
    screen[...] = dot(chi[...].astype(jnp.bfloat16), metric[...])


def finish(ids, got, metric, ri_count):
    sources, rows, columns = got.shape
    total = metric.shape[0]
    blocks = 2 * ids.shape[1]
    scratch = pltpu.VMEM((blocks, rows, LANES), jnp.float32)
    vmem = pl.BlockSpec(memory_space=pltpu.VMEM)
    return pl.pallas_call(
        functools.partial(finish_kernel, ri_count),
        in_specs=[pl.BlockSpec(memory_space=pltpu.SMEM), vmem, vmem],
        out_specs=[vmem, vmem],
        out_shape=[jax.ShapeDtypeStruct((rows, total), jnp.float32)] * 2,
        scratch_shapes=[scratch, scratch],
        compiler_params=pltpu.CompilerParams(vmem_limit_bytes=VMEM_LIMIT),
        name="finish",
    )(ids, got, metric)


def swap(array, axes, step):
    count = lax.axis_size(axes)
    return lax.ppermute(array, axes, [(i, i ^ step) for i in range(count)])


def gathered(array, axis, step):
    other = swap(array, axis, step)
    upper = (lax.axis_index(axis) & step) != 0
    return jnp.where(upper, jnp.stack([other, array]), jnp.stack([array, other]))


def folded(coulomb, rows):
    own_rows, total = coulomb.shape
    return jnp.concatenate(jnp.split(coulomb, rows // own_rows, 1), 0)


def gather_metric(coulomb, other, ids):
    rows, total = coulomb.shape
    ri_count, pair_count = lax.axis_size("ri"), lax.axis_size("pair")
    other = jnp.concatenate(jnp.split(other, other.shape[0] // rows, 0), 1)
    upper = (lax.axis_index("ri") & 2) != 0
    out = jnp.where(upper, jnp.stack([other, coulomb]), jnp.stack([coulomb, other]))
    step = 4
    while step < ri_count:
        out = gathered(out, "ri", step).reshape(-1, rows, total)
        step *= 2
    out = out.reshape(1, -1, total)
    count, kcount = ids.shape
    riding = jnp.pad(ids.astype(jnp.bfloat16), ((0, out.shape[1] - count), (0, LANES - kcount)))
    out = jnp.concatenate([out, riding[None]], 2)
    step = 1
    while step < pair_count:
        out = gathered(out, "pair", step)
        out = out.reshape((-1,) + out.shape[2:])
        step *= 2
    all_ids = out[:, :count, total : total + kcount].astype(jnp.int32).reshape(-1, kcount)
    out = gathered(out[:, :, :total], "ri", 1)
    out = out.reshape(2, -1, rows, total).swapaxes(0, 1).reshape(-1, total)
    return out, all_ids


def shards(three_c, green_occ, green_virt, pair_size, ri_ids, coulomb):
    everyone = ("pair", "ri")
    ri_count = lax.axis_size("ri")
    devices = lax.axis_size(everyone)
    here = lax.axis_index("ri")
    kcount = ri_ids.shape[1]
    pairs, _, rows, square = three_c.shape
    three_c = three_c.reshape(pairs, rows, square)

    parts = {}
    before = here
    for step in list(range(2, ri_count)) + [1]:
        part = lax.dynamic_slice_in_dim(three_c, before ^ step, 1, 0)
        if step == 2:
            part = jnp.concatenate([part, folded(coulomb, rows)[None]], 2)
        part, before = lax.optimization_barrier((part, here))
        parts[step] = swap(part, "ri", step)
    metric, all_ids = gather_metric(coulomb, parts[2][0, :, square:], ri_ids)

    pick = lambda array: lax.dynamic_index_in_dim(array, here, 0, keepdims=False)
    scalars = jnp.stack([here, pick(pair_size)]).astype(jnp.int32)
    ids = pick(ri_ids)[here ^ jnp.arange(kcount, dtype=jnp.int32)]
    occ, virt, left, right = first_blocks(scalars, three_c, parts[1], green_occ, green_virt)
    lefts, rights = [left], [right]
    for step in range(2, ri_count - 1):
        left, right = next_block(parts[step], occ, virt, square)
        lefts.append(left)
        rights.append(right)
    pieces = last_block(ids, parts[ri_count - 1], occ, virt, lefts, rights)
    pieces = pieces.reshape(devices, -1, kcount * rows)
    got = lax.all_to_all(pieces, everyone, 0, 0, tiled=True)
    return tuple(finish(all_ids, got, metric, ri_count))


def solution(mesh):
    placed = (
        P(("snap", "pair"), "ri", None, None),
        P(("snap", "pair"), None, None),
        P(("snap", "pair"), None, None),
        P(("snap", "pair")),
        P(("snap", "pair"), None),
        P(("snap", "pair", "ri"), None),
    )
    return jax.shard_map(
        shards,
        mesh=mesh,
        in_specs=placed,
        out_specs=(P(("snap", "pair", "ri"), None), P(("snap", "pair", "ri"), None)),
        check_vma=False,
    )
```

time: 75.9 us -> 55 us (0.72)
  Pallas kernels: 18.7 us -> 10.8 us
  waiting for transfers between devices: 29.9 us -> 22 us
  starting transfers between devices: 18.2 us -> 12.6 us
  other arithmetic: 1.38 us -> 3.49 us
  local copies, waits for them, and re-layouts: 6.38 us -> 5 us
    ppermute x9 -> x6, waiting for transfers between devices: 29.7 us -> 14.8 us  [swap(): return lax.ppermute(array, axes, [(i, i ^ step) for i in range(count)])]
    pallas_call x6 -> x3, Pallas kernels: 17 us -> 9.1 us  [the longest x1 4.05 us: first_blocks(): pl.pallas_call(first_kernel, grid_spec=pltpu.PrefetchScalarGridSpec(num_s...]
    all_to_all x1, waiting for transfers between devices: 0.19 us -> 7.16 us  [shards(): got = lax.all_to_all(pieces, everyone, 0, 0, tiled=True)]
    ppermute x9 -> x6, starting transfers between devices: 14.3 us -> 8.77 us  [swap(): return lax.ppermute(array, axes, [(i, i ^ step) for i in range(count)])]
    unnamed x14 -> x12, local copies, waits for them, and re-layouts: 2.43 us -> 0.04 us
    select_n x7 -> x3, other arithmetic: 0.12 us -> 1.78 us  [gathered(): jnp.where(upper, jnp.stack([other, array]), jnp.stack([array, other]))]
    split x0 -> x2, local copies, waits for them, and re-layouts: none -> 0.89 us  [the longest x1 0.89 us: folded(): return jnp.concatenate(jnp.split(coulomb, rows // own_rows, 1), 0)]
    concatenate x0 -> x2, other arithmetic: none -> 0.86 us  [the longest x1 0.84 us: shards(): part = jnp.concatenate([part, folded(coulomb, rows)[None]], 2)]
  transfers between devices with their start and end apart: 10 -> 7, of which waited for: 4 -> 4; matrix products, arithmetic and copies ran while one was open for 3% -> 10% of each run, Pallas kernels for 23% -> 17%
where the time goes in v3:
time: 55 us; the launch traced here: 54.7 us
  waiting for transfers between devices  22 us (40%)
  starting transfers between devices  12.6 us (23%)
  Pallas kernels  10.8 us (20%)
  local copies, waits for them, and re-layouts  5 us (9%)
  other arithmetic  3.49 us (6%)
  between operations  0.79 us (1%)
    ppermute x6, waiting for transfers between devices, swap(): return lax.ppermute(array, axes, [(i, i ^ step) for i in range(count)])  14.8 us
    ppermute x6, starting transfers between devices, swap(): return lax.ppermute(array, axes, [(i, i ^ step) for i in range(count)])  8.77 us
    all_to_all x1, waiting for transfers between devices, shards(): got = lax.all_to_all(pieces, everyone, 0, 0, tiled=True)  7.16 us
    pallas_call x1, Pallas kernels, first_blocks(): pl.pallas_call(first_kernel, grid_spec=pltpu.PrefetchScalarGridSpec(num_s...  4.05 us
    pallas_call x1, Pallas kernels, last_block(): pl.pallas_call(functools.partial(last_kernel, len(lefts)), in_specs=[pl.B...  3.95 us
    all_to_all x1, starting transfers between devices, shards(): got = lax.all_to_all(pieces, everyone, 0, 0, tiled=True)  3.88 us
    dynamic_slice x3, local copies, waits for them, and re-layouts, shards(): part = lax.dynamic_slice_in_dim(three_c, before ^ step, 1, 0)  2.78 us
    select_n x3, other arithmetic, gathered(): jnp.where(upper, jnp.stack([other, array]), jnp.stack([array, other]))  1.78 us
  transfers between devices with their start and end apart: 7, of which 4 were waited for; matrix products, arithmetic and copies ran while one was open for 10% of the time, Pallas kernels for 17%

profile of v3, /device:TPU:0, one launch (start us, length us, event | category | flops | bytes accessed | tf_op | source)
XLA Modules:
  0.0 54.7 jit_solution(12067552559761449570)
XLA Ops:
  0.6 0.0 copy-start
  0.6 0.9 %fusion.4 = (bf16[32,256]{1,0:T(8,128)(2,1)S(1)}, bf16[32,256]{1,0:T(8,128)(2,1)S(1)}) fusion(bf16[32,512]{1,0:T(8,128)(2,1)} %param.11), kind=kLoop, calls=%fused_computation.24 | loop fusion | bytes 65536 | tf_op jit(solution)/shard_map/split | solution.py:216
  1.5 0.0 copy-start.5
  1.6 0.0 copy-start.3
  1.6 1.1 %dynamic-slice_bitcast_fusion.2 = bf16[1,64,4096]{2,1,0:T(8,128)(2,1)S(1)} fusion(bf16[4,1,64,4096]{3,2,1,0:T(8,128)(2,1)} %param.6, s32[]{:T(128)S(6)} %select_n.89), kind=kLoop, calls=%fused_computation.6 | loop fusion | bytes 1048580 | tf_op jit(solution)/shard_map/dynamic_slice | solution.py:256
  2.7 0.0 copy-start.1
  2.7 0.0 copy-start.2
  2.7 0.8 %pad_maximum_fusion = bf16[1,64,4352]{2,1,0:T(8,128)(2,1)} fusion(bf16[1,64,256]{2,1,0:T(8,128)(2,1)S(1)} %maximum_bitcast_fusion, bf16[1,64,4096]{2,1,0:T(8,128)(2,1)S(1)} %dynamic-slice_bitcast_fusion.2), kind=kLoop, calls=%fused_computation.1 | loop fusion | flops 1114112 | bytes 1114112 | tf_op jit(solution)/shard_map/concatenate | solution.py:258
  3.5 2.9 %collective-permute-start = (bf16[1,64,4352]{2,1,0:T(8,128)(2,1)}, bf16[1,64,4352]{2,1,0:T(8,128)(2,1)S(1)}, u32[]{:S(2)}, u32[]{:S(2)}) collective-permute-start(bf16[1,64,4352]{2,1,0:T(8,128)(2,1)} %pad_maximum_fusion), channel_id=1, source_target_pairs={{0,2},{1,3},{2,0},{3,1},{4,6},{5,7},{6,4},{7,5},{8,10},{9,11},{10,... | collective-permute-start | bytes 1671176 | tf_op jit(solution)/shard_map/ppermute | solution.py:205
  6.5 0.8 %dynamic-slice_bitcast_fusion.1 = bf16[1,64,4096]{2,1,0:T(8,128)(2,1)} fusion(bf16[4,1,64,4096]{3,2,1,0:T(8,128)(2,1)S(1)} %copy-done, s32[]{:T(128)S(6)} %select_n.99), kind=kLoop, calls=%fused_computation.5 | loop fusion | bytes 1048580 | tf_op jit(solution)/shard_map/dynamic_slice | solution.py:256
  7.3 0.8 %dynamic-slice_bitcast_fusion = bf16[1,64,4096]{2,1,0:T(8,128)(2,1)} fusion(bf16[4,1,64,4096]{3,2,1,0:T(8,128)(2,1)S(1)} %copy-done, s32[]{:T(128)S(6)} %select_n.100), kind=kLoop, calls=%fused_computation.4 | loop fusion | bytes 1048580 | tf_op jit(solution)/shard_map/dynamic_slice | solution.py:256
  8.2 0.1 collective-permute-start.4
  8.3 0.6 %dynamic_slice.28 = s32[1]{0:T(128)} dynamic-slice(s32[4]{0:T(128)S(1)} %copy-done.5, s32[]{:T(128)S(6)} %select_n.97), dynamic_slice_sizes={1} | dynamic-slice | bytes 12 | tf_op jit(solution)/shard_map/jit(dynamic_index_in_dim)/dynamic_slice | solution.py:263
  8.9 11.2 %collective-permute-done.block = bf16[1,64,4352]{2,1,0:T(8,128)(2,1)S(1)} collective-permute-done((bf16[1,64,4352]{2,1,0:T(8,128)(2,1)}, bf16[1,64,4352]{2,1,0:T(8,128)(2,1)S(1)}, u32[]{:S(2)}, u32[]{:S(2)}) %collective-permute-start) | collective-permute-done | bytes 557088 | tf_op jit(solution)/shard_map/ppermute | solution.py:205
  20.2 2.2 %collective-permute-start.1 = (bf16[1,64,640]{2,1,0:T(8,128)(2,1)S(1)}, bf16[1,64,640]{2,1,0:T(8,128)(2,1)S(1)}, u32[]{:S(2)}, u32[]{:S(2)}) collective-permute-start(bf16[1,64,640]{2,1,0:T(8,128)(2,1)S(1)} %get-tuple-element.26), channel_id=1, source_target_pairs={{0,4},{4,0},{8,12},{12,8},{1,5},{5,1},{9,13},{13,9},{2,6},{6,2},{1... | collective-permute-start | bytes 245768 | tf_op jit(solution)/shard_map/ppermute | solution.py:205
  22.4 2.4 %collective-permute-done.1 = bf16[1,64,640]{2,1,0:T(8,128)(2,1)S(1)} collective-permute-done((bf16[1,64,640]{2,1,0:T(8,128)(2,1)S(1)}, bf16[1,64,640]{2,1,0:T(8,128)(2,1)S(1)}, u32[]{:S(2)}, u32[]{:S(2)}) %collective-permute-start.1) | collective-permute-done | bytes 81952 | tf_op jit(solution)/shard_map/ppermute | solution.py:205
  24.8 0.7 %maximum_select_fusion.2 = bf16[2,64,640]{2,1,0:T(8,128)(2,1)} fusion(bf16[1,64,128]{2,1,0:T(8,128)(2,1)S(1)} %pad_bitcast_fusion, bf16[1,64,512]{2,1,0:T(8,128)(2,1)S(1)} %bitcast.43, bf16[1,64,640]{2,1,0:T(8,128)(2,1)S(1)} %collective-permute-done.1, pred[]{:T(512)S(6)} %ne.13), kind=kLoop, calls=%fused_computation.8 | loop fusion | flops 1064960 | bytes 327681 | tf_op jit(solution)/shard_map/jit(_where)/select_n | solution.py:211
  25.5 3.0 %collective-permute-start.2 = (bf16[2,64,640]{2,1,0:T(8,128)(2,1)}, bf16[2,64,640]{2,1,0:T(8,128)(2,1)}, u32[]{:S(2)}, u32[]{:S(2)}) collective-permute-start(bf16[2,64,640]{2,1,0:T(8,128)(2,1)} %maximum_select_fusion.2), channel_id=1, source_target_pairs={{0,8},{4,12},{8,0},{12,4},{1,9},{5,13},{9,1},{13,5},{2,10},{6,14},... | collective-permute-start | bytes 491528 | tf_op jit(solution)/shard_map/ppermute | solution.py:205
  28.5 0.7 %pad_add_fusion.scalars = s32[2]{0:T(128)S(1)} fusion(s32[1]{0:T(128)} %dynamic_slice.28, s32[1]{0:T(128)} %bitcast.16), kind=kLoop, calls=%fused_computation.22 | loop fusion | flops 2 | bytes 16 | tf_op jit(solution)/shard_map/stack | solution.py:264
  29.3 0.6 %gather_fusion = s32[4]{0:T(128)S(1)} fusion(s32[4]{0:T(128)S(1)} %fusion.1, s32[1024]{0:T(1024)S(1)} %pad_clamp_fusion), kind=kCustom, calls=%fused_computation | custom fusion | bytes 48 | tf_op jit(solution)/shard_map/gather | solution.py:265
  29.9 4.0 %first_blocks.1 = (bf16[256,256]{1,0:T(8,128)(2,1)S(1)}, bf16[512,512]{1,0:T(8,128)(2,1)S(1)}, bf16[128,4096]{1,0:T(8,128)(2,1)S(1)}, bf16[128,4096]{1,0:T(8,128)(2,1)S(1)}) custom-call(s32[2]{0:T(128)S(1)} %pad_add_fusion.scalars, bf16[4,64,4096]{2,1,0:T(8,128)(2,1)S(1)} %bitcast.37, bf16[1,64,4096]{2,1,0:T(8,128)(2,1)} %collective-permute-done.4.other, ...), custom_call_target="tpu_custom_call" | custom-call | tf_op jit(solution)/shard_map/first_blocks/pallas_call | solution.py:95
  34.0 1.1 %next_block.1 = (bf16[64,4096]{1,0:T(8,128)(2,1)S(1)}, bf16[64,4096]{1,0:T(8,128)(2,1)S(1)}) custom-call(bf16[1,64,4352]{2,1,0:T(8,128)(2,1)S(1)} %collective-permute-done.block, bf16[256,256]{1,0:T(8,128)(2,1)S(1)} %get-tuple-element.18.occ, bf16[512,512]{1,0:T(8,128)(2,1)S(1)} %get-tuple-element.19.virt), custom_call_target="tpu_custom_call" | custom-call | tf_op jit(solution)/shard_map/next_block/pallas_call | solution.py:116
  35.1 0.0 collective-permute-done.3.block
  35.1 4.0 %last_block.1 = bf16[8,64,256]{2,1,0:T(8,128)(2,1)} custom-call(s32[4]{0:T(128)S(1)} %gather_fusion, bf16[1,64,4096]{2,1,0:T(8,128)(2,1)S(1)} %collective-permute-done.3.block, bf16[256,256]{1,0:T(8,128)(2,1)S(1)} %get-tuple-element.18.occ, bf16[512,512]{1,0:T(8,128)(2,1)S(1)} %get-tuple-element.19.virt, bf16[128,4096]{1,0:T(8,128)(2,1)S(1)} %get-tuple-element.20.refs_0_, ...), custom_call_target="tpu_custom_call" | custom-call | tf_op jit(solution)/shard_map/last_block/pallas_call | solution.py:150
  39.0 3.9 %all-to-all-start = ((bf16[16,32,256]{2,1,0:T(8,128)(2,1)}), bf16[16,32,256]{2,1,0:T(8,128)(2,1)S(1)}, u32[]{:S(2)}, u32[]{:S(2)}) async-start(bf16[16,32,256]{2,1,0:T(8,128)(2,1)} %bitcast.19), calls=%async_computation | async-start | bytes 524288 | tf_op jit(solution)/shard_map/all_to_all | solution.py:274
  43.0 0.0 collective-permute-done.2
  43.0 1.1 %maximum_select_fusion.1 = bf16[2,2,64,640]{3,2,1,0:T(8,128)(2,1)S(1)} fusion(bf16[1,2,64,640]{3,2,1,0:T(8,128)(2,1)S(1)} %maximum_select_fusion.3, bf16[1,2,64,640]{3,2,1,0:T(8,128)(2,1)} %bitcast.8, pred[]{:T(512)S(6)} %ne.12), kind=kLoop, calls=%fused_computation.7 | loop fusion | flops 491520 | bytes 655361 | tf_op jit(solution)/shard_map/jit(_where)/select_n | solution.py:211
  44.1 0.5 collective-permute-start.5
  44.5 1.1 %collective-permute-done.5 = bf16[4,64,512]{2,1,0:T(8,128)(2,1)S(1)} collective-permute-done((bf16[4,64,512]{2,1,0:T(8,128)(2,1)S(1)}, bf16[4,64,512]{2,1,0:T(8,128)(2,1)S(1)}, u32[]{:S(2)}, u32[]{:S(2)}) %collective-permute-start.5) | collective-permute-done | bytes 262176 | tf_op jit(solution)/shard_map/ppermute | solution.py:205
  45.7 0.1 fusion
  45.8 7.2 %all-to-all-done.got = bf16[16,32,256]{2,1,0:T(8,128)(2,1)S(1)} async-done(((bf16[16,32,256]{2,1,0:T(8,128)(2,1)}), bf16[16,32,256]{2,1,0:T(8,128)(2,1)S(1)}, u32[]{:S(2)}, u32[]{:S(2)}) %all-to-all-start) | async-done | bytes 262176 | tf_op jit(solution)/shard_map/all_to_all | solution.py:274
  53.0 1.7 %finish.1 = (f32[32,512]{1,0:T(8,128)}, f32[32,512]{1,0:T(8,128)}) custom-call(s32[16,4]{1,0:T(8,128)S(1)} %convert.1.ids, bf16[16,32,256]{2,1,0:T(8,128)(2,1)S(1)} %all-to-all-done.got, bf16[512,512]{1,0:T(8,128)(2,1)S(1)} %bitcast.38), custom_call_target="tpu_custom_call" | custom-call | tf_op jit(solution)/shard_map/finish/pallas_call | solution.py:192
  (24 shorter events, 0.2 us)
Async XLA Ops:
  0.6 5.8 %copy-start = (bf16[4,1,64,4096]{3,2,1,0:T(8,128)(2,1)S(1)}, bf16[4,1,64,4096]{3,2,1,0:T(8,128)(2,1)}, u32[]{:S(2)}) copy-start(bf16[4,1,64,4096]{3,2,1,0:T(8,128)(2,1)} %param.6) | copy-start | bytes 6291460
  1.5 6.7 %copy-start.4 = (s32[4,4]{1,0:T(4,128)S(1)}, s32[4,4]{1,0:T(4,128)}, u32[]{:S(2)}) copy-start(s32[4,4]{1,0:T(4,128)} %param.10) | copy-start | bytes 196
  1.5 6.7 %copy-start.5 = (s32[4]{0:T(128)S(1)}, s32[4]{0:T(128)}, u32[]{:S(2)}) copy-start(s32[4]{0:T(128)} %param.9) | copy-start | bytes 52
  1.6 18.6 %copy-start.3 = (bf16[32,512]{1,0:T(8,128)(2,1)S(1)}, bf16[32,512]{1,0:T(8,128)(2,1)}, u32[]{:S(2)}) copy-start(bf16[32,512]{1,0:T(8,128)(2,1)} %param.11) | copy-start | bytes 98308
  2.7 27.2 %copy-start.1 = (bf16[4,64,64]{2,1,0:T(8,128)(2,1)S(1)}, bf16[4,64,64]{2,1,0:T(8,128)(2,1)}, u32[]{:S(2)}) copy-start(bf16[4,64,64]{2,1,0:T(8,128)(2,1)} %occ.1) | copy-start | bytes 98308
  2.7 27.2 %copy-start.2 = (bf16[4,64,64]{2,1,0:T(8,128)(2,1)S(1)}, bf16[4,64,64]{2,1,0:T(8,128)(2,1)}, u32[]{:S(2)}) copy-start(bf16[4,64,64]{2,1,0:T(8,128)(2,1)} %virt.1) | copy-start | bytes 98308
  3.5 16.6 %collective-permute-start = (bf16[1,64,4352]{2,1,0:T(8,128)(2,1)}, bf16[1,64,4352]{2,1,0:T(8,128)(2,1)S(1)}, u32[]{:S(2)}, u32[]{:S(2)}) collective-permute-start(bf16[1,64,4352]{2,1,0:T(8,128)(2,1)} %pad_maximum_fusion), channel_id=1, source_target_pairs={{0,2},{1,3},{2,0},{3,1},{4,6},{5,7},{6,4},{7,5},{8,10},{9,11},{10,... | collective-permute-start | bytes 1671176 | tf_op jit(solution)/shard_map/ppermute | solution.py:205
  7.3 27.8 %collective-permute-start.3 = (bf16[1,64,4096]{2,1,0:T(8,128)(2,1)}, bf16[1,64,4096]{2,1,0:T(8,128)(2,1)S(1)}, u32[]{:S(2)}, u32[]{:S(2)}) collective-permute-start(bf16[1,64,4096]{2,1,0:T(8,128)(2,1)} %dynamic-slice_bitcast_fusion.1), channel_id=1, source_target_pairs={{0,3},{1,2},{2,1},{3,0},{4,7},{5,6},{6,5},{7,4},{8,11},{9,10},{10,... | collective-permute-start | bytes 1572872 | tf_op jit(solution)/shard_map/ppermute | solution.py:205
  8.2 21.7 %collective-permute-start.4 = (bf16[1,64,4096]{2,1,0:T(8,128)(2,1)}, bf16[1,64,4096]{2,1,0:T(8,128)(2,1)}, u32[]{:S(2)}, u32[]{:S(2)}) collective-permute-start(bf16[1,64,4096]{2,1,0:T(8,128)(2,1)} %dynamic-slice_bitcast_fusion), channel_id=1, source_target_pairs={{0,1},{1,0},{2,3},{3,2},{4,5},{5,4},{6,7},{7,6},{8,9},{9,8},{10,11... | collective-permute-start | bytes 1572872 | tf_op jit(solution)/shard_map/ppermute | solution.py:205
  20.2 4.6 %collective-permute-start.1 = (bf16[1,64,640]{2,1,0:T(8,128)(2,1)S(1)}, bf16[1,64,640]{2,1,0:T(8,128)(2,1)S(1)}, u32[]{:S(2)}, u32[]{:S(2)}) collective-permute-start(bf16[1,64,640]{2,1,0:T(8,128)(2,1)S(1)} %get-tuple-element.26), channel_id=1, source_target_pairs={{0,4},{4,0},{8,12},{12,8},{1,5},{5,1},{9,13},{13,9},{2,6},{6,2},{1... | collective-permute-start | bytes 245768 | tf_op jit(solution)/shard_map/ppermute | solution.py:205
  25.5 17.5 %collective-permute-start.2 = (bf16[2,64,640]{2,1,0:T(8,128)(2,1)}, bf16[2,64,640]{2,1,0:T(8,128)(2,1)}, u32[]{:S(2)}, u32[]{:S(2)}) collective-permute-start(bf16[2,64,640]{2,1,0:T(8,128)(2,1)} %maximum_select_fusion.2), channel_id=1, source_target_pairs={{0,8},{4,12},{8,0},{12,4},{1,9},{5,13},{9,1},{13,5},{2,10},{6,14},... | collective-permute-start | bytes 491528 | tf_op jit(solution)/shard_map/ppermute | solution.py:205
  39.0 13.9 %all-to-all-start = ((bf16[16,32,256]{2,1,0:T(8,128)(2,1)}), bf16[16,32,256]{2,1,0:T(8,128)(2,1)S(1)}, u32[]{:S(2)}, u32[]{:S(2)}) async-start(bf16[16,32,256]{2,1,0:T(8,128)(2,1)} %bitcast.19), calls=%async_computation | async-start | bytes 524288 | tf_op jit(solution)/shard_map/all_to_all | solution.py:274
  44.1 1.6 %collective-permute-start.5 = (bf16[4,64,512]{2,1,0:T(8,128)(2,1)S(1)}, bf16[4,64,512]{2,1,0:T(8,128)(2,1)S(1)}, u32[]{:S(2)}, u32[]{:S(2)}) collective-permute-start(bf16[4,64,512]{2,1,0:T(8,128)(2,1)S(1)} %slice.16), channel_id=1, source_target_pairs={{0,1},{1,0},{2,3},{3,2},{4,5},{5,4},{6,7},{7,6},{8,9},{9,8},{10,11... | collective-permute-start | bytes 786440 | tf_op jit(solution)/shard_map/ppermute | solution.py:205

commit v4 on v1

v4 whole, which is shorter than its diff:
```python
import functools

import jax
import jax.numpy as jnp
from jax import lax
from jax.experimental import pallas as pl
from jax.experimental.pallas import tpu as pltpu
from jax.sharding import PartitionSpec as P

LANES = 128
SUB = 8
TOKEN = (16, 128)
VMEM_LIMIT = 20 * 1024 * 1024
SMALL_LIMIT = 4 * 1024 * 1024
VMEM = pl.BlockSpec(memory_space=pltpu.VMEM)
SMEM = pl.BlockSpec(memory_space=pltpu.SMEM)
ANY = pl.BlockSpec(memory_space=pl.ANY)


def iota(shape, dim):
    return lax.broadcasted_iota(jnp.int32, shape, dim)


def one(hit):
    return jnp.where(hit, 1.0, 0.0).astype(jnp.bfloat16)


def dot(a, b):
    return jnp.dot(a, b, preferred_element_type=jnp.float32)


def dot_nt(a, b):
    return lax.dot_general(a, b, (((1,), (1,)), ((), ())), preferred_element_type=jnp.float32)


def half(shape):
    return jax.ShapeDtypeStruct(shape, jnp.bfloat16)


def far(shape):
    return pltpu.HBM(shape, jnp.bfloat16)


def near(shape):
    return pltpu.VMEM(shape, jnp.bfloat16)


def in_near(array):
    return pltpu.with_memory_space_constraint(array, pltpu.VMEM)


def in_far(array):
    return pltpu.with_memory_space_constraint(array, pltpu.HBM)


def started(sems, pairs):
    copies = [pltpu.make_async_copy(a, b, sems.at[i]) for i, (a, b) in enumerate(pairs)]
    for copy in copies:
        copy.start()
    return copies


def finished(copies):
    for copy in copies:
        copy.wait()


def limit(size):
    return pltpu.CompilerParams(vmem_limit_bytes=size)


def pick_kernel(step, first, riding, pieces, *refs):
    three_c = refs[0]
    out, token, held, sems_in, sems_out = refs[-5:]
    token[...] = jnp.zeros_like(token)
    count, _ = held.shape
    square = three_c.shape[2]
    here = lax.axis_index("ri")
    step_rows = count // pieces
    pairs_in, pairs_out = [], []
    if riding:
        coulomb = refs[1]
        rows, total = coulomb.shape
        fold = count // rows
        wide = total // fold
        for i in range(fold):
            there = held.at[pl.ds(i * rows, rows), pl.ds(square, wide)]
            pairs_in.append((coulomb.at[:, pl.ds(i * wide, wide)], there))
    rides = len(pairs_in)
    for i in range(pieces):
        at = pl.ds(i * step_rows, step_rows)
        source = three_c.at[here ^ step, pl.ds(first + i * step_rows, step_rows)]
        pairs_in.append((source, held.at[at, pl.ds(0, square)]))
        pairs_out.append((held.at[at], out.at[0, at]))
    copies = started(sems_in, pairs_in)
    finished(copies[:rides])
    going = []
    for i, (a, b) in enumerate(pairs_out):
        copies[rides + i].wait()
        copy = pltpu.make_async_copy(a, b, sems_out.at[i])
        copy.start()
        going.append(copy)
    finished(going)


def pick(three_c, step, first, count, coulomb=None, hold=None):
    square = three_c.shape[2]
    riding = coulomb is not None
    operands = [in_far(three_c)] + [in_far(a) for a in (coulomb,) if a is not None] + [a for a in (hold,) if a is not None]
    extra = coulomb.size // count if riding else 0
    rides = count // coulomb.shape[0] if riding else 0
    pieces = count // 16
    return pl.pallas_call(
        functools.partial(pick_kernel, step, first, riding, pieces),
        in_specs=[ANY] * (len(operands) - (hold is not None)) + [VMEM] * (hold is not None),
        out_specs=[ANY, VMEM],
        out_shape=[far((1, count, square + extra)), half(TOKEN)],
        scratch_shapes=[
            pltpu.VMEM((count, square + extra), jnp.bfloat16),
            pltpu.SemaphoreType.DMA((rides + pieces,)),
            pltpu.SemaphoreType.DMA((pieces,)),
        ],
        compiler_params=limit(SMALL_LIMIT),
        name="pick",
    )(*operands)


def along_x_kernel(block, coulomb, ids, hold, out):
    rows, total = coulomb.shape
    upper = (lax.axis_index("ri") & 2) != 0
    own = coulomb[...]
    fold = block.shape[1] // rows
    tail = block[0]
    other = jnp.concatenate([tail[i * rows : (i + 1) * rows] for i in range(fold)], 1)
    out[0, :rows, :total] = jnp.where(upper, other, own)
    out[0, rows:, :total] = jnp.where(upper, own, other)
    out[0, :, total:] = ids[...]


def rows_along_x(block, coulomb, ids, hold):
    rows, total = coulomb.shape
    return pl.pallas_call(
        along_x_kernel,
        in_specs=[VMEM] * 4,
        out_specs=VMEM,
        out_shape=half((1, 2 * rows, total + LANES)),
        compiler_params=limit(SMALL_LIMIT),
        name="rows_along_x",
    )(block, coulomb, ids, hold)


def prepared(size, occ, virt, occ_out, virt_out):
    width = occ.shape[0]
    full = occ_out.shape[0]
    spread = one(iota((full, width), 0) % width == iota((full, width), 1))
    tiled = dot_nt(dot(spread, occ).astype(jnp.bfloat16), spread)
    same = iota((full, full), 0) // width == iota((full, full), 1) // width
    occ_out[...] = jnp.where(same, tiled, 0.0).astype(jnp.bfloat16)

    keep = (iota((width, width), 0) < size) & (iota((width, width), 1) < size)
    kept = jnp.where(keep, virt.astype(jnp.float32), 0.0).astype(jnp.bfloat16)
    side = virt_out.shape[0] // 2
    same = iota((side, 2 * side), 0) % SUB == iota((side, 2 * side), 1) % SUB
    for parity in range(2):
        wanted = 2 * (iota((side, width), 0) // SUB) + parity
        picked_rows = one(wanted == iota((side, width), 1))
        column = iota((2 * side, width), 0)
        wanted = 2 * (column % side // SUB) + (column // side + parity) % 2
        picked_columns = one(wanted == iota((2 * side, width), 1))
        part = dot_nt(dot(picked_rows, kept).astype(jnp.bfloat16), picked_columns)
        virt_out[parity * side : (parity + 1) * side, :] = jnp.where(same, part, 0.0).astype(jnp.bfloat16)


def transform(block, occ, virt, left, right):
    rows, square = right.shape
    full = occ.shape[0]
    chunks = square // LANES
    side = chunks * SUB
    wide = [block[:, c * full : (c + 1) * full] for c in range(square // full)]
    out = dot(jnp.concatenate(wide, 0), occ[...]).astype(jnp.bfloat16)
    for c in range(square // full):
        left[:, c * full : (c + 1) * full] = out[c * rows : (c + 1) * rows]
    low = iota((side, 2 * LANES), 1) % LANES < LANES // 2
    for row in range(0, rows, 2 * SUB):
        tile = block[row : row + 2 * SUB, :square].astype(jnp.float32)
        plain, turned = [], []
        for i in range(2):
            part = tile[i * SUB : (i + 1) * SUB]
            stacked = jnp.concatenate([part[:, c * LANES : (c + 1) * LANES] for c in range(chunks)], 0)
            plain.append(stacked)
            turned.append(pltpu.roll(stacked, LANES // 2, 1))
        operand = jnp.concatenate([jnp.concatenate(plain, 1), jnp.concatenate(turned, 1)], 0)
        out = dot(virt[...], operand.astype(jnp.bfloat16))
        out = jnp.where(low, out[:side], out[side:])
        for c in range(chunks):
            piece = out[c * SUB : (c + 1) * SUB]
            piece = jnp.concatenate([piece[:, :LANES], piece[:, LANES:]], 0)
            right[row : row + 2 * SUB, c * LANES : (c + 1) * LANES] = piece.astype(jnp.bfloat16)


def first_kernel(sizes, ids, three_c, other, occ, virt, *refs):
    occ_out, virt_out, left, right, place_out, token, own, place, sem, sems = refs
    token[...] = jnp.zeros_like(token)
    here = lax.axis_index("ri")
    copy = pltpu.make_async_copy(three_c.at[here], own, sem)
    copy.start()
    prepared(sizes[here], occ[here], virt[here], occ_out, virt_out)
    rows, square = own.shape
    column = iota(place.shape, 1)
    wanted = jnp.zeros(place.shape, jnp.int32)
    for j in range(ids.shape[1]):
        wanted = jnp.where(column // rows == j, ids[here, here ^ j], wanted)
    row = iota(place.shape, 0)
    place[...] = one((row // rows == wanted) & (row % rows == column % rows))
    copies = started(sems, [(place, place_out)])
    copy.wait()
    for i, block in enumerate((own, other.at[0])):
        at = slice(i * rows, (i + 1) * rows)
        transform(block, occ_out, virt_out, left.at[at], right.at[at])
    finished(copies)


def first_blocks(three_c, other, occ, virt, sizes, ids):
    _, rows, square = three_c.shape
    width = occ.shape[-1]
    kcount = ids.shape[1]
    shapes = [(4 * width, 4 * width), (SUB * width, SUB * width)] + [(2 * rows, square)] * 2
    place = (2 * kcount * rows, kcount * rows)
    return pl.pallas_call(
        first_kernel,
        in_specs=[SMEM, SMEM, ANY, VMEM, VMEM, VMEM],
        out_specs=[VMEM] * 4 + [ANY, VMEM],
        out_shape=[near(shape) for shape in shapes] + [far(place), half(TOKEN)],
        scratch_shapes=[
            pltpu.VMEM((rows, square), jnp.bfloat16),
            pltpu.VMEM(place, jnp.bfloat16),
            pltpu.SemaphoreType.DMA,
            pltpu.SemaphoreType.DMA((1,)),
        ],
        compiler_params=limit(VMEM_LIMIT),
        name="first_blocks",
    )(sizes, ids, in_far(three_c), other, occ, virt)


def next_kernel(block, occ, virt, hold, left_out, right_out, token, left, right, sems):
    token[...] = jnp.zeros_like(token)
    transform(block.at[0], occ, virt, left, right)
    finished(started(sems, [(left, left_out), (right, right_out)]))


def next_block(block, occ, virt, hold, square):
    shape = (block.shape[1], square)
    return pl.pallas_call(
        next_kernel,
        in_specs=[VMEM] * 4,
        out_specs=[ANY, ANY, VMEM],
        out_shape=[far(shape), far(shape), half(TOKEN)],
        scratch_shapes=[pltpu.VMEM(shape, jnp.bfloat16)] * 2 + [pltpu.SemaphoreType.DMA((2,))],
        compiler_params=limit(VMEM_LIMIT),
        name="next_block",
    )(block, in_near(occ), in_near(virt), hold)


def last_kernel(count, block, occ, virt, left_first, right_first, place_far, *refs):
    out, left, right, place, sems = refs[2 * count :]
    pairs, row = [], 0
    for i in range(count):
        at = pl.ds(row, refs[i].shape[0])
        pairs += [(refs[i], left.at[at]), (refs[count + i], right.at[at])]
        row += refs[i].shape[0]
    copies = started(sems, pairs + [(place_far, place)])
    transform(block.at[0], occ, virt, left.at[row:], right.at[row:])
    finished(copies)
    square = left.shape[1]
    step = 1024
    total = None
    for c in range(0, square, step):
        a = jnp.concatenate([ref[:, c : c + step] for ref in (left_first, left)], 0)
        b = jnp.concatenate([ref[:, c : c + step] for ref in (right_first, right)], 0)
        part = dot_nt(a, b)
        total = part if total is None else total + part
    out[...] = dot(place[...], total.astype(jnp.bfloat16)).astype(jnp.bfloat16)


def last_block(block, occ, virt, place, lefts, rights):
    _, rows, square = block.shape
    count = len(lefts) - 1
    rest = (place.shape[1] - lefts[0].shape[0], square)
    scratch = [pltpu.VMEM(shape, jnp.bfloat16) for shape in (rest, rest, place.shape)]
    return pl.pallas_call(
        functools.partial(last_kernel, count),
        in_specs=[VMEM] * 5 + [ANY] * (1 + 2 * count),
        out_specs=VMEM,
        out_shape=half(place.shape),
        scratch_shapes=scratch + [pltpu.SemaphoreType.DMA((1 + 2 * count,))],
        compiler_params=limit(VMEM_LIMIT),
        name="last_block",
    )(block, *map(in_near, (occ, virt, lefts[0], rights[0])), *map(in_far, [place] + lefts[1:] + rights[1:]))


def finish_kernel(kcount, place, got, metric, chi, screen):
    rows, total = chi.shape
    blocks = 2 * kcount
    width = total // blocks
    placed = dot(place[...], got[...])
    low = iota((rows, LANES), 1) < width

    def block(t):
        straight, turned = None, None
        for j in range(kcount):
            at = (j * blocks + t) * rows
            piece = placed[at : at + rows, j // 2 * LANES : (j // 2 + 1) * LANES]
            if j % 2 == t % 2:
                straight = piece if straight is None else straight + piece
            else:
                turned = piece if turned is None else turned + piece
        return straight + pltpu.roll(turned, width, 1)

    for t in range(0, blocks, 2):
        chi[:, t * width : (t + 2) * width] = jnp.where(low, block(t), block(t + 1))
    screen[...] = dot(chi[...].astype(jnp.bfloat16), metric[...])


def finish(place, got, metric, kcount):
    total = metric.shape[0]
    rows = place.shape[0] // (2 * kcount * kcount)
    return pl.pallas_call(
        functools.partial(finish_kernel, kcount),
        in_specs=[VMEM] * 3,
        out_specs=[VMEM, VMEM],
        out_shape=[jax.ShapeDtypeStruct((rows, total), jnp.float32)] * 2,
        compiler_params=limit(VMEM_LIMIT),
        name="finish",
    )(place, got, metric)


def placing_kernel(hits, out):
    high, wide = hits.shape
    rows = out.shape[0] // high
    down = one(iota((high * rows, high), 0) // rows == iota((high * rows, high), 1))
    across = one(iota((wide * rows, wide), 0) // rows == iota((wide * rows, wide), 1))
    spread = dot_nt(dot(down, hits[...]).astype(jnp.bfloat16), across)
    same = iota(out.shape, 0) % rows == iota(out.shape, 1) % rows
    out[...] = jnp.where(same, spread, 0.0).astype(jnp.bfloat16)


def placing(hits, rows):
    return pl.pallas_call(
        placing_kernel,
        in_specs=[VMEM],
        out_specs=VMEM,
        out_shape=half((hits.shape[0] * rows, hits.shape[1] * rows)),
        compiler_params=limit(VMEM_LIMIT),
        name="placing",
    )(hits)


def swap(array, axes, step):
    count = lax.axis_size(axes)
    return lax.ppermute(array, axes, [(i, i ^ step) for i in range(count)])


def gathered(array, axis, step):
    other = swap(array, axis, step)
    upper = (lax.axis_index(axis) & step) != 0
    return jnp.where(upper, jnp.stack([other, array]), jnp.stack([array, other]))


def gather_metric(out, total, own_rows, pairs, kcount):
    ri_count, pair_count = lax.axis_size("ri"), lax.axis_size("pair")
    chips = ri_count // 4
    _, rows, wide = out.shape
    step = 4
    while step < ri_count:
        out = gathered(out, "ri", step).reshape(-1, rows, wide)
        step *= 2
    step = 1
    while step < pair_count:
        out = gathered(out, "pair", step).reshape(-1, rows, wide)
        step *= 2
    all_ids = out.reshape(pair_count, chips, rows, wide)[:, 0, :pairs, total : total + kcount]
    out = out[:, :, :total].reshape(-1, rows // 2, total)[:, :own_rows]
    out = gathered(out, "ri", 1).swapaxes(0, 1).reshape(-1, total)
    return out, all_ids.reshape(-1, kcount)


def shards(three_c, green_occ, green_virt, pair_size, ri_ids, coulomb):
    everyone = ("pair", "ri")
    ri_count = lax.axis_size("ri")
    devices = lax.axis_size(everyone)
    kcount = ri_ids.shape[1]
    blocks = 2 * kcount
    pairs, _, rows, square = three_c.shape
    out_rows, total = coulomb.shape
    three_c = three_c.reshape(pairs, rows, square)
    slots = jnp.arange(kcount, dtype=jnp.int32)
    block_ids = jnp.arange(blocks, dtype=jnp.int32)
    riding_rows = max(16, out_rows)
    riding = jnp.pad(coulomb, ((0, riding_rows - out_rows), (0, 0)))

    parts, token = {}, None
    for step in list(range(2, ri_count)) + [1]:
        part, token = pick(three_c, step, 0, rows, coulomb=riding if step == 2 else None, hold=token)
        parts[step] = swap(part, "ri", step)
    occ, virt, left, right, place, token = first_blocks(
        three_c, parts[1], green_occ, green_virt, pair_size, ri_ids
    )
    lefts, rights, held = [left], [right], []
    for step in range(2, ri_count - 1):
        left, right, token = next_block(parts[step], occ, virt, token, square)
        lefts.append(left)
        rights.append(right)
        held.append(token)
    pieces = last_block(parts[ri_count - 1], occ, virt, place, lefts, rights)

    slot = jnp.arange(pairs, dtype=jnp.int32)[:, None] ^ slots[None, :]
    relative = jnp.sum(jnp.where(slot[:, :, None] == slots, ri_ids[:, None, :], 0), 2)
    ids = jnp.pad(relative.astype(jnp.bfloat16), ((0, 2 * riding_rows - pairs), (0, LANES - kcount)))
    metric = rows_along_x(parts[2][:, :, square:], riding, ids, held[0])
    metric, all_ids = gather_metric(metric, total, out_rows, pairs, kcount)
    hits = all_ids.T[:, None, :] == block_ids.astype(jnp.bfloat16)[None, :, None]
    placed = placing(hits.astype(jnp.bfloat16).reshape(kcount * blocks, devices), out_rows)

    got = lax.all_to_all(pieces.reshape(devices, out_rows, kcount * rows), everyone, 0, 0, tiled=True)
    return tuple(finish(placed, got.reshape(devices * out_rows, kcount * rows), metric, kcount))


def solution(mesh):
    placed = (
        P(("snap", "pair"), "ri", None, None),
        P(("snap", "pair"), None, None),
        P(("snap", "pair"), None, None),
        P(("snap", "pair")),
        P(("snap", "pair"), None),
        P(("snap", "pair", "ri"), None),
    )
    return jax.shard_map(
        shards,
        mesh=mesh,
        in_specs=placed,
        out_specs=(P(("snap", "pair", "ri"), None), P(("snap", "pair", "ri"), None)),
        check_vma=False,
    )
```

time: 107 us -> 51.3 us (0.48)
  local copies, waits for them, and re-layouts: 35 us -> 0.25 us
  blocking collectives: 31.8 us -> 0 us
  Pallas kernels: 0 us -> 17.3 us
  matrix products: 14.8 us -> 0 us
  starting transfers between devices: 9.05 us -> 14.8 us
  waiting for transfers between devices: 13.6 us -> 15.7 us
  other arithmetic: 0.66 us -> 2.14 us
    all_gather x1 -> x0, blocking collectives: 19.4 us -> none  [shards(): metric = lax.all_gather(coulomb, everyone, axis=0, tiled=True)]
    pallas_call x0 -> x9, Pallas kernels: none -> 17.3 us  [the longest x3 6.13 us: pick(): pl.pallas_call(functools.partial(pick_kernel, step, first, riding, pieces...]
    dot_general x6 -> x0, matrix products: 14.8 us -> none  [the longest x1 5.5 us: block_products(): jnp.einsum('ms,krsl->krml', virt * keep, shaped, preferred_element_type=j...]
    reshape x4 -> x0, local copies, waits for them, and re-layouts: 12.6 us -> none  [the longest x1 6.61 us: block_products(): right = right.astype(jnp.bfloat16).reshape(kcount * rows, square)]
    unnamed x1 -> x0, blocking collectives: 12.4 us -> none
    all_to_all x1, waiting for transfers between devices: 0.01 us -> 7.23 us  [shards(): lax.all_to_all(pieces.reshape(devices, out_rows, kcount * rows), everyone...]
    concatenate x5 -> x0, local copies, waits for them, and re-layouts: 6.48 us -> none  [shards(): left, right = block_products(jnp.concatenate(parts, 0), occ, virt, size)]
    convert_element_type x1 -> x0, local copies, waits for them, and re-layouts: 6.3 us -> none  [block_products(): right = right.astype(jnp.bfloat16).reshape(kcount * rows, square)]
  transfers between devices with their start and end apart: 4 -> 7, of which waited for: 2 -> 5; matrix products, arithmetic and copies ran while one was open for 10% -> 5% of each run, Pallas kernels for 0% -> 28%
where the time goes in v4:
time: 51.3 us; the launch traced here: 50.9 us
  Pallas kernels  17.3 us (34%)
  waiting for transfers between devices  15.7 us (31%)
  starting transfers between devices  14.8 us (29%)
  other arithmetic  2.14 us (4%)
  between operations  0.78 us (2%)
    ppermute x6, starting transfers between devices, swap(): return lax.ppermute(array, axes, [(i, i ^ step) for i in range(count)])  8.95 us
    ppermute x6, waiting for transfers between devices, swap(): return lax.ppermute(array, axes, [(i, i ^ step) for i in range(count)])  8.45 us
    all_to_all x1, waiting for transfers between devices, shards(): lax.all_to_all(pieces.reshape(devices, out_rows, kcount * rows), everyone...  7.23 us
    pallas_call x3, Pallas kernels, pick(): pl.pallas_call(functools.partial(pick_kernel, step, first, riding, pieces...  6.13 us
    all_to_all x1, starting transfers between devices, shards(): lax.all_to_all(pieces.reshape(devices, out_rows, kcount * rows), everyone...  5.85 us
    pallas_call x1, Pallas kernels, last_block(): pl.pallas_call(functools.partial(last_kernel, count), in_specs=[VMEM] * 5...  4.32 us
    pallas_call x1, Pallas kernels, first_blocks(): pl.pallas_call(first_kernel, in_specs=[SMEM, SMEM, ANY, VMEM, VMEM, VMEM]...  3.19 us
    select_n x4, other arithmetic, gathered(): jnp.where(upper, jnp.stack([other, array]), jnp.stack([array, other]))  1.83 us
  transfers between devices with their start and end apart: 7, of which 5 were waited for; matrix products, arithmetic and copies ran while one was open for 5% of the time, Pallas kernels for 28%

profile of v4, /device:TPU:0, one launch (start us, length us, event | category | flops | bytes accessed | tf_op | source)
XLA Modules:
  0.0 50.9 jit_solution(3427761090367260050)
XLA Ops:
  0.6 1.9 %pick.3 = (bf16[1,64,4352]{2,1,0:T(8,128)(2,1)}, bf16[16,128]{1,0:T(8,128)(2,1)S(1)}) custom-call(bf16[4,64,4096]{2,1,0:T(8,128)(2,1)} %bitcast.21, bf16[32,512]{1,0:T(8,128)(2,1)} %coulomb.1), custom_call_target="tpu_custom_call" | custom-call | tf_op jit(solution)/shard_map/pick/pallas_call | solution.py:113
  2.5 3.0 %collective-permute-start = (bf16[1,64,4352]{2,1,0:T(8,128)(2,1)}, bf16[1,64,4352]{2,1,0:T(8,128)(2,1)S(1)}, u32[]{:S(2)}, u32[]{:S(2)}) collective-permute-start(bf16[1,64,4352]{2,1,0:T(8,128)(2,1)} %get-tuple-element.16), channel_id=1, source_target_pairs={{0,2},{1,3},{2,0},{3,1},{4,6},{5,7},{6,4},{7,5},{8,10},{9,11},{10,... | collective-permute-start | bytes 1671176 | tf_op jit(solution)/shard_map/ppermute | solution.py:360
  5.5 1.8 %pick.4 = (bf16[1,64,4096]{2,1,0:T(8,128)(2,1)}, bf16[16,128]{1,0:T(8,128)(2,1)S(1)}) custom-call(bf16[4,64,4096]{2,1,0:T(8,128)(2,1)} %bitcast.22, bf16[16,128]{1,0:T(8,128)(2,1)S(1)} %get-tuple-element.17.refs_1_), custom_call_target="tpu_custom_call" | custom-call | tf_op jit(solution)/shard_map/pick/pallas_call | solution.py:113
  7.4 2.4 %pick.5 = (bf16[1,64,4096]{2,1,0:T(8,128)(2,1)}, bf16[16,128]{1,0:T(8,128)(2,1)}) custom-call(bf16[4,64,4096]{2,1,0:T(8,128)(2,1)} %bitcast.23, bf16[16,128]{1,0:T(8,128)(2,1)S(1)} %get-tuple-element.18.refs_1_), custom_call_target="tpu_custom_call" | custom-call | tf_op jit(solution)/shard_map/pick/pallas_call | solution.py:113
  9.8 0.0 copy-start
  9.8 0.1 collective-permute-start.1
  9.9 0.2 collective-permute-start.4
  10.1 0.0 copy-done.3
  10.1 0.2 select_reduce_fusion
  10.3 1.7 %collective-permute-done.1.other = bf16[1,64,4096]{2,1,0:T(8,128)(2,1)S(1)} collective-permute-done((bf16[1,64,4096]{2,1,0:T(8,128)(2,1)}, bf16[1,64,4096]{2,1,0:T(8,128)(2,1)S(1)}, u32[]{:S(2)}, u32[]{:S(2)}) %collective-permute-start.1) | collective-permute-done | bytes 524320 | tf_op jit(solution)/shard_map/ppermute | solution.py:360
  12.0 0.0 copy-done.1
  12.0 0.0 copy-done.2
  12.0 3.2 %first_blocks.1 = (bf16[256,256]{1,0:T(8,128)(2,1)S(1)}, bf16[512,512]{1,0:T(8,128)(2,1)S(1)}, bf16[128,4096]{1,0:T(8,128)(2,1)S(1)}, bf16[128,4096]{1,0:T(8,128...) custom-call(s32[4]{0:T(128)S(1)} %copy-done.4, s32[4,4]{1,0:T(4,128)S(1)} %copy-done.3, ...), custom_call_target="tpu_custom_call" | custom-call | tf_op jit(solution)/shard_map/first_blocks/pallas_call | solution.py:229
  15.2 4.0 %collective-permute-done.block = bf16[1,64,4352]{2,1,0:T(8,128)(2,1)S(1)} collective-permute-done((bf16[1,64,4352]{2,1,0:T(8,128)(2,1)}, bf16[1,64,4352]{2,1,0:T(8,128)(2,1)S(1)}, u32[]{:S(2)}, u32[]{:S(2)}) %collective-permute-start) | collective-permute-done | bytes 557088 | tf_op jit(solution)/shard_map/ppermute | solution.py:360
  19.2 1.7 %next_block.1 = (bf16[64,4096]{1,0:T(8,128)(2,1)}, bf16[64,4096]{1,0:T(8,128)(2,1)}, bf16[16,128]{1,0:T(8,128)(2,1)S(1)}) custom-call(bf16[1,64,4352]{2,1,0:T(8,128)(2,1)S(1)} %collective-permute-done.block, bf16[256,256]{1,0:T(8,128)(2,1)S(1)} %get-tuple-element.20.occ, bf16[512,512]{1,0:T(8,128)(2,1)S(1)} %get-tuple-element.21.virt, ...), custom_call_target="tpu_custom_call" | custom-call | tf_op jit(solution)/shard_map/next_block/pallas_call | solution.py:253
  21.0 2.2 %collective-permute-start.2 = (bf16[1,64,640]{2,1,0:T(8,128)(2,1)S(1)}, bf16[1,64,640]{2,1,0:T(8,128)(2,1)S(1)}, u32[]{:S(2)}, u32[]{:S(2)}) collective-permute-start(bf16[1,64,640]{2,1,0:T(8,128)(2,1)S(1)} %rows_along_x.1), channel_id=1, source_target_pairs={{0,4},{4,0},{8,12},{12,8},{1,5},{5,1},{9,13},{13,9},{2,6},{6,2},{1... | collective-permute-start | bytes 245768 | tf_op jit(solution)/shard_map/ppermute | solution.py:360
  23.2 2.4 %collective-permute-done.2 = bf16[1,64,640]{2,1,0:T(8,128)(2,1)S(1)} collective-permute-done((bf16[1,64,640]{2,1,0:T(8,128)(2,1)S(1)}, bf16[1,64,640]{2,1,0:T(8,128)(2,1)S(1)}, u32[]{:S(2)}, u32[]{:S(2)}) %collective-permute-start.2) | collective-permute-done | bytes 81952 | tf_op jit(solution)/shard_map/ppermute | solution.py:360
  25.6 0.7 %maximum_select_fusion.2 = bf16[2,64,640]{2,1,0:T(8,128)(2,1)} fusion(bf16[1,64,640]{2,1,0:T(8,128)(2,1)S(1)} %rows_along_x.1, bf16[1,64,640]{2,1,0:T(8,128)(2,1)S(1)} %collective-permute-done.2, pred[]{:T(512)S(6)} %ne.10), kind=kLoop, calls=%fused_computation.2 | loop fusion | flops 245760 | bytes 327681 | tf_op jit(solution)/shard_map/jit(_where)/select_n | solution.py:366
  26.3 3.0 %collective-permute-start.3 = (bf16[2,64,640]{2,1,0:T(8,128)(2,1)}, bf16[2,64,640]{2,1,0:T(8,128)(2,1)}, u32[]{:S(2)}, u32[]{:S(2)}) collective-permute-start(bf16[2,64,640]{2,1,0:T(8,128)(2,1)} %maximum_select_fusion.2), channel_id=1, source_target_pairs={{0,8},{4,12},{8,0},{12,4},{1,9},{5,13},{9,1},{13,5},{2,10},{6,14},... | collective-permute-start | bytes 491528 | tf_op jit(solution)/shard_map/ppermute | solution.py:360
  29.3 0.0 collective-permute-done.4.block
  29.3 4.3 %last_block.1 = bf16[512,256]{1,0:T(8,128)(2,1)} custom-call(bf16[1,64,4096]{2,1,0:T(8,128)(2,1)S(1)} %collective-permute-done.4.block, bf16[256,256]{1,0:T(8,128)(2,1)S(1)} %get-tuple-element.20.occ, bf16[512,512]{1,0:T(8,128)(2,1)S(1)} %get-tuple-element.21.virt, bf16[128,4096]{1,0:T(8,128)(2,1)S(1)} %get-tuple-element.25.left_first, ...), custom_call_target="tpu_custom_call" | custom-call | tf_op jit(solution)/shard_map/last_block/pallas_call | solution.py:290
  33.7 5.8 %all-to-all-start = ((bf16[16,32,256]{2,1,0:T(8,128)(2,1)}), bf16[16,32,256]{2,1,0:T(8,128)(2,1)S(1)}, u32[]{:S(2)}, u32[]{:S(2)}) async-start(bf16[16,32,256]{2,1,0:T(8,128)(2,1)} %bitcast.7), calls=%async_computation | async-start | bytes 524288 | tf_op jit(solution)/shard_map/all_to_all | solution.py:424
  39.6 0.0 collective-permute-done.3
  39.6 1.1 %maximum_select_fusion.1 = bf16[2,2,64,640]{3,2,1,0:T(8,128)(2,1)S(1)} fusion(bf16[1,2,64,640]{3,2,1,0:T(8,128)(2,1)S(1)} %maximum_select_fusion.3, bf16[1,2,64,640]{3,2,1,0:T(8,128)(2,1)} %bitcast.1, pred[]{:T(512)S(6)} %ne.9), kind=kLoop, calls=%fused_computation.1 | loop fusion | flops 491520 | bytes 655361 | tf_op jit(solution)/shard_map/jit(_where)/select_n | solution.py:366
  40.7 0.5 collective-permute-start.5
  41.1 0.1 eq.39
  41.2 0.1 copy.11
  41.3 0.1 compare_convert_fusion.hits
  41.4 0.5 %placing.1.place = bf16[1024,512]{1,0:T(8,128)(2,1)S(1)} custom-call(bf16[32,16]{1,0:T(8,128)(2,1)S(1)} %compare_convert_fusion.hits), custom_call_target="tpu_custom_call" | custom-call | tf_op jit(solution)/shard_map/placing/pallas_call | solution.py:348
  41.9 0.3 collective-permute-done.5
  42.3 7.2 %all-to-all-done = bf16[16,32,256]{2,1,0:T(8,128)(2,1)S(1)} async-done(((bf16[16,32,256]{2,1,0:T(8,128)(2,1)}), bf16[16,32,256]{2,1,0:T(8,128)(2,1)S(1)}, u32[]{:S(2)}, u32[]{:S(2)}) %all-to-all-start) | async-done | bytes 262176 | tf_op jit(solution)/shard_map/all_to_all | solution.py:424
  49.6 1.4 %finish.1 = (f32[32,512]{1,0:T(8,128)}, f32[32,512]{1,0:T(8,128)}) custom-call(bf16[1024,512]{1,0:T(8,128)(2,1)S(1)} %placing.1.place, bf16[512,256]{1,0:T(8,128)(2,1)S(1)} %bitcast.19, bf16[512,512]{1,0:T(8,128)(2,1)S(1)} %bitcast.18), custom_call_target="tpu_custom_call" | custom-call | tf_op jit(solution)/shard_map/finish/pallas_call | solution.py:327
  (17 shorter events, 0.2 us)
Async XLA Ops:
  2.5 16.7 %collective-permute-start = (bf16[1,64,4352]{2,1,0:T(8,128)(2,1)}, bf16[1,64,4352]{2,1,0:T(8,128)(2,1)S(1)}, u32[]{:S(2)}, u32[]{:S(2)}) collective-permute-start(bf16[1,64,4352]{2,1,0:T(8,128)(2,1)} %get-tuple-element.16), channel_id=1, source_target_pairs={{0,2},{1,3},{2,0},{3,1},{4,6},{5,7},{6,4},{7,5},{8,10},{9,11},{10,... | collective-permute-start | bytes 1671176 | tf_op jit(solution)/shard_map/ppermute | solution.py:360
  5.5 4.5 %copy-start.3 = (s32[4,4]{1,0:T(4,128)S(1)}, s32[4,4]{1,0:T(4,128)}, u32[]{:S(2)}) copy-start(s32[4,4]{1,0:T(4,128)} %ids.1) | copy-start | bytes 196
  5.5 6.5 %copy-start.1 = (bf16[4,64,64]{2,1,0:T(8,128)(2,1)S(1)}, bf16[4,64,64]{2,1,0:T(8,128)(2,1)}, u32[]{:S(2)}) copy-start(bf16[4,64,64]{2,1,0:T(8,128)(2,1)} %occ.1) | copy-start | bytes 98308
  5.5 6.5 %copy-start.2 = (bf16[4,64,64]{2,1,0:T(8,128)(2,1)S(1)}, bf16[4,64,64]{2,1,0:T(8,128)(2,1)}, u32[]{:S(2)}) copy-start(bf16[4,64,64]{2,1,0:T(8,128)(2,1)} %virt.1) | copy-start | bytes 98308
  5.5 6.5 %copy-start.4 = (s32[4]{0:T(128)S(1)}, s32[4]{0:T(128)}, u32[]{:S(2)}) copy-start(s32[4]{0:T(128)} %sizes.1) | copy-start | bytes 52
  9.8 11.1 %copy-start = (bf16[32,512]{1,0:T(8,128)(2,1)S(1)}, bf16[32,512]{1,0:T(8,128)(2,1)}, u32[]{:S(2)}) copy-start(bf16[32,512]{1,0:T(8,128)(2,1)} %coulomb.1) | copy-start | bytes 98308
  9.8 2.2 %collective-permute-start.1 = (bf16[1,64,4096]{2,1,0:T(8,128)(2,1)}, bf16[1,64,4096]{2,1,0:T(8,128)(2,1)S(1)}, u32[]{:S(2)}, u32[]{:S(2)}) collective-permute-start(bf16[1,64,4096]{2,1,0:T(8,128)(2,1)} %get-tuple-element.19), channel_id=1, source_target_pairs={{0,1},{1,0},{2,3},{3,2},{4,5},{5,4},{6,7},{7,6},{8,9},{9,8},{10,11... | collective-permute-start | bytes 1572872 | tf_op jit(solution)/shard_map/ppermute | solution.py:360
  9.9 19.4 %collective-permute-start.4 = (bf16[1,64,4096]{2,1,0:T(8,128)(2,1)}, bf16[1,64,4096]{2,1,0:T(8,128)(2,1)S(1)}, u32[]{:S(2)}, u32[]{:S(2)}) collective-permute-start(bf16[1,64,4096]{2,1,0:T(8,128)(2,1)} %get-tuple-element.24), channel_id=1, source_target_pairs={{0,3},{1,2},{2,1},{3,0},{4,7},{5,6},{6,5},{7,4},{8,11},{9,10},{10,... | collective-permute-start | bytes 1572872 | tf_op jit(solution)/shard_map/ppermute | solution.py:360
  21.0 4.6 %collective-permute-start.2 = (bf16[1,64,640]{2,1,0:T(8,128)(2,1)S(1)}, bf16[1,64,640]{2,1,0:T(8,128)(2,1)S(1)}, u32[]{:S(2)}, u32[]{:S(2)}) collective-permute-start(bf16[1,64,640]{2,1,0:T(8,128)(2,1)S(1)} %rows_along_x.1), channel_id=1, source_target_pairs={{0,4},{4,0},{8,12},{12,8},{1,5},{5,1},{9,13},{13,9},{2,6},{6,2},{1... | collective-permute-start | bytes 245768 | tf_op jit(solution)/shard_map/ppermute | solution.py:360
  26.3 13.3 %collective-permute-start.3 = (bf16[2,64,640]{2,1,0:T(8,128)(2,1)}, bf16[2,64,640]{2,1,0:T(8,128)(2,1)}, u32[]{:S(2)}, u32[]{:S(2)}) collective-permute-start(bf16[2,64,640]{2,1,0:T(8,128)(2,1)} %maximum_select_fusion.2), channel_id=1, source_target_pairs={{0,8},{4,12},{8,0},{12,4},{1,9},{5,13},{9,1},{13,5},{2,10},{6,14},... | collective-permute-start | bytes 491528 | tf_op jit(solution)/shard_map/ppermute | solution.py:360
  33.7 15.9 %all-to-all-start = ((bf16[16,32,256]{2,1,0:T(8,128)(2,1)}), bf16[16,32,256]{2,1,0:T(8,128)(2,1)S(1)}, u32[]{:S(2)}, u32[]{:S(2)}) async-start(bf16[16,32,256]{2,1,0:T(8,128)(2,1)} %bitcast.7), calls=%async_computation | async-start | bytes 524288 | tf_op jit(solution)/shard_map/all_to_all | solution.py:424
  40.7 1.6 %collective-permute-start.5 = (bf16[8,32,512]{2,1,0:T(8,128)(2,1)S(1)}, bf16[8,32,512]{2,1,0:T(8,128)(2,1)S(1)}, u32[]{:S(2)}, u32[]{:S(2)}) collective-permute-start(bf16[8,32,512]{2,1,0:T(8,128)(2,1)S(1)} %bitcast.27), channel_id=1, source_target_pairs={{0,1},{1,0},{2,3},{3,2},{4,5},{5,4},{6,7},{7,6},{8,9},{9,8},{10,11... | collective-permute-start | bytes 786440 | tf_op jit(solution)/shard_map/ppermute | solution.py:360

commit v5 on v4

v5 whole, which is shorter than its diff:
```python
import functools

import jax
import jax.numpy as jnp
from jax import lax
from jax.experimental import pallas as pl
from jax.experimental.pallas import tpu as pltpu
from jax.sharding import PartitionSpec as P

LANES = 128
SUB = 8
TOKEN = (16, 128)
VMEM_LIMIT = 20 * 1024 * 1024
SMALL_LIMIT = 4 * 1024 * 1024
VMEM = pl.BlockSpec(memory_space=pltpu.VMEM)
SMEM = pl.BlockSpec(memory_space=pltpu.SMEM)
ANY = pl.BlockSpec(memory_space=pl.ANY)


def iota(shape, dim):
    return lax.broadcasted_iota(jnp.int32, shape, dim)


def one(hit):
    return jnp.where(hit, 1.0, 0.0).astype(jnp.bfloat16)


def dot(a, b):
    return jnp.dot(a, b, preferred_element_type=jnp.float32)


def dot_nt(a, b):
    return lax.dot_general(a, b, (((1,), (1,)), ((), ())), preferred_element_type=jnp.float32)


def half(shape):
    return jax.ShapeDtypeStruct(shape, jnp.bfloat16)


def far(shape):
    return pltpu.HBM(shape, jnp.bfloat16)


def near(shape):
    return pltpu.VMEM(shape, jnp.bfloat16)


def in_near(array):
    return pltpu.with_memory_space_constraint(array, pltpu.VMEM)


def in_far(array):
    return pltpu.with_memory_space_constraint(array, pltpu.HBM)


def started(sems, pairs):
    copies = [pltpu.make_async_copy(a, b, sems.at[i]) for i, (a, b) in enumerate(pairs)]
    for copy in copies:
        copy.start()
    return copies


def finished(copies):
    for copy in copies:
        copy.wait()


def limit(size):
    return pltpu.CompilerParams(vmem_limit_bytes=size)


def pick_kernel(step, riding, *refs):
    three_c = refs[0]
    out, token, sems = refs[-3:]
    token[...] = jnp.zeros_like(token)
    _, count, _ = out.shape
    square = three_c.shape[2]
    pairs = [(three_c.at[lax.axis_index("ri") ^ step], out.at[0, :, pl.ds(0, square)])]
    if riding:
        coulomb = refs[1]
        rows, total = coulomb.shape
        fold = count // rows
        wide = total // fold
        for i in range(fold):
            there = out.at[0, pl.ds(i * rows, rows), pl.ds(square, wide)]
            pairs.append((coulomb.at[:, pl.ds(i * wide, wide)], there))
    finished(started(sems, pairs))


def pick(three_c, step, coulomb=None, hold=None):
    _, count, square = three_c.shape
    riding = coulomb is not None
    operands = [in_far(three_c)] + [in_far(a) for a in (coulomb,) if riding] + [a for a in (hold,) if a is not None]
    extra = coulomb.size // count if riding else 0
    rides = count // coulomb.shape[0] if riding else 0
    return pl.pallas_call(
        functools.partial(pick_kernel, step, riding),
        in_specs=[ANY] * (1 + riding) + [VMEM] * (hold is not None),
        out_specs=[VMEM, VMEM],
        out_shape=[near((1, count, square + extra)), half(TOKEN)],
        scratch_shapes=[pltpu.SemaphoreType.DMA((1 + rides,))],
        compiler_params=limit(SMALL_LIMIT),
        name="pick",
    )(*operands)


def along_x_kernel(block, coulomb, ids, hold, out):
    rows, total = coulomb.shape
    upper = (lax.axis_index("ri") & 2) != 0
    own = coulomb[...]
    fold = block.shape[1] // rows
    tail = block[0, :, block.shape[2] - total // fold :]
    other = jnp.concatenate([tail[i * rows : (i + 1) * rows] for i in range(fold)], 1)
    out[0, :rows, :total] = jnp.where(upper, other, own)
    out[0, rows:, :total] = jnp.where(upper, own, other)
    out[0, :, total:] = ids[...]


def rows_along_x(block, coulomb, ids, hold):
    rows, total = coulomb.shape
    return pl.pallas_call(
        along_x_kernel,
        in_specs=[VMEM] * 4,
        out_specs=VMEM,
        out_shape=half((1, 2 * rows, total + LANES)),
        compiler_params=limit(SMALL_LIMIT),
        name="rows_along_x",
    )(block, coulomb, ids, hold)


def prepared(size, occ, virt, occ_out, virt_out, back_out=None):
    width = occ.shape[0]
    full = occ_out.shape[0]
    spread = one(iota((full, width), 0) % width == iota((full, width), 1))
    tiled = dot_nt(dot(spread, occ).astype(jnp.bfloat16), spread)
    same = iota((full, full), 0) // width == iota((full, full), 1) // width
    occ_out[...] = jnp.where(same, tiled, 0.0).astype(jnp.bfloat16)

    keep = (iota((width, width), 0) < size) & (iota((width, width), 1) < size)
    kept = jnp.where(keep, virt.astype(jnp.float32), 0.0).astype(jnp.bfloat16)
    side = virt_out.shape[0] // 2
    same = iota((side, 2 * side), 0) % SUB == iota((side, 2 * side), 1) % SUB
    for parity in range(2):
        wanted = 2 * (iota((side, width), 0) // SUB) + parity
        picked_rows = one(wanted == iota((side, width), 1))
        column = iota((2 * side, width), 0)
        wanted = 2 * (column % side // SUB) + (column // side + parity) % 2
        picked_columns = one(wanted == iota((2 * side, width), 1))
        for target, product in ((virt_out, dot), (back_out, dot_nt)):
            if target is not None:
                part = dot_nt(product(picked_rows, kept).astype(jnp.bfloat16), picked_columns)
                target[parity * side : (parity + 1) * side, :] = jnp.where(same, part, 0.0).astype(jnp.bfloat16)


def times_occ(block, occ, left, product=dot):
    rows, square = left.shape
    full = occ.shape[0]
    wide = [block[:, c * full : (c + 1) * full] for c in range(square // full)]
    out = product(jnp.concatenate(wide, 0), occ[...]).astype(jnp.bfloat16)
    for c in range(square // full):
        left[:, c * full : (c + 1) * full] = out[c * rows : (c + 1) * rows]


def times_virt(virt, block, right):
    rows, square = right.shape
    chunks = square // LANES
    side = chunks * SUB
    low = iota((side, 2 * LANES), 1) % LANES < LANES // 2
    for row in range(0, rows, 2 * SUB):
        tile = block[row : row + 2 * SUB, :square].astype(jnp.float32)
        plain, turned = [], []
        for i in range(2):
            part = tile[i * SUB : (i + 1) * SUB]
            stacked = jnp.concatenate([part[:, c * LANES : (c + 1) * LANES] for c in range(chunks)], 0)
            plain.append(stacked)
            turned.append(pltpu.roll(stacked, LANES // 2, 1))
        operand = jnp.concatenate([jnp.concatenate(plain, 1), jnp.concatenate(turned, 1)], 0)
        out = dot(virt[...], operand.astype(jnp.bfloat16))
        out = jnp.where(low, out[:side], out[side:])
        for c in range(chunks):
            piece = out[c * SUB : (c + 1) * SUB]
            piece = jnp.concatenate([piece[:, :LANES], piece[:, LANES:]], 0)
            right[row : row + 2 * SUB, c * LANES : (c + 1) * LANES] = piece.astype(jnp.bfloat16)


def long_dot(lefts, rights, pad=0):
    square = lefts[0].shape[1]
    step = 1024
    total = None
    for c in range(0, square, step):
        a = jnp.concatenate([ref[:, c : c + step] for ref in lefts], 0)
        b = [ref[:, c : c + step] for ref in rights]
        zeros = [jnp.zeros((abs(pad), step), jnp.bfloat16)] if pad else []
        b = jnp.concatenate(b + zeros if pad > 0 else zeros + b, 0)
        part = dot_nt(a, b)
        total = part if total is None else total + part
    return total


def corner_kernel(step, sizes, three_c, occ, virt, hold, out, token, occ_wide, virt_wide, left, right, sem):
    token[...] = jnp.zeros_like(token)
    there = lax.axis_index("ri") ^ step
    rows, square = left.shape
    block = out.at[0, :, pl.ds(0, square)]
    copy = pltpu.make_async_copy(three_c.at[there], block, sem)
    copy.start()
    prepared(sizes[there], occ[there], virt[there], occ_wide, virt_wide)
    copy.wait()
    times_occ(block, occ_wide, left)
    times_virt(virt_wide, block, right)
    out[0, :, square:] = long_dot([left], [right], -rows).astype(jnp.bfloat16)


def corner(three_c, step, occ, virt, sizes, hold):
    _, rows, square = three_c.shape
    width = occ.shape[-1]
    shapes = [(4 * width, 4 * width), (SUB * width, SUB * width), (rows, square), (rows, square)]
    return pl.pallas_call(
        functools.partial(corner_kernel, step),
        in_specs=[SMEM, ANY, VMEM, VMEM, VMEM],
        out_specs=[VMEM, VMEM],
        out_shape=[near((1, rows, square + 2 * rows)), half(TOKEN)],
        scratch_shapes=[pltpu.VMEM(shape, jnp.bfloat16) for shape in shapes] + [pltpu.SemaphoreType.DMA],
        compiler_params=limit(VMEM_LIMIT),
        name="corner",
    )(sizes, in_far(three_c), occ, virt, hold)


def first_kernel(sizes, ids, three_c, other, occ, virt, hold, *refs):
    occ_out, virt_out, back_out, place, left, right, left_back, right_back, token, own, sem = refs
    token[...] = jnp.zeros_like(token)
    here = lax.axis_index("ri")
    copy = pltpu.make_async_copy(three_c.at[here], own, sem)
    copy.start()
    prepared(sizes[here], occ[here], virt[here], occ_out, virt_out, back_out)
    rows, square = own.shape
    column = iota(place.shape, 1)
    wanted = jnp.zeros(place.shape, jnp.int32)
    for j in range(ids.shape[1]):
        wanted = jnp.where(column // rows == j, ids[here, here ^ j], wanted)
    row = iota(place.shape, 0)
    place[...] = one((row // rows == wanted) & (row % rows == column % rows))
    copy.wait()
    for i, block in enumerate((own, other.at[0])):
        at = slice(i * rows, (i + 1) * rows)
        times_occ(block, occ_out, left.at[at])
        times_virt(virt_out, block, right.at[at])
        times_virt(back_out, left.at[at], left_back.at[at])
        times_occ(right.at[at], occ_out, right_back.at[at], dot_nt)


def first_blocks(three_c, other, occ, virt, sizes, ids, hold):
    _, rows, square = three_c.shape
    width = occ.shape[-1]
    kcount = ids.shape[1]
    shapes = [(4 * width, 4 * width)] + [(SUB * width, SUB * width)] * 2
    shapes += [(2 * kcount * rows, kcount * rows)] + [(2 * rows, square)] * 4
    return pl.pallas_call(
        first_kernel,
        in_specs=[SMEM, SMEM, ANY] + [VMEM] * 4,
        out_specs=[VMEM] * 9,
        out_shape=[near(shape) for shape in shapes] + [half(TOKEN)],
        scratch_shapes=[pltpu.VMEM((rows, square), jnp.bfloat16), pltpu.SemaphoreType.DMA],
        compiler_params=limit(VMEM_LIMIT),
        name="first_blocks",
    )(sizes, ids, in_far(three_c), other, occ, virt, hold)


def next_kernel(block, occ, virt, virt_back, hold, left, right, left_back, right_back, token):
    token[...] = jnp.zeros_like(token)
    times_occ(block.at[0], occ, left)
    times_virt(virt, block.at[0], right)
    times_virt(virt_back, left, left_back)
    times_occ(right, occ, right_back, dot_nt)


def next_block(block, occ, virt, virt_back, hold, square):
    shape = (block.shape[1], square)
    return pl.pallas_call(
        next_kernel,
        in_specs=[VMEM] * 5,
        out_specs=[VMEM] * 5,
        out_shape=[near(shape)] * 4 + [half(TOKEN)],
        compiler_params=limit(VMEM_LIMIT),
        name="next_block",
    )(block, *map(in_near, (occ, virt, virt_back)), hold)


def inner_kernel(count, *refs):
    out, token = refs[2 * count :]
    token[...] = jnp.zeros_like(token)
    out[...] = long_dot(refs[:count], refs[count : 2 * count], out.shape[1] - out.shape[0]).astype(jnp.bfloat16)


def inner_chi(lefts, rights):
    rows = sum(left.shape[0] for left in lefts)
    wide = rows + lefts[-1].shape[0]
    return pl.pallas_call(
        functools.partial(inner_kernel, len(lefts)),
        in_specs=[VMEM] * (2 * len(lefts)),
        out_specs=[VMEM, VMEM],
        out_shape=[near((rows, wide)), half(TOKEN)],
        compiler_params=limit(VMEM_LIMIT),
        name="inner_chi",
    )(*map(in_near, lefts + rights))


def last_kernel(count, block, place, inner, *refs):
    right_backs, left_backs, out = refs[:count], refs[count : 2 * count], refs[2 * count]
    square = left_backs[0].shape[1]
    rows = block.shape[1]
    came = block.at[0, :, pl.ds(0, square)]
    aside = jnp.zeros((rows, inner.shape[1] - 2 * rows), jnp.float32)
    bottom = long_dot([came], right_backs, rows)
    bottom = bottom + jnp.concatenate([aside, block[0, :, square:].astype(jnp.float32)], 1)
    columns = long_dot(left_backs, [came], -rows)
    head, tail = inner[:, : -2 * rows], inner[:, -2 * rows :]
    top = jnp.concatenate([head, tail + columns.astype(jnp.bfloat16)], 1)
    total = jnp.concatenate([top, bottom.astype(jnp.bfloat16)], 0)
    out[...] = dot(place[...], total).astype(jnp.bfloat16)


def last_block(block, place, inner, right_backs, left_backs):
    return pl.pallas_call(
        functools.partial(last_kernel, len(left_backs)),
        in_specs=[VMEM] * (3 + 2 * len(left_backs)),
        out_specs=VMEM,
        out_shape=half(place.shape),
        compiler_params=limit(VMEM_LIMIT),
        name="last_block",
    )(block, *map(in_near, (place, inner, *right_backs, *left_backs)))


def finish_kernel(kcount, place, got, metric, chi, screen):
    rows, total = chi.shape
    blocks = 2 * kcount
    width = total // blocks
    placed = dot(place[...], got[...])
    low = iota((rows, LANES), 1) < width

    def block(t):
        straight, turned = None, None
        for j in range(kcount):
            at = (j * blocks + t) * rows
            piece = placed[at : at + rows, j // 2 * LANES : (j // 2 + 1) * LANES]
            if j % 2 == t % 2:
                straight = piece if straight is None else straight + piece
            else:
                turned = piece if turned is None else turned + piece
        return straight + pltpu.roll(turned, width, 1)

    for t in range(0, blocks, 2):
        chi[:, t * width : (t + 2) * width] = jnp.where(low, block(t), block(t + 1))
    screen[...] = dot(chi[...].astype(jnp.bfloat16), metric[...])


def finish(place, got, metric, kcount):
    total = metric.shape[0]
    rows = place.shape[0] // (2 * kcount * kcount)
    return pl.pallas_call(
        functools.partial(finish_kernel, kcount),
        in_specs=[VMEM] * 3,
        out_specs=[VMEM, VMEM],
        out_shape=[jax.ShapeDtypeStruct((rows, total), jnp.float32)] * 2,
        compiler_params=limit(VMEM_LIMIT),
        name="finish",
    )(place, got, metric)


def placing_kernel(hits, out):
    high, wide = hits.shape
    rows = out.shape[0] // high
    down = one(iota((high * rows, high), 0) // rows == iota((high * rows, high), 1))
    across = one(iota((wide * rows, wide), 0) // rows == iota((wide * rows, wide), 1))
    spread = dot_nt(dot(down, hits[...]).astype(jnp.bfloat16), across)
    same = iota(out.shape, 0) % rows == iota(out.shape, 1) % rows
    out[...] = jnp.where(same, spread, 0.0).astype(jnp.bfloat16)


def placing(hits, rows):
    return pl.pallas_call(
        placing_kernel,
        in_specs=[VMEM],
        out_specs=VMEM,
        out_shape=half((hits.shape[0] * rows, hits.shape[1] * rows)),
        compiler_params=limit(VMEM_LIMIT),
        name="placing",
    )(hits)


def swap(array, axes, step):
    count = lax.axis_size(axes)
    return lax.ppermute(array, axes, [(i, i ^ step) for i in range(count)])


def join_kernel(axis, step, own, other, *refs):
    out = refs[-1]
    upper = (lax.axis_index(axis) & step) != 0
    out[0] = jnp.where(upper, other[...], own[...])
    out[1] = jnp.where(upper, own[...], other[...])


def gathered(array, axis, step, hold=None):
    other = swap(array, axis, step)
    return pl.pallas_call(
        functools.partial(join_kernel, axis, step),
        in_specs=[VMEM] * (2 + (hold is not None)),
        out_specs=VMEM,
        out_shape=half((2,) + array.shape),
        compiler_params=limit(SMALL_LIMIT),
        name="join",
    )(array, other, *([] if hold is None else [hold]))


def gather_metric(out, total, own_rows, pairs, kcount, hold):
    ri_count, pair_count = lax.axis_size("ri"), lax.axis_size("pair")
    chips = ri_count // 4
    _, rows, wide = out.shape
    step = 4
    while step < ri_count:
        out = gathered(out, "ri", step).reshape(-1, rows, wide)
        step *= 2
    step = 1
    while step < pair_count:
        out = gathered(out, "pair", step, hold if step == 1 else None).reshape(-1, rows, wide)
        step *= 2
    all_ids = out.reshape(pair_count, chips, rows, wide)[:, 0, :pairs, total : total + kcount]
    out = out[:, :, :total].reshape(-1, rows // 2, total)[:, :own_rows]
    out = gathered(out, "ri", 1).swapaxes(0, 1).reshape(-1, total)
    return out, all_ids.reshape(-1, kcount)


def shards(three_c, green_occ, green_virt, pair_size, ri_ids, coulomb):
    everyone = ("pair", "ri")
    ri_count = lax.axis_size("ri")
    devices = lax.axis_size(everyone)
    kcount = ri_ids.shape[1]
    blocks = 2 * kcount
    pairs, _, rows, square = three_c.shape
    out_rows, total = coulomb.shape
    three_c = three_c.reshape(pairs, rows, square)
    slots = jnp.arange(kcount, dtype=jnp.int32)
    block_ids = jnp.arange(blocks, dtype=jnp.int32)
    riding_rows = max(16, out_rows)
    riding = jnp.pad(coulomb, ((0, riding_rows - out_rows), (0, 0)))

    parts, token = {}, None
    last = ri_count - 1
    for step in [2, 1] + list(range(3, last)):
        part, token = pick(three_c, step, coulomb=riding if step == 2 else None, hold=token)
        parts[step] = swap(part, "ri", step)
    part, token = corner(three_c, last, green_occ, green_virt, pair_size, token)
    parts[last] = swap(part, "ri", last)
    occ, virt, virt_back, place, left, right, left_back, right_back, token = first_blocks(
        three_c, parts[1], green_occ, green_virt, pair_size, ri_ids, token
    )
    lefts, rights, left_backs, right_backs = [left], [right], [left_back], [right_back]
    first_token = token
    for step in range(2, last):
        left, right, left_back, right_back, token = next_block(parts[step], occ, virt, virt_back, token, square)
        lefts.append(left)
        rights.append(right)
        left_backs.append(left_back)
        right_backs.append(right_back)
    inner, token = inner_chi(lefts, rights)
    pieces = last_block(parts[last], place, inner, right_backs, left_backs)

    slot = jnp.arange(pairs, dtype=jnp.int32)[:, None] ^ slots[None, :]
    relative = jnp.sum(jnp.where(slot[:, :, None] == slots, ri_ids[:, None, :], 0), 2)
    ids = jnp.pad(relative.astype(jnp.bfloat16), ((0, 2 * riding_rows - pairs), (0, LANES - kcount)))
    metric = rows_along_x(parts[2], riding, ids, first_token)
    metric, all_ids = gather_metric(metric, total, out_rows, pairs, kcount, token)
    hits = all_ids.T[:, None, :] == block_ids.astype(jnp.bfloat16)[None, :, None]
    placed = placing(hits.astype(jnp.bfloat16).reshape(kcount * blocks, devices), out_rows)

    got = lax.all_to_all(pieces.reshape(devices, out_rows, kcount * rows), everyone, 0, 0, tiled=True)
    return tuple(finish(placed, got.reshape(devices * out_rows, kcount * rows), metric, kcount))


def solution(mesh):
    placed = (
        P(("snap", "pair"), "ri", None, None),
        P(("snap", "pair"), None, None),
        P(("snap", "pair"), None, None),
        P(("snap", "pair")),
        P(("snap", "pair"), None),
        P(("snap", "pair", "ri"), None),
    )
    return jax.shard_map(
        shards,
        mesh=mesh,
        in_specs=placed,
        out_specs=(P(("snap", "pair", "ri"), None), P(("snap", "pair", "ri"), None)),
        check_vma=False,
    )
```

time: 51.3 us -> 48.5 us (0.945)
  waiting for transfers between devices: 15.7 us -> 13.8 us
  other arithmetic: 2.14 us -> 0.31 us
  starting transfers between devices: 14.8 us -> 15.9 us
    ppermute x6, waiting for transfers between devices: 8.45 us -> 5.62 us  [swap(): return lax.ppermute(array, axes, [(i, i ^ step) for i in range(count)])]
    select_n x4 -> x0, other arithmetic: 1.83 us -> none  [gathered(): jnp.where(upper, jnp.stack([other, array]), jnp.stack([array, other]))]
    all_to_all x1, waiting for transfers between devices: 7.23 us -> 8.23 us  [shards(): lax.all_to_all(pieces.reshape(devices, out_rows, kcount * rows), everyone...]
    all_to_all x1, starting transfers between devices: 5.85 us -> 6.61 us  [shards(): lax.all_to_all(pieces.reshape(devices, out_rows, kcount * rows), everyone...]
    pallas_call x6 -> x10, Pallas kernels: 15.4 us -> 15.1 us  [the longest x1 4.93 us: first_blocks(): pl.pallas_call(first_kernel, in_specs=[SMEM, SMEM, ANY] + [VMEM] * 4, out...]
  transfers between devices with their start and end apart: 7 -> 7, of which waited for: 5 -> 4; matrix products, arithmetic and copies ran while one was open for 5% -> 1% of each run, Pallas kernels for 28% -> 30%
where the time goes in v5:
time: 48.5 us; the launch traced here: 48.2 us
  Pallas kernels  17.1 us (35%)
  starting transfers between devices  15.9 us (33%)
  waiting for transfers between devices  13.8 us (28%)
  between operations  0.83 us (2%)
    ppermute x6, starting transfers between devices, swap(): return lax.ppermute(array, axes, [(i, i ^ step) for i in range(count)])  9.27 us
    all_to_all x1, waiting for transfers between devices, shards(): lax.all_to_all(pieces.reshape(devices, out_rows, kcount * rows), everyone...  8.23 us
    all_to_all x1, starting transfers between devices, shards(): lax.all_to_all(pieces.reshape(devices, out_rows, kcount * rows), everyone...  6.61 us
    ppermute x6, waiting for transfers between devices, swap(): return lax.ppermute(array, axes, [(i, i ^ step) for i in range(count)])  5.62 us
    pallas_call x1, Pallas kernels, first_blocks(): pl.pallas_call(first_kernel, in_specs=[SMEM, SMEM, ANY] + [VMEM] * 4, out...  4.93 us
    pallas_call x1, Pallas kernels, corner(): pl.pallas_call(functools.partial(corner_kernel, step), in_specs=[SMEM, AN...  3.32 us
    pallas_call x2, Pallas kernels, pick(): pl.pallas_call(functools.partial(pick_kernel, step, riding), in_specs=[AN...  2.18 us
    pallas_call x1, Pallas kernels, next_block(): pl.pallas_call(next_kernel, in_specs=[VMEM] * 5, out_specs=[VMEM] * 5, ou...  2.09 us
  transfers between devices with their start and end apart: 7, of which 4 were waited for; matrix products, arithmetic and copies ran while one was open for 1% of the time, Pallas kernels for 30%

profile of v5, /device:TPU:0, one launch (start us, length us, event | category | flops | bytes accessed | tf_op | source)
XLA Modules:
  0.0 48.2 jit_solution(9475602889363530343)
XLA Ops:
  0.6 0.0 copy-start
  0.6 0.0 copy-start.1
  0.7 0.0 copy-start.4
  0.7 1.1 %pick.2 = (bf16[1,64,4352]{2,1,0:T(8,128)(2,1)S(1)}, bf16[16,128]{1,0:T(8,128)(2,1)S(1)}) custom-call(bf16[4,64,4096]{2,1,0:T(8,128)(2,1)} %bitcast.22, bf16[32,512]{1,0:T(8,128)(2,1)} %coulomb.1), custom_call_target="tpu_custom_call" | custom-call | tf_op jit(solution)/shard_map/pick/pallas_call | solution.py:96
  1.8 3.0 %collective-permute-start = (bf16[1,64,4352]{2,1,0:T(8,128)(2,1)S(1)}, bf16[1,64,4352]{2,1,0:T(8,128)(2,1)S(1)}, u32[]{:S(2)}, u32[]{:S(2)}) collective-permute-start(bf16[1,64,4352]{2,1,0:T(8,128)(2,1)S(1)} %get-tuple-element.23), channel_id=1, source_target_pairs={{0,2},{1,3},{2,0},{3,1},{4,6},{5,7},{6,4},{7,5},{8,10},{9,11},{10,... | collective-permute-start | bytes 1671176 | tf_op jit(solution)/shard_map/ppermute | solution.py:393
  4.8 1.1 %pick.3 = (bf16[1,64,4096]{2,1,0:T(8,128)(2,1)S(1)}, bf16[16,128]{1,0:T(8,128)(2,1)S(1)}) custom-call(bf16[4,64,4096]{2,1,0:T(8,128)(2,1)} %bitcast.23, bf16[16,128]{1,0:T(8,128)(2,1)S(1)} %get-tuple-element.24.refs_1_), custom_call_target="tpu_custom_call" | custom-call | tf_op jit(solution)/shard_map/pick/pallas_call | solution.py:96
  5.9 0.1 collective-permute-start.1
  5.9 0.0 copy-done
  6.0 0.0 copy-start.2
  6.0 3.3 %corner.1 = (bf16[1,64,4224]{2,1,0:T(8,128)(2,1)S(1)}, bf16[16,128]{1,0:T(8,128)(2,1)S(1)}) custom-call(s32[4]{0:T(128)S(1)} %copy-done.4, bf16[4,64,4096]{2,1,0:T(8,128)(2,1)} %bitcast.24, bf16[4,64,64]{2,1,0:T(8,128)(2,1)S(1)} %copy-done, bf16[4,64,64]{2,1,0:T(8,128)(2,1)S(1)} %copy-done.1, bf16[16,128]{1,0:T(8,128)(2,1)S(1)} %get-tuple-element.26.hold), custom_call_target="tpu_custom_call" | custom-call | tf_op jit(solution)/shard_map/corner/pallas_call | solution.py:218
  9.3 0.2 collective-permute-start.4
  9.5 0.2 select_reduce_fusion
  9.7 0.0 collective-permute-done.1.other
  9.7 4.9 %first_blocks.1 = (bf16[256,256]{1,0:T(8,128)(2,1)S(1)}, bf16[512,512]{1,0:T(8,128)(2,1)S(1)}, bf16[512,512]{1,0:T(8,128)(2,1)S(1)}, bf16[512,256]{1,0:T(8,128)(...) custom-call(s32[4]{0:T(128)S(1)} %copy-done.4, ...), custom_call_target="tpu_custom_call" | custom-call | tf_op jit(solution)/shard_map/first_blocks/pallas_call | solution.py:258
  14.7 3.6 %collective-permute-done.block = bf16[1,64,4352]{2,1,0:T(8,128)(2,1)S(1)} collective-permute-done((bf16[1,64,4352]{2,1,0:T(8,128)(2,1)S(1)}, bf16[1,64,4352]{2,1,0:T(8,128)(2,1)S(1)}, u32[]{:S(2)}, u32[]{:S(2)}) %collective-permute-start) | collective-permute-done | bytes 557088 | tf_op jit(solution)/shard_map/ppermute | solution.py:393
  18.3 2.2 %collective-permute-start.2 = (bf16[1,64,640]{2,1,0:T(8,128)(2,1)S(1)}, bf16[1,64,640]{2,1,0:T(8,128)(2,1)S(1)}, u32[]{:S(2)}, u32[]{:S(2)}) collective-permute-start(bf16[1,64,640]{2,1,0:T(8,128)(2,1)S(1)} %rows_along_x.1.own), channel_id=1, source_target_pairs={{0,4},{4,0},{8,12},{12,8},{1,5},{5,1},{9,13},{13,9},{2,6},{6,2},{1... | collective-permute-start | bytes 245768 | tf_op jit(solution)/shard_map/ppermute | solution.py:393
  20.5 2.1 %next_block.1 = (bf16[64,4096]{1,0:T(8,128)(2,1)S(1)}, bf16[64,4096]{1,0:T(8,128)(2,1)S(1)}, bf16[64,4096]{1,0:T(8,128)(2,1)S(1)}, bf16[64,4096]{1,0:T(8,128)(2,1)S(1)}, bf16[16,128]{1,0:T(8,128)(2,1)}) custom-call(bf16[1,64,4352]{2,1,0:T(8,128)(2,1)S(1)} %collective-permute-done.block, bf16[256,256]{1,0:T(8,128)(2,1)S(1)} %get-tuple-element.30.occ, ...), custom_call_target="tpu_custom_call" | custom-call | tf_op jit(solution)/shard_map/next_block/pallas_call | solution.py:279
  22.6 0.6 %inner_chi.1 = (bf16[192,256]{1,0:T(8,128)(2,1)S(1)}, bf16[16,128]{1,0:T(8,128)(2,1)S(1)}) custom-call(bf16[128,4096]{1,0:T(8,128)(2,1)S(1)} %get-tuple-element.29.refs_0_, bf16[64,4096]{1,0:T(8,128)(2,1)S(1)} %get-tuple-element.33.refs_1_, bf16[128,4096]{1,0:T(8,128)(2,1)S(1)} %get-tuple-element.34.refs_2_, bf16[64,4096]{1,0:T(8,128)(2,1)S(1)} %get-tuple-element.35.refs_3_), custom_call_target="tpu_custom_call" | custom-call | tf_op jit(solution)/shard_map/inner_chi/pallas_call | solution.py:298
  23.2 0.0 collective-permute-done.2.other
  23.2 3.4 %collective-permute-start.3 = (bf16[2,64,640]{2,1,0:T(8,128)(2,1)S(1)}, bf16[2,64,640]{2,1,0:T(8,128)(2,1)S(1)}, u32[]{:S(2)}, u32[]{:S(2)}) collective-permute-start(bf16[2,64,640]{2,1,0:T(8,128)(2,1)S(1)} %bitcast.20), channel_id=1, source_target_pairs={{0,8},{4,12},{8,0},{12,4},{1,9},{5,13},{9,1},{13,5},{2,10},{6,14},... | collective-permute-start | bytes 491528 | tf_op jit(solution)/shard_map/ppermute | solution.py:393
  26.6 1.7 %collective-permute-done.4.block = bf16[1,64,4224]{2,1,0:T(8,128)(2,1)S(1)} collective-permute-done((bf16[1,64,4224]{2,1,0:T(8,128)(2,1)S(1)}, bf16[1,64,4224]{2,1,0:T(8,128)(2,1)S(1)}, u32[]{:S(2)}, u32[]{:S(2)}) %collective-permute-start.4) | collective-permute-done | bytes 540704 | tf_op jit(solution)/shard_map/ppermute | solution.py:393
  28.3 1.9 %last_block.1 = bf16[512,256]{1,0:T(8,128)(2,1)} custom-call(bf16[1,64,4224]{2,1,0:T(8,128)(2,1)S(1)} %collective-permute-done.4.block, bf16[512,256]{1,0:T(8,128)(2,1)S(1)} %get-tuple-element.38.place, bf16[192,256]{1,0:T(8,128)(2,1)S(1)} %get-tuple-element.39.inner, bf16[128,4096]{1,0:T(8,128)(2,1)S(1)} %get-tuple-element.40.refs_0_, ...), custom_call_target="tpu_custom_call" | custom-call | tf_op jit(solution)/shard_map/last_block/pallas_call | solution.py:324
  30.2 6.6 %all-to-all-start = ((bf16[16,32,256]{2,1,0:T(8,128)(2,1)}), bf16[16,32,256]{2,1,0:T(8,128)(2,1)S(1)}, u32[]{:S(2)}, u32[]{:S(2)}) async-start(bf16[16,32,256]{2,1,0:T(8,128)(2,1)} %bitcast.5), calls=%async_computation | async-start | bytes 524288 | tf_op jit(solution)/shard_map/all_to_all | solution.py:476
  36.8 0.0 collective-permute-done.3.other
  36.9 0.5 collective-permute-start.5
  37.4 0.1 eq.39
  37.5 0.1 copy.13
  37.5 0.1 compare_convert_fusion.hits
  37.6 0.5 %placing.1.place = bf16[1024,512]{1,0:T(8,128)(2,1)S(1)} custom-call(bf16[32,16]{1,0:T(8,128)(2,1)S(1)} %compare_convert_fusion.hits), custom_call_target="tpu_custom_call" | custom-call | tf_op jit(solution)/shard_map/placing/pallas_call | solution.py:381
  38.2 0.3 collective-permute-done.5.other
  38.6 8.2 %all-to-all-done = bf16[16,32,256]{2,1,0:T(8,128)(2,1)S(1)} async-done(((bf16[16,32,256]{2,1,0:T(8,128)(2,1)}), bf16[16,32,256]{2,1,0:T(8,128)(2,1)S(1)}, u32[]{:S(2)}, u32[]{:S(2)}) %all-to-all-start) | async-done | bytes 262176 | tf_op jit(solution)/shard_map/all_to_all | solution.py:476
  46.8 1.4 %finish.1 = (f32[32,512]{1,0:T(8,128)}, f32[32,512]{1,0:T(8,128)}) custom-call(bf16[1024,512]{1,0:T(8,128)(2,1)S(1)} %placing.1.place, bf16[512,256]{1,0:T(8,128)(2,1)S(1)} %bitcast.17, bf16[512,512]{1,0:T(8,128)(2,1)S(1)} %bitcast.13), custom_call_target="tpu_custom_call" | custom-call | tf_op jit(solution)/shard_map/finish/pallas_call | solution.py:360
  (17 shorter events, 0.2 us)
Async XLA Ops:
  0.6 5.3 %copy-start = (bf16[4,64,64]{2,1,0:T(8,128)(2,1)S(1)}, bf16[4,64,64]{2,1,0:T(8,128)(2,1)}, u32[]{:S(2)}) copy-start(bf16[4,64,64]{2,1,0:T(8,128)(2,1)} %occ.3) | copy-start | bytes 98308
  0.6 5.3 %copy-start.1 = (bf16[4,64,64]{2,1,0:T(8,128)(2,1)S(1)}, bf16[4,64,64]{2,1,0:T(8,128)(2,1)}, u32[]{:S(2)}) copy-start(bf16[4,64,64]{2,1,0:T(8,128)(2,1)} %virt.3) | copy-start | bytes 98308
  0.7 5.3 %copy-start.4 = (s32[4]{0:T(128)S(1)}, s32[4]{0:T(128)}, u32[]{:S(2)}) copy-start(s32[4]{0:T(128)} %sizes.3) | copy-start | bytes 52
  1.8 16.5 %collective-permute-start = (bf16[1,64,4352]{2,1,0:T(8,128)(2,1)S(1)}, bf16[1,64,4352]{2,1,0:T(8,128)(2,1)S(1)}, u32[]{:S(2)}, u32[]{:S(2)}) collective-permute-start(bf16[1,64,4352]{2,1,0:T(8,128)(2,1)S(1)} %get-tuple-element.23), channel_id=1, source_target_pairs={{0,2},{1,3},{2,0},{3,1},{4,6},{5,7},{6,4},{7,5},{8,10},{9,11},{10,... | collective-permute-start | bytes 1671176 | tf_op jit(solution)/shard_map/ppermute | solution.py:393
  4.8 4.7 %copy-start.3 = (s32[4,4]{1,0:T(4,128)S(1)}, s32[4,4]{1,0:T(4,128)}, u32[]{:S(2)}) copy-start(s32[4,4]{1,0:T(4,128)} %ids.1) | copy-start | bytes 196
  5.9 3.9 %collective-permute-start.1 = (bf16[1,64,4096]{2,1,0:T(8,128)(2,1)S(1)}, bf16[1,64,4096]{2,1,0:T(8,128)(2,1)S(1)}, u32[]{:S(2)}, u32[]{:S(2)}) collective-permute-start(bf16[1,64,4096]{2,1,0:T(8,128)(2,1)S(1)} %get-tuple-element.25), channel_id=1, source_target_pairs={{0,1},{1,0},{2,3},{3,2},{4,5},{5,4},{6,7},{7,6},{8,9},{9,8},{10,11... | collective-permute-start | bytes 1572872 | tf_op jit(solution)/shard_map/ppermute | solution.py:393
  6.0 12.3 %copy-start.2 = (bf16[32,512]{1,0:T(8,128)(2,1)S(1)}, bf16[32,512]{1,0:T(8,128)(2,1)}, u32[]{:S(2)}) copy-start(bf16[32,512]{1,0:T(8,128)(2,1)} %coulomb.1) | copy-start | bytes 98308
  9.3 18.9 %collective-permute-start.4 = (bf16[1,64,4224]{2,1,0:T(8,128)(2,1)S(1)}, bf16[1,64,4224]{2,1,0:T(8,128)(2,1)S(1)}, u32[]{:S(2)}, u32[]{:S(2)}) collective-permute-start(bf16[1,64,4224]{2,1,0:T(8,128)(2,1)S(1)} %get-tuple-element.37), channel_id=1, source_target_pairs={{0,3},{1,2},{2,1},{3,0},{4,7},{5,6},{6,5},{7,4},{8,11},{9,10},{10,... | collective-permute-start | bytes 1622024 | tf_op jit(solution)/shard_map/ppermute | solution.py:393
  18.3 4.9 %collective-permute-start.2 = (bf16[1,64,640]{2,1,0:T(8,128)(2,1)S(1)}, bf16[1,64,640]{2,1,0:T(8,128)(2,1)S(1)}, u32[]{:S(2)}, u32[]{:S(2)}) collective-permute-start(bf16[1,64,640]{2,1,0:T(8,128)(2,1)S(1)} %rows_along_x.1.own), channel_id=1, source_target_pairs={{0,4},{4,0},{8,12},{12,8},{1,5},{5,1},{9,13},{13,9},{2,6},{6,2},{1... | collective-permute-start | bytes 245768 | tf_op jit(solution)/shard_map/ppermute | solution.py:393
  23.2 13.6 %collective-permute-start.3 = (bf16[2,64,640]{2,1,0:T(8,128)(2,1)S(1)}, bf16[2,64,640]{2,1,0:T(8,128)(2,1)S(1)}, u32[]{:S(2)}, u32[]{:S(2)}) collective-permute-start(bf16[2,64,640]{2,1,0:T(8,128)(2,1)S(1)} %bitcast.20), channel_id=1, source_target_pairs={{0,8},{4,12},{8,0},{12,4},{1,9},{5,13},{9,1},{13,5},{2,10},{6,14},... | collective-permute-start | bytes 491528 | tf_op jit(solution)/shard_map/ppermute | solution.py:393
  30.2 16.7 %all-to-all-start = ((bf16[16,32,256]{2,1,0:T(8,128)(2,1)}), bf16[16,32,256]{2,1,0:T(8,128)(2,1)S(1)}, u32[]{:S(2)}, u32[]{:S(2)}) async-start(bf16[16,32,256]{2,1,0:T(8,128)(2,1)} %bitcast.5), calls=%async_computation | async-start | bytes 524288 | tf_op jit(solution)/shard_map/all_to_all | solution.py:476
  36.9 1.6 %collective-permute-start.5 = (bf16[8,32,512]{2,1,0:T(8,128)(2,1)S(1)}, bf16[8,32,512]{2,1,0:T(8,128)(2,1)S(1)}, u32[]{:S(2)}, u32[]{:S(2)}) collective-permute-start(bf16[8,32,512]{2,1,0:T(8,128)(2,1)S(1)} %bitcast.18), channel_id=1, source_target_pairs={{0,1},{1,0},{2,3},{3,2},{4,5},{5,4},{6,7},{7,6},{8,9},{9,8},{10,11... | collective-permute-start | bytes 786440 | tf_op jit(solution)/shard_map/ppermute | solution.py:393

commit v6 on v5

--- a/solution.py
+++ b/solution.py
@@ -331,37 +331,47 @@
     )(block, *map(in_near, (place, inner, *right_backs, *left_backs)))
 
 
-def finish_kernel(kcount, place, got, metric, chi, screen):
+def finish_kernel(kcount, place, got, metric, chi_out, screen_out, chi, screen, sems):
     rows, total = chi.shape
     blocks = 2 * kcount
     width = total // blocks
-    placed = dot(place[...], got[...])
-    low = iota((rows, LANES), 1) < width
-
-    def block(t):
-        straight, turned = None, None
-        for j in range(kcount):
-            at = (j * blocks + t) * rows
-            piece = placed[at : at + rows, j // 2 * LANES : (j // 2 + 1) * LANES]
-            if j % 2 == t % 2:
-                straight = piece if straight is None else straight + piece
-            else:
-                turned = piece if turned is None else turned + piece
-        return straight + pltpu.roll(turned, width, 1)
-
-    for t in range(0, blocks, 2):
-        chi[:, t * width : (t + 2) * width] = jnp.where(low, block(t), block(t + 1))
+    group = place.shape[0] // (kcount * blocks)
+    devices = got.shape[0] // rows
+    low = iota((group, LANES), 1) < width
+    for first in range(0, rows, group):
+        part = got[...]
+        if group < rows:
+            part = jnp.concatenate([part[d * rows + first : d * rows + first + group] for d in range(devices)], 0)
+        placed = dot(place[...], part)
+
+        def block(t):
+            straight, turned = None, None
+            for j in range(kcount):
+                at = (j * blocks + t) * group
+                piece = placed[at : at + group, j // 2 * LANES : (j // 2 + 1) * LANES]
+                if j % 2 == t % 2:
+                    straight = piece if straight is None else straight + piece
+                else:
+                    turned = piece if turned is None else turned + piece
+            return straight + pltpu.roll(turned, width, 1)
+
+        for t in range(0, blocks, 2):
+            chi[first : first + group, t * width : (t + 2) * width] = jnp.where(low, block(t), block(t + 1))
+    copies = started(sems, [(chi, chi_out)])
     screen[...] = dot(chi[...].astype(jnp.bfloat16), metric[...])
-
-
-def finish(place, got, metric, kcount):
-    total = metric.shape[0]
-    rows = place.shape[0] // (2 * kcount * kcount)
+    copies.append(pltpu.make_async_copy(screen, screen_out, sems.at[1]))
+    copies[-1].start()
+    finished(copies)
+
+
+def finish(place, got, metric, kcount, rows):
+    shape = (rows, metric.shape[0])
     return pl.pallas_call(
         functools.partial(finish_kernel, kcount),
         in_specs=[VMEM] * 3,
-        out_specs=[VMEM, VMEM],
-        out_shape=[jax.ShapeDtypeStruct((rows, total), jnp.float32)] * 2,
+        out_specs=[ANY, ANY],
+        out_shape=[jax.ShapeDtypeStruct(shape, jnp.float32)] * 2,
+        scratch_shapes=[pltpu.VMEM(shape, jnp.float32)] * 2 + [pltpu.SemaphoreType.DMA((2,))],
         compiler_params=limit(VMEM_LIMIT),
         name="finish",
     )(place, got, metric)
@@ -471,10 +481,10 @@
     metric = rows_along_x(parts[2], riding, ids, first_token)
     metric, all_ids = gather_metric(metric, total, out_rows, pairs, kcount, token)
     hits = all_ids.T[:, None, :] == block_ids.astype(jnp.bfloat16)[None, :, None]
-    placed = placing(hits.astype(jnp.bfloat16).reshape(kcount * blocks, devices), out_rows)
+    placed = placing(hits.astype(jnp.bfloat16).reshape(kcount * blocks, devices), min(out_rows, 16))
 
     got = lax.all_to_all(pieces.reshape(devices, out_rows, kcount * rows), everyone, 0, 0, tiled=True)
-    return tuple(finish(placed, got.reshape(devices * out_rows, kcount * rows), metric, kcount))
+    return tuple(finish(placed, got.reshape(devices * out_rows, kcount * rows), metric, kcount, out_rows))
 
 
 def solution(mesh):

time: 48.5 us -> 48.3 us (level)
  no operation moved by 1% of the time
where the time goes in v6:
time: 48.3 us; the launch traced here: 48 us
  Pallas kernels  16.7 us (35%)
  starting transfers between devices  15.9 us (33%)
  waiting for transfers between devices  14 us (29%)
  between operations  0.83 us (2%)
    ppermute x6, starting transfers between devices, swap(): return lax.ppermute(array, axes, [(i, i ^ step) for i in range(count)])  9.27 us
    all_to_all x1, waiting for transfers between devices, shards(): lax.all_to_all(pieces.reshape(devices, out_rows, kcount * rows), everyone...  8.23 us
    all_to_all x1, starting transfers between devices, shards(): lax.all_to_all(pieces.reshape(devices, out_rows, kcount * rows), everyone...  6.61 us
    ppermute x6, waiting for transfers between devices, swap(): return lax.ppermute(array, axes, [(i, i ^ step) for i in range(count)])  5.79 us
    pallas_call x1, Pallas kernels, first_blocks(): pl.pallas_call(first_kernel, in_specs=[SMEM, SMEM, ANY] + [VMEM] * 4, out...  4.93 us
    pallas_call x1, Pallas kernels, corner(): pl.pallas_call(functools.partial(corner_kernel, step), in_specs=[SMEM, AN...  3.32 us
    pallas_call x2, Pallas kernels, pick(): pl.pallas_call(functools.partial(pick_kernel, step, riding), in_specs=[AN...  2.18 us
    pallas_call x1, Pallas kernels, next_block(): pl.pallas_call(next_kernel, in_specs=[VMEM] * 5, out_specs=[VMEM] * 5, ou...  2.09 us
  transfers between devices with their start and end apart: 7, of which 4 were waited for; matrix products, arithmetic and copies ran while one was open for 1% of the time, Pallas kernels for 30%

profile of v6, /device:TPU:0, one launch (start us, length us, event | category | flops | bytes accessed | tf_op | source)
XLA Modules:
  0.0 48.0 jit_solution(3616283681167327657)
XLA Ops:
  0.6 0.0 copy-start
  0.6 0.0 copy-start.1
  0.7 0.0 copy-start.4
  0.7 1.1 %pick.2 = (bf16[1,64,4352]{2,1,0:T(8,128)(2,1)S(1)}, bf16[16,128]{1,0:T(8,128)(2,1)S(1)}) custom-call(bf16[4,64,4096]{2,1,0:T(8,128)(2,1)} %bitcast.22, bf16[32,512]{1,0:T(8,128)(2,1)} %coulomb.1), custom_call_target="tpu_custom_call" | custom-call | tf_op jit(solution)/shard_map/pick/pallas_call | solution.py:96
  1.8 3.0 %collective-permute-start = (bf16[1,64,4352]{2,1,0:T(8,128)(2,1)S(1)}, bf16[1,64,4352]{2,1,0:T(8,128)(2,1)S(1)}, u32[]{:S(2)}, u32[]{:S(2)}) collective-permute-start(bf16[1,64,4352]{2,1,0:T(8,128)(2,1)S(1)} %get-tuple-element.23), channel_id=1, source_target_pairs={{0,2},{1,3},{2,0},{3,1},{4,6},{5,7},{6,4},{7,5},{8,10},{9,11},{10,... | collective-permute-start | bytes 1671176 | tf_op jit(solution)/shard_map/ppermute | solution.py:403
  4.8 1.1 %pick.3 = (bf16[1,64,4096]{2,1,0:T(8,128)(2,1)S(1)}, bf16[16,128]{1,0:T(8,128)(2,1)S(1)}) custom-call(bf16[4,64,4096]{2,1,0:T(8,128)(2,1)} %bitcast.23, bf16[16,128]{1,0:T(8,128)(2,1)S(1)} %get-tuple-element.24.refs_1_), custom_call_target="tpu_custom_call" | custom-call | tf_op jit(solution)/shard_map/pick/pallas_call | solution.py:96
  5.9 0.1 collective-permute-start.1
  5.9 0.0 copy-done
  6.0 0.0 copy-start.2
  6.0 3.3 %corner.1 = (bf16[1,64,4224]{2,1,0:T(8,128)(2,1)S(1)}, bf16[16,128]{1,0:T(8,128)(2,1)S(1)}) custom-call(s32[4]{0:T(128)S(1)} %copy-done.4, bf16[4,64,4096]{2,1,0:T(8,128)(2,1)} %bitcast.24, bf16[4,64,64]{2,1,0:T(8,128)(2,1)S(1)} %copy-done, bf16[4,64,64]{2,1,0:T(8,128)(2,1)S(1)} %copy-done.1, bf16[16,128]{1,0:T(8,128)(2,1)S(1)} %get-tuple-element.26.hold), custom_call_target="tpu_custom_call" | custom-call | tf_op jit(solution)/shard_map/corner/pallas_call | solution.py:218
  9.3 0.2 collective-permute-start.4
  9.5 0.2 select_reduce_fusion
  9.7 0.0 collective-permute-done.1.other
  9.7 4.9 %first_blocks.1 = (bf16[256,256]{1,0:T(8,128)(2,1)S(1)}, bf16[512,512]{1,0:T(8,128)(2,1)S(1)}, bf16[512,512]{1,0:T(8,128)(2,1)S(1)}, bf16[512,256]{1,0:T(8,128)(...) custom-call(s32[4]{0:T(128)S(1)} %copy-done.4, ...), custom_call_target="tpu_custom_call" | custom-call | tf_op jit(solution)/shard_map/first_blocks/pallas_call | solution.py:258
  14.7 3.6 %collective-permute-done.block = bf16[1,64,4352]{2,1,0:T(8,128)(2,1)S(1)} collective-permute-done((bf16[1,64,4352]{2,1,0:T(8,128)(2,1)S(1)}, bf16[1,64,4352]{2,1,0:T(8,128)(2,1)S(1)}, u32[]{:S(2)}, u32[]{:S(2)}) %collective-permute-start) | collective-permute-done | bytes 557088 | tf_op jit(solution)/shard_map/ppermute | solution.py:403
  18.3 2.2 %collective-permute-start.2 = (bf16[1,64,640]{2,1,0:T(8,128)(2,1)S(1)}, bf16[1,64,640]{2,1,0:T(8,128)(2,1)S(1)}, u32[]{:S(2)}, u32[]{:S(2)}) collective-permute-start(bf16[1,64,640]{2,1,0:T(8,128)(2,1)S(1)} %rows_along_x.1.own), channel_id=1, source_target_pairs={{0,4},{4,0},{8,12},{12,8},{1,5},{5,1},{9,13},{13,9},{2,6},{6,2},{1... | collective-permute-start | bytes 245768 | tf_op jit(solution)/shard_map/ppermute | solution.py:403
  20.5 2.1 %next_block.1 = (bf16[64,4096]{1,0:T(8,128)(2,1)S(1)}, bf16[64,4096]{1,0:T(8,128)(2,1)S(1)}, bf16[64,4096]{1,0:T(8,128)(2,1)S(1)}, bf16[64,4096]{1,0:T(8,128)(2,1)S(1)}, bf16[16,128]{1,0:T(8,128)(2,1)}) custom-call(bf16[1,64,4352]{2,1,0:T(8,128)(2,1)S(1)} %collective-permute-done.block, bf16[256,256]{1,0:T(8,128)(2,1)S(1)} %get-tuple-element.30.occ, ...), custom_call_target="tpu_custom_call" | custom-call | tf_op jit(solution)/shard_map/next_block/pallas_call | solution.py:279
  22.6 0.6 %inner_chi.1 = (bf16[192,256]{1,0:T(8,128)(2,1)S(1)}, bf16[16,128]{1,0:T(8,128)(2,1)S(1)}) custom-call(bf16[128,4096]{1,0:T(8,128)(2,1)S(1)} %get-tuple-element.29.refs_0_, bf16[64,4096]{1,0:T(8,128)(2,1)S(1)} %get-tuple-element.33.refs_1_, bf16[128,4096]{1,0:T(8,128)(2,1)S(1)} %get-tuple-element.34.refs_2_, bf16[64,4096]{1,0:T(8,128)(2,1)S(1)} %get-tuple-element.35.refs_3_), custom_call_target="tpu_custom_call" | custom-call | tf_op jit(solution)/shard_map/inner_chi/pallas_call | solution.py:298
  23.2 0.0 collective-permute-done.2.other
  23.2 3.4 %collective-permute-start.3 = (bf16[2,64,640]{2,1,0:T(8,128)(2,1)S(1)}, bf16[2,64,640]{2,1,0:T(8,128)(2,1)S(1)}, u32[]{:S(2)}, u32[]{:S(2)}) collective-permute-start(bf16[2,64,640]{2,1,0:T(8,128)(2,1)S(1)} %bitcast.20), channel_id=1, source_target_pairs={{0,8},{4,12},{8,0},{12,4},{1,9},{5,13},{9,1},{13,5},{2,10},{6,14},... | collective-permute-start | bytes 491528 | tf_op jit(solution)/shard_map/ppermute | solution.py:403
  26.6 1.7 %collective-permute-done.4.block = bf16[1,64,4224]{2,1,0:T(8,128)(2,1)S(1)} collective-permute-done((bf16[1,64,4224]{2,1,0:T(8,128)(2,1)S(1)}, bf16[1,64,4224]{2,1,0:T(8,128)(2,1)S(1)}, u32[]{:S(2)}, u32[]{:S(2)}) %collective-permute-start.4) | collective-permute-done | bytes 540704 | tf_op jit(solution)/shard_map/ppermute | solution.py:403
  28.3 1.9 %last_block.1 = bf16[512,256]{1,0:T(8,128)(2,1)} custom-call(bf16[1,64,4224]{2,1,0:T(8,128)(2,1)S(1)} %collective-permute-done.4.block, bf16[512,256]{1,0:T(8,128)(2,1)S(1)} %get-tuple-element.38.place, bf16[192,256]{1,0:T(8,128)(2,1)S(1)} %get-tuple-element.39.inner, bf16[128,4096]{1,0:T(8,128)(2,1)S(1)} %get-tuple-element.40.refs_0_, ...), custom_call_target="tpu_custom_call" | custom-call | tf_op jit(solution)/shard_map/last_block/pallas_call | solution.py:324
  30.2 6.6 %all-to-all-start = ((bf16[16,32,256]{2,1,0:T(8,128)(2,1)}), bf16[16,32,256]{2,1,0:T(8,128)(2,1)S(1)}, u32[]{:S(2)}, u32[]{:S(2)}) async-start(bf16[16,32,256]{2,1,0:T(8,128)(2,1)} %bitcast.5), calls=%async_computation | async-start | bytes 524288 | tf_op jit(solution)/shard_map/all_to_all | solution.py:486
  36.8 0.0 collective-permute-done.3.other
  36.9 0.5 collective-permute-start.5
  37.4 0.1 eq.39
  37.5 0.1 copy.13
  37.5 0.1 compare_convert_fusion.hits
  37.6 0.4 placing.1.place
  38.0 0.5 %collective-permute-done.5.other = bf16[8,32,512]{2,1,0:T(8,128)(2,1)S(1)} collective-permute-done((bf16[8,32,512]{2,1,0:T(8,128)(2,1)S(1)}, bf16[8,32,512]{2,1,0:T(8,128)(2,1)S(1)}, u32[]{:S(2)}, u32[]{:S(2)}) %collective-permute-start.5) | collective-permute-done | bytes 262176 | tf_op jit(solution)/shard_map/ppermute | solution.py:403
  38.6 8.2 %all-to-all-done = bf16[16,32,256]{2,1,0:T(8,128)(2,1)S(1)} async-done(((bf16[16,32,256]{2,1,0:T(8,128)(2,1)}), bf16[16,32,256]{2,1,0:T(8,128)(2,1)S(1)}, u32[]{:S(2)}, u32[]{:S(2)}) %all-to-all-start) | async-done | bytes 262176 | tf_op jit(solution)/shard_map/all_to_all | solution.py:486
  46.8 1.2 %finish.1 = (f32[32,512]{1,0:T(8,128)}, f32[32,512]{1,0:T(8,128)}) custom-call(bf16[512,256]{1,0:T(8,128)(2,1)S(1)} %placing.1.place, bf16[512,256]{1,0:T(8,128)(2,1)S(1)} %bitcast.17, bf16[512,512]{1,0:T(8,128)(2,1)S(1)} %bitcast.13), custom_call_target="tpu_custom_call" | custom-call | tf_op jit(solution)/shard_map/finish/pallas_call | solution.py:369
  (17 shorter events, 0.2 us)
Async XLA Ops:
  0.6 5.3 %copy-start = (bf16[4,64,64]{2,1,0:T(8,128)(2,1)S(1)}, bf16[4,64,64]{2,1,0:T(8,128)(2,1)}, u32[]{:S(2)}) copy-start(bf16[4,64,64]{2,1,0:T(8,128)(2,1)} %occ.3) | copy-start | bytes 98308
  0.6 5.3 %copy-start.1 = (bf16[4,64,64]{2,1,0:T(8,128)(2,1)S(1)}, bf16[4,64,64]{2,1,0:T(8,128)(2,1)}, u32[]{:S(2)}) copy-start(bf16[4,64,64]{2,1,0:T(8,128)(2,1)} %virt.3) | copy-start | bytes 98308
  0.7 5.3 %copy-start.4 = (s32[4]{0:T(128)S(1)}, s32[4]{0:T(128)}, u32[]{:S(2)}) copy-start(s32[4]{0:T(128)} %sizes.3) | copy-start | bytes 52
  1.8 16.5 %collective-permute-start = (bf16[1,64,4352]{2,1,0:T(8,128)(2,1)S(1)}, bf16[1,64,4352]{2,1,0:T(8,128)(2,1)S(1)}, u32[]{:S(2)}, u32[]{:S(2)}) collective-permute-start(bf16[1,64,4352]{2,1,0:T(8,128)(2,1)S(1)} %get-tuple-element.23), channel_id=1, source_target_pairs={{0,2},{1,3},{2,0},{3,1},{4,6},{5,7},{6,4},{7,5},{8,10},{9,11},{10,... | collective-permute-start | bytes 1671176 | tf_op jit(solution)/shard_map/ppermute | solution.py:403
  4.8 4.7 %copy-start.3 = (s32[4,4]{1,0:T(4,128)S(1)}, s32[4,4]{1,0:T(4,128)}, u32[]{:S(2)}) copy-start(s32[4,4]{1,0:T(4,128)} %ids.1) | copy-start | bytes 196
  5.9 3.9 %collective-permute-start.1 = (bf16[1,64,4096]{2,1,0:T(8,128)(2,1)S(1)}, bf16[1,64,4096]{2,1,0:T(8,128)(2,1)S(1)}, u32[]{:S(2)}, u32[]{:S(2)}) collective-permute-start(bf16[1,64,4096]{2,1,0:T(8,128)(2,1)S(1)} %get-tuple-element.25), channel_id=1, source_target_pairs={{0,1},{1,0},{2,3},{3,2},{4,5},{5,4},{6,7},{7,6},{8,9},{9,8},{10,11... | collective-permute-start | bytes 1572872 | tf_op jit(solution)/shard_map/ppermute | solution.py:403
  6.0 12.3 %copy-start.2 = (bf16[32,512]{1,0:T(8,128)(2,1)S(1)}, bf16[32,512]{1,0:T(8,128)(2,1)}, u32[]{:S(2)}) copy-start(bf16[32,512]{1,0:T(8,128)(2,1)} %coulomb.1) | copy-start | bytes 98308
  9.3 18.9 %collective-permute-start.4 = (bf16[1,64,4224]{2,1,0:T(8,128)(2,1)S(1)}, bf16[1,64,4224]{2,1,0:T(8,128)(2,1)S(1)}, u32[]{:S(2)}, u32[]{:S(2)}) collective-permute-start(bf16[1,64,4224]{2,1,0:T(8,128)(2,1)S(1)} %get-tuple-element.37), channel_id=1, source_target_pairs={{0,3},{1,2},{2,1},{3,0},{4,7},{5,6},{6,5},{7,4},{8,11},{9,10},{10,... | collective-permute-start | bytes 1622024 | tf_op jit(solution)/shard_map/ppermute | solution.py:403
  18.3 4.9 %collective-permute-start.2 = (bf16[1,64,640]{2,1,0:T(8,128)(2,1)S(1)}, bf16[1,64,640]{2,1,0:T(8,128)(2,1)S(1)}, u32[]{:S(2)}, u32[]{:S(2)}) collective-permute-start(bf16[1,64,640]{2,1,0:T(8,128)(2,1)S(1)} %rows_along_x.1.own), channel_id=1, source_target_pairs={{0,4},{4,0},{8,12},{12,8},{1,5},{5,1},{9,13},{13,9},{2,6},{6,2},{1... | collective-permute-start | bytes 245768 | tf_op jit(solution)/shard_map/ppermute | solution.py:403
  23.2 13.6 %collective-permute-start.3 = (bf16[2,64,640]{2,1,0:T(8,128)(2,1)S(1)}, bf16[2,64,640]{2,1,0:T(8,128)(2,1)S(1)}, u32[]{:S(2)}, u32[]{:S(2)}) collective-permute-start(bf16[2,64,640]{2,1,0:T(8,128)(2,1)S(1)} %bitcast.20), channel_id=1, source_target_pairs={{0,8},{4,12},{8,0},{12,4},{1,9},{5,13},{9,1},{13,5},{2,10},{6,14},... | collective-permute-start | bytes 491528 | tf_op jit(solution)/shard_map/ppermute | solution.py:403
  30.2 16.7 %all-to-all-start = ((bf16[16,32,256]{2,1,0:T(8,128)(2,1)}), bf16[16,32,256]{2,1,0:T(8,128)(2,1)S(1)}, u32[]{:S(2)}, u32[]{:S(2)}) async-start(bf16[16,32,256]{2,1,0:T(8,128)(2,1)} %bitcast.5), calls=%async_computation | async-start | bytes 524288 | tf_op jit(solution)/shard_map/all_to_all | solution.py:486
  36.9 1.6 %collective-permute-start.5 = (bf16[8,32,512]{2,1,0:T(8,128)(2,1)S(1)}, bf16[8,32,512]{2,1,0:T(8,128)(2,1)S(1)}, u32[]{:S(2)}, u32[]{:S(2)}) collective-permute-start(bf16[8,32,512]{2,1,0:T(8,128)(2,1)S(1)} %bitcast.18), channel_id=1, source_target_pairs={{0,1},{1,0},{2,3},{3,2},{4,5},{5,4},{6,7},{7,6},{8,9},{9,8},{10,11... | collective-permute-start | bytes 786440 | tf_op jit(solution)/shard_map/ppermute | solution.py:403

commit v7 on v6

--- a/solution.py
+++ b/solution.py
@@ -430,14 +430,19 @@
     while step < ri_count:
         out = gathered(out, "ri", step).reshape(-1, rows, wide)
         step *= 2
-    step = 1
-    while step < pair_count:
-        out = gathered(out, "pair", step, hold if step == 1 else None).reshape(-1, rows, wide)
-        step *= 2
-    all_ids = out.reshape(pair_count, chips, rows, wide)[:, 0, :pairs, total : total + kcount]
+    step = pair_count // 2
+    bits = 0
+    while step:
+        out = gathered(out, "pair", step, None if bits else hold).reshape(-1, rows, wide)
+        step //= 2
+        bits += 1
+    back = tuple(reversed(range(bits)))
+    all_ids = out.reshape((2,) * bits + (chips, rows, wide))[..., 0, :pairs, total : total + kcount]
+    all_ids = all_ids.transpose(back + (bits, bits + 1)).reshape(-1, kcount)
     out = out[:, :, :total].reshape(-1, rows // 2, total)[:, :own_rows]
-    out = gathered(out, "ri", 1).swapaxes(0, 1).reshape(-1, total)
-    return out, all_ids.reshape(-1, kcount)
+    out = gathered(out, "ri", 1).reshape((2,) + (2,) * bits + (2 * chips, own_rows, total))
+    out = out.transpose(tuple(1 + bit for bit in back) + (bits + 1, 0, bits + 2, bits + 3))
+    return out.reshape(-1, total), all_ids
 
 
 def shards(three_c, green_occ, green_virt, pair_size, ri_ids, coulomb):

time: 48.3 us -> 48.3 us (level)
  starting transfers between devices: 15.9 us -> 15.2 us
  waiting for transfers between devices: 14 us -> 14.6 us
    ppermute x6, starting transfers between devices: 9.27 us -> 8.62 us  [swap(): return lax.ppermute(array, axes, [(i, i ^ step) for i in range(count)])]
    ppermute x6, waiting for transfers between devices: 5.79 us -> 6.43 us  [swap(): return lax.ppermute(array, axes, [(i, i ^ step) for i in range(count)])]
where the time goes in v7:
time: 48.3 us; the launch traced here: 48 us
  Pallas kernels  16.7 us (35%)
  starting transfers between devices  15.2 us (31%)
  waiting for transfers between devices  14.6 us (30%)
  between operations  0.84 us (2%)
    ppermute x6, starting transfers between devices, swap(): return lax.ppermute(array, axes, [(i, i ^ step) for i in range(count)])  8.62 us
    all_to_all x1, waiting for transfers between devices, shards(): lax.all_to_all(pieces.reshape(devices, out_rows, kcount * rows), everyone...  8.14 us
    all_to_all x1, starting transfers between devices, shards(): lax.all_to_all(pieces.reshape(devices, out_rows, kcount * rows), everyone...  6.61 us
    ppermute x6, waiting for transfers between devices, swap(): return lax.ppermute(array, axes, [(i, i ^ step) for i in range(count)])  6.43 us
    pallas_call x1, Pallas kernels, first_blocks(): pl.pallas_call(first_kernel, in_specs=[SMEM, SMEM, ANY] + [VMEM] * 4, out...  4.93 us
    pallas_call x1, Pallas kernels, corner(): pl.pallas_call(functools.partial(corner_kernel, step), in_specs=[SMEM, AN...  3.32 us
    pallas_call x2, Pallas kernels, pick(): pl.pallas_call(functools.partial(pick_kernel, step, riding), in_specs=[AN...  2.18 us
    pallas_call x1, Pallas kernels, next_block(): pl.pallas_call(next_kernel, in_specs=[VMEM] * 5, out_specs=[VMEM] * 5, ou...  2.09 us
  transfers between devices with their start and end apart: 7, of which 4 were waited for; matrix products, arithmetic and copies ran while one was open for 1% of the time, Pallas kernels for 30%

profile of v7, /device:TPU:0, one launch (start us, length us, event | category | flops | bytes accessed | tf_op | source)
XLA Modules:
  0.0 48.0 jit_solution(10224454940024921758)
XLA Ops:
  0.6 0.0 copy-start
  0.6 0.0 copy-start.1
  0.7 0.0 copy-start.4
  0.7 1.1 %pick.2 = (bf16[1,64,4352]{2,1,0:T(8,128)(2,1)S(1)}, bf16[16,128]{1,0:T(8,128)(2,1)S(1)}) custom-call(bf16[4,64,4096]{2,1,0:T(8,128)(2,1)} %bitcast.29, bf16[32,512]{1,0:T(8,128)(2,1)} %coulomb.1), custom_call_target="tpu_custom_call" | custom-call | tf_op jit(solution)/shard_map/pick/pallas_call | solution.py:96
  1.8 3.0 %collective-permute-start = (bf16[1,64,4352]{2,1,0:T(8,128)(2,1)S(1)}, bf16[1,64,4352]{2,1,0:T(8,128)(2,1)S(1)}, u32[]{:S(2)}, u32[]{:S(2)}) collective-permute-start(bf16[1,64,4352]{2,1,0:T(8,128)(2,1)S(1)} %get-tuple-element.23), channel_id=1, source_target_pairs={{0,2},{1,3},{2,0},{3,1},{4,6},{5,7},{6,4},{7,5},{8,10},{9,11},{10,... | collective-permute-start | bytes 1671176 | tf_op jit(solution)/shard_map/ppermute | solution.py:403
  4.8 1.1 %pick.3 = (bf16[1,64,4096]{2,1,0:T(8,128)(2,1)S(1)}, bf16[16,128]{1,0:T(8,128)(2,1)S(1)}) custom-call(bf16[4,64,4096]{2,1,0:T(8,128)(2,1)} %bitcast.30, bf16[16,128]{1,0:T(8,128)(2,1)S(1)} %get-tuple-element.24.refs_1_), custom_call_target="tpu_custom_call" | custom-call | tf_op jit(solution)/shard_map/pick/pallas_call | solution.py:96
  5.9 0.1 collective-permute-start.1
  6.0 0.0 copy-start.2
  6.0 3.3 %corner.1 = (bf16[1,64,4224]{2,1,0:T(8,128)(2,1)S(1)}, bf16[16,128]{1,0:T(8,128)(2,1)S(1)}) custom-call(s32[4]{0:T(128)S(1)} %copy-done.4, bf16[4,64,4096]{2,1,0:T(8,128)(2,1)} %bitcast.31, bf16[4,64,64]{2,1,0:T(8,128)(2,1)S(1)} %copy-done, bf16[4,64,64]{2,1,0:T(8,128)(2,1)S(1)} %copy-done.1, bf16[16,128]{1,0:T(8,128)(2,1)S(1)} %get-tuple-element.26.hold), custom_call_target="tpu_custom_call" | custom-call | tf_op jit(solution)/shard_map/corner/pallas_call | solution.py:218
  9.3 0.2 collective-permute-start.4
  9.5 0.2 select_reduce_fusion
  9.7 0.0 collective-permute-done.1.other
  9.7 4.9 %first_blocks.1 = (bf16[256,256]{1,0:T(8,128)(2,1)S(1)}, bf16[512,512]{1,0:T(8,128)(2,1)S(1)}, bf16[512,512]{1,0:T(8,128)(2,1)S(1)}, bf16[512,256]{1,0:T(8,128)(...) custom-call(s32[4]{0:T(128)S(1)} %copy-done.4, ...), custom_call_target="tpu_custom_call" | custom-call | tf_op jit(solution)/shard_map/first_blocks/pallas_call | solution.py:258
  14.7 3.6 %collective-permute-done.block = bf16[1,64,4352]{2,1,0:T(8,128)(2,1)S(1)} collective-permute-done((bf16[1,64,4352]{2,1,0:T(8,128)(2,1)S(1)}, bf16[1,64,4352]{2,1,0:T(8,128)(2,1)S(1)}, u32[]{:S(2)}, u32[]{:S(2)}) %collective-permute-start) | collective-permute-done | bytes 557088 | tf_op jit(solution)/shard_map/ppermute | solution.py:403
  18.3 3.2 %collective-permute-start.2 = (bf16[1,64,640]{2,1,0:T(8,128)(2,1)S(1)}, bf16[1,64,640]{2,1,0:T(8,128)(2,1)S(1)}, u32[]{:S(2)}, u32[]{:S(2)}) collective-permute-start(bf16[1,64,640]{2,1,0:T(8,128)(2,1)S(1)} %rows_along_x.1.own), channel_id=1, source_target_pairs={{0,8},{4,12},{8,0},{12,4},{1,9},{5,13},{9,1},{13,5},{2,10},{6,14},... | collective-permute-start | bytes 245768 | tf_op jit(solution)/shard_map/ppermute | solution.py:403
  21.5 2.1 %next_block.1 = (bf16[64,4096]{1,0:T(8,128)(2,1)S(1)}, bf16[64,4096]{1,0:T(8,128)(2,1)S(1)}, bf16[64,4096]{1,0:T(8,128)(2,1)S(1)}, bf16[64,4096]{1,0:T(8,128)(2,1)S(1)}, bf16[16,128]{1,0:T(8,128)(2,1)}) custom-call(bf16[1,64,4352]{2,1,0:T(8,128)(2,1)S(1)} %collective-permute-done.block, bf16[256,256]{1,0:T(8,128)(2,1)S(1)} %get-tuple-element.30.occ, ...), custom_call_target="tpu_custom_call" | custom-call | tf_op jit(solution)/shard_map/next_block/pallas_call | solution.py:279
  23.6 0.6 %inner_chi.1 = (bf16[192,256]{1,0:T(8,128)(2,1)S(1)}, bf16[16,128]{1,0:T(8,128)(2,1)S(1)}) custom-call(bf16[128,4096]{1,0:T(8,128)(2,1)S(1)} %get-tuple-element.29.refs_0_, bf16[64,4096]{1,0:T(8,128)(2,1)S(1)} %get-tuple-element.33.refs_1_, bf16[128,4096]{1,0:T(8,128)(2,1)S(1)} %get-tuple-element.34.refs_2_, bf16[64,4096]{1,0:T(8,128)(2,1)S(1)} %get-tuple-element.35.refs_3_), custom_call_target="tpu_custom_call" | custom-call | tf_op jit(solution)/shard_map/inner_chi/pallas_call | solution.py:298
  24.2 0.0 collective-permute-done.2.other
  24.2 1.7 %collective-permute-start.3 = (bf16[2,64,640]{2,1,0:T(8,128)(2,1)S(1)}, bf16[2,64,640]{2,1,0:T(8,128)(2,1)S(1)}, u32[]{:S(2)}, u32[]{:S(2)}) collective-permute-start(bf16[2,64,640]{2,1,0:T(8,128)(2,1)S(1)} %bitcast.27), channel_id=1, source_target_pairs={{0,4},{4,0},{8,12},{12,8},{1,5},{5,1},{9,13},{13,9},{2,6},{6,2},{1... | collective-permute-start | bytes 491528 | tf_op jit(solution)/shard_map/ppermute | solution.py:403
  25.9 2.4 %collective-permute-done.4.block = bf16[1,64,4224]{2,1,0:T(8,128)(2,1)S(1)} collective-permute-done((bf16[1,64,4224]{2,1,0:T(8,128)(2,1)S(1)}, bf16[1,64,4224]{2,1,0:T(8,128)(2,1)S(1)}, u32[]{:S(2)}, u32[]{:S(2)}) %collective-permute-start.4) | collective-permute-done | bytes 540704 | tf_op jit(solution)/shard_map/ppermute | solution.py:403
  28.3 1.9 %last_block.1 = bf16[512,256]{1,0:T(8,128)(2,1)} custom-call(bf16[1,64,4224]{2,1,0:T(8,128)(2,1)S(1)} %collective-permute-done.4.block, bf16[512,256]{1,0:T(8,128)(2,1)S(1)} %get-tuple-element.38.place, bf16[192,256]{1,0:T(8,128)(2,1)S(1)} %get-tuple-element.39.inner, bf16[128,4096]{1,0:T(8,128)(2,1)S(1)} %get-tuple-element.40.refs_0_, ...), custom_call_target="tpu_custom_call" | custom-call | tf_op jit(solution)/shard_map/last_block/pallas_call | solution.py:324
  30.2 6.6 %all-to-all-start = ((bf16[16,32,256]{2,1,0:T(8,128)(2,1)}), bf16[16,32,256]{2,1,0:T(8,128)(2,1)S(1)}, u32[]{:S(2)}, u32[]{:S(2)}) async-start(bf16[16,32,256]{2,1,0:T(8,128)(2,1)} %bitcast.7), calls=%async_computation | async-start | bytes 524288 | tf_op jit(solution)/shard_map/all_to_all | solution.py:491
  36.8 0.1 eq.39
  36.9 0.0 collective-permute-done.3.other
  37.0 0.5 collective-permute-start.5
  37.4 0.1 copy.10
  37.6 0.1 reshape.54
  37.7 0.1 compare_convert_fusion.hits
  37.7 0.4 placing.1.place
  38.1 0.5 %collective-permute-done.5.other = bf16[8,32,512]{2,1,0:T(8,128)(2,1)S(1)} collective-permute-done((bf16[8,32,512]{2,1,0:T(8,128)(2,1)S(1)}, bf16[8,32,512]{2,1,0:T(8,128)(2,1)S(1)}, u32[]{:S(2)}, u32[]{:S(2)}) %collective-permute-start.5) | collective-permute-done | bytes 262176 | tf_op jit(solution)/shard_map/ppermute | solution.py:403
  38.7 8.1 %all-to-all-done = bf16[16,32,256]{2,1,0:T(8,128)(2,1)S(1)} async-done(((bf16[16,32,256]{2,1,0:T(8,128)(2,1)}), bf16[16,32,256]{2,1,0:T(8,128)(2,1)S(1)}, u32[]{:S(2)}, u32[]{:S(2)}) %all-to-all-start) | async-done | bytes 262176 | tf_op jit(solution)/shard_map/all_to_all | solution.py:491
  46.8 1.2 %finish.1 = (f32[32,512]{1,0:T(8,128)}, f32[32,512]{1,0:T(8,128)}) custom-call(bf16[512,256]{1,0:T(8,128)(2,1)S(1)} %placing.1.place, bf16[512,256]{1,0:T(8,128)(2,1)S(1)} %bitcast.24, bf16[512,512]{1,0:T(8,128)(2,1)S(1)} %bitcast.20), custom_call_target="tpu_custom_call" | custom-call | tf_op jit(solution)/shard_map/finish/pallas_call | solution.py:369
  (18 shorter events, 0.2 us)
Async XLA Ops:
  0.6 5.3 %copy-start = (bf16[4,64,64]{2,1,0:T(8,128)(2,1)S(1)}, bf16[4,64,64]{2,1,0:T(8,128)(2,1)}, u32[]{:S(2)}) copy-start(bf16[4,64,64]{2,1,0:T(8,128)(2,1)} %occ.3) | copy-start | bytes 98308
  0.6 5.3 %copy-start.1 = (bf16[4,64,64]{2,1,0:T(8,128)(2,1)S(1)}, bf16[4,64,64]{2,1,0:T(8,128)(2,1)}, u32[]{:S(2)}) copy-start(bf16[4,64,64]{2,1,0:T(8,128)(2,1)} %virt.3) | copy-start | bytes 98308
  0.7 5.3 %copy-start.4 = (s32[4]{0:T(128)S(1)}, s32[4]{0:T(128)}, u32[]{:S(2)}) copy-start(s32[4]{0:T(128)} %sizes.3) | copy-start | bytes 52
  1.8 16.5 %collective-permute-start = (bf16[1,64,4352]{2,1,0:T(8,128)(2,1)S(1)}, bf16[1,64,4352]{2,1,0:T(8,128)(2,1)S(1)}, u32[]{:S(2)}, u32[]{:S(2)}) collective-permute-start(bf16[1,64,4352]{2,1,0:T(8,128)(2,1)S(1)} %get-tuple-element.23), channel_id=1, source_target_pairs={{0,2},{1,3},{2,0},{3,1},{4,6},{5,7},{6,4},{7,5},{8,10},{9,11},{10,... | collective-permute-start | bytes 1671176 | tf_op jit(solution)/shard_map/ppermute | solution.py:403
  4.8 4.7 %copy-start.3 = (s32[4,4]{1,0:T(4,128)S(1)}, s32[4,4]{1,0:T(4,128)}, u32[]{:S(2)}) copy-start(s32[4,4]{1,0:T(4,128)} %ids.1) | copy-start | bytes 196
  5.9 3.9 %collective-permute-start.1 = (bf16[1,64,4096]{2,1,0:T(8,128)(2,1)S(1)}, bf16[1,64,4096]{2,1,0:T(8,128)(2,1)S(1)}, u32[]{:S(2)}, u32[]{:S(2)}) collective-permute-start(bf16[1,64,4096]{2,1,0:T(8,128)(2,1)S(1)} %get-tuple-element.25), channel_id=1, source_target_pairs={{0,1},{1,0},{2,3},{3,2},{4,5},{5,4},{6,7},{7,6},{8,9},{9,8},{10,11... | collective-permute-start | bytes 1572872 | tf_op jit(solution)/shard_map/ppermute | solution.py:403
  6.0 12.3 %copy-start.2 = (bf16[32,512]{1,0:T(8,128)(2,1)S(1)}, bf16[32,512]{1,0:T(8,128)(2,1)}, u32[]{:S(2)}) copy-start(bf16[32,512]{1,0:T(8,128)(2,1)} %coulomb.1) | copy-start | bytes 98308
  9.3 18.9 %collective-permute-start.4 = (bf16[1,64,4224]{2,1,0:T(8,128)(2,1)S(1)}, bf16[1,64,4224]{2,1,0:T(8,128)(2,1)S(1)}, u32[]{:S(2)}, u32[]{:S(2)}) collective-permute-start(bf16[1,64,4224]{2,1,0:T(8,128)(2,1)S(1)} %get-tuple-element.37), channel_id=1, source_target_pairs={{0,3},{1,2},{2,1},{3,0},{4,7},{5,6},{6,5},{7,4},{8,11},{9,10},{10,... | collective-permute-start | bytes 1622024 | tf_op jit(solution)/shard_map/ppermute | solution.py:403
  18.3 5.9 %collective-permute-start.2 = (bf16[1,64,640]{2,1,0:T(8,128)(2,1)S(1)}, bf16[1,64,640]{2,1,0:T(8,128)(2,1)S(1)}, u32[]{:S(2)}, u32[]{:S(2)}) collective-permute-start(bf16[1,64,640]{2,1,0:T(8,128)(2,1)S(1)} %rows_along_x.1.own), channel_id=1, source_target_pairs={{0,8},{4,12},{8,0},{12,4},{1,9},{5,13},{9,1},{13,5},{2,10},{6,14},... | collective-permute-start | bytes 245768 | tf_op jit(solution)/shard_map/ppermute | solution.py:403
  24.2 12.7 %collective-permute-start.3 = (bf16[2,64,640]{2,1,0:T(8,128)(2,1)S(1)}, bf16[2,64,640]{2,1,0:T(8,128)(2,1)S(1)}, u32[]{:S(2)}, u32[]{:S(2)}) collective-permute-start(bf16[2,64,640]{2,1,0:T(8,128)(2,1)S(1)} %bitcast.27), channel_id=1, source_target_pairs={{0,4},{4,0},{8,12},{12,8},{1,5},{5,1},{9,13},{13,9},{2,6},{6,2},{1... | collective-permute-start | bytes 491528 | tf_op jit(solution)/shard_map/ppermute | solution.py:403
  30.2 16.7 %all-to-all-start = ((bf16[16,32,256]{2,1,0:T(8,128)(2,1)}), bf16[16,32,256]{2,1,0:T(8,128)(2,1)S(1)}, u32[]{:S(2)}, u32[]{:S(2)}) async-start(bf16[16,32,256]{2,1,0:T(8,128)(2,1)} %bitcast.7), calls=%async_computation | async-start | bytes 524288 | tf_op jit(solution)/shard_map/all_to_all | solution.py:491
  37.0 1.6 %collective-permute-start.5 = (bf16[8,32,512]{2,1,0:T(8,128)(2,1)S(1)}, bf16[8,32,512]{2,1,0:T(8,128)(2,1)S(1)}, u32[]{:S(2)}, u32[]{:S(2)}) collective-permute-start(bf16[8,32,512]{2,1,0:T(8,128)(2,1)S(1)} %bitcast.25), channel_id=1, source_target_pairs={{0,1},{1,0},{2,3},{3,2},{4,5},{5,4},{6,7},{7,6},{8,9},{9,8},{10,11... | collective-permute-start | bytes 786440 | tf_op jit(solution)/shard_map/ppermute | solution.py:403

commit v8 on v6

--- a/solution.py
+++ b/solution.py
@@ -286,49 +286,54 @@
     )(block, *map(in_near, (occ, virt, virt_back)), hold)
 
 
-def inner_kernel(count, *refs):
-    out, token = refs[2 * count :]
+def inner_kernel(count, place, *refs):
+    tail, head, token = refs[2 * count :]
     token[...] = jnp.zeros_like(token)
-    out[...] = long_dot(refs[:count], refs[count : 2 * count], out.shape[1] - out.shape[0]).astype(jnp.bfloat16)
-
-
-def inner_chi(lefts, rights):
+    high, wide = place.shape[1] - tail.shape[1] // 2, place.shape[1]
+    inner = long_dot(refs[:count], refs[count : 2 * count], wide - high).astype(jnp.bfloat16)
+    tail[...] = inner[:, head.shape[1] :]
+    padded = jnp.concatenate([inner[:, : head.shape[1]], jnp.zeros((wide - high, head.shape[1]), jnp.bfloat16)], 0)
+    head[...] = dot(place[...], padded).astype(jnp.bfloat16)
+
+
+def inner_chi(place, lefts, rights):
     rows = sum(left.shape[0] for left in lefts)
     wide = rows + lefts[-1].shape[0]
     return pl.pallas_call(
         functools.partial(inner_kernel, len(lefts)),
-        in_specs=[VMEM] * (2 * len(lefts)),
-        out_specs=[VMEM, VMEM],
-        out_shape=[near((rows, wide)), half(TOKEN)],
+        in_specs=[VMEM] * (1 + 2 * len(lefts)),
+        out_specs=[VMEM] * 3,
+        out_shape=[near((rows, LANES)), near((place.shape[0], wide - LANES)), half(TOKEN)],
         compiler_params=limit(VMEM_LIMIT),
         name="inner_chi",
-    )(*map(in_near, lefts + rights))
-
-
-def last_kernel(count, block, place, inner, *refs):
-    right_backs, left_backs, out = refs[:count], refs[count : 2 * count], refs[2 * count]
+    )(*map(in_near, [place] + lefts + rights))
+
+
+def last_kernel(count, block, place, tail, head, *refs):
+    right_backs, left_backs = refs[:count], refs[count : 2 * count]
+    out = refs[2 * count]
     square = left_backs[0].shape[1]
     rows = block.shape[1]
+    split = head.shape[1]
     came = block.at[0, :, pl.ds(0, square)]
-    aside = jnp.zeros((rows, inner.shape[1] - 2 * rows), jnp.float32)
     bottom = long_dot([came], right_backs, rows)
-    bottom = bottom + jnp.concatenate([aside, block[0, :, square:].astype(jnp.float32)], 1)
+    early = jnp.concatenate([jnp.zeros((LANES - rows, split), jnp.bfloat16), bottom[:, :split].astype(jnp.bfloat16)], 0)
+    low = bottom[:, split:] + block[0, :, square:].astype(jnp.float32)
     columns = long_dot(left_backs, [came], -rows)
-    head, tail = inner[:, : -2 * rows], inner[:, -2 * rows :]
-    top = jnp.concatenate([head, tail + columns.astype(jnp.bfloat16)], 1)
-    total = jnp.concatenate([top, bottom.astype(jnp.bfloat16)], 0)
-    out[...] = dot(place[...], total).astype(jnp.bfloat16)
-
-
-def last_block(block, place, inner, right_backs, left_backs):
+    late = jnp.concatenate([tail[...] + columns.astype(jnp.bfloat16), low.astype(jnp.bfloat16)], 0)
+    out[:, split:] = dot(place[...], late).astype(jnp.bfloat16)
+    out[:, :split] = head[...] + dot(place[:, split:], early).astype(jnp.bfloat16)
+
+
+def last_block(block, place, tail, head, right_backs, left_backs):
     return pl.pallas_call(
         functools.partial(last_kernel, len(left_backs)),
-        in_specs=[VMEM] * (3 + 2 * len(left_backs)),
+        in_specs=[VMEM] * (4 + 2 * len(left_backs)),
         out_specs=VMEM,
         out_shape=half(place.shape),
         compiler_params=limit(VMEM_LIMIT),
         name="last_block",
-    )(block, *map(in_near, (place, inner, *right_backs, *left_backs)))
+    )(block, *map(in_near, (place, tail, head, *right_backs, *left_backs)))
 
 
 def finish_kernel(kcount, place, got, metric, chi_out, screen_out, chi, screen, sems):
@@ -342,13 +347,16 @@
         part = got[...]
         if group < rows:
             part = jnp.concatenate([part[d * rows + first : d * rows + first + group] for d in range(devices)], 0)
-        placed = dot(place[...], part)
+        step = 2 * blocks * group
+        placed = [
+            dot(place[h * step : (h + 1) * step, :], part[:, h * LANES : (h + 1) * LANES]) for h in range(kcount // 2)
+        ]
 
         def block(t):
             straight, turned = None, None
             for j in range(kcount):
-                at = (j * blocks + t) * group
-                piece = placed[at : at + group, j // 2 * LANES : (j // 2 + 1) * LANES]
+                at = (j % 2 * blocks + t) * group
+                piece = placed[j // 2][at : at + group]
                 if j % 2 == t % 2:
                     straight = piece if straight is None else straight + piece
                 else:
@@ -472,8 +480,8 @@
         rights.append(right)
         left_backs.append(left_back)
         right_backs.append(right_back)
-    inner, token = inner_chi(lefts, rights)
-    pieces = last_block(parts[last], place, inner, right_backs, left_backs)
+    tail, head, token = inner_chi(place, lefts, rights)
+    pieces = last_block(parts[last], place, tail, head, right_backs, left_backs)
 
     slot = jnp.arange(pairs, dtype=jnp.int32)[:, None] ^ slots[None, :]
     relative = jnp.sum(jnp.where(slot[:, :, None] == slots, ri_ids[:, None, :], 0), 2)

time: 48.3 us -> 48.3 us (level)
  transfers between devices with their start and end apart: 7 -> 7, of which waited for: 4 -> 4; matrix products, arithmetic and copies ran while one was open for 1% -> 1% of each run, Pallas kernels for 30% -> 31%
where the time goes in v8:
time: 48.3 us; the launch traced here: 48 us
  Pallas kernels  17 us (35%)
  starting transfers between devices  15.6 us (32%)
  waiting for transfers between devices  14.1 us (29%)
  between operations  0.83 us (2%)
    ppermute x6, starting transfers between devices, swap(): return lax.ppermute(array, axes, [(i, i ^ step) for i in range(count)])  8.94 us
    all_to_all x1, waiting for transfers between devices, shards(): lax.all_to_all(pieces.reshape(devices, out_rows, kcount * rows), everyone...  8.23 us
    all_to_all x1, starting transfers between devices, shards(): lax.all_to_all(pieces.reshape(devices, out_rows, kcount * rows), everyone...  6.62 us
    ppermute x6, waiting for transfers between devices, swap(): return lax.ppermute(array, axes, [(i, i ^ step) for i in range(count)])  5.84 us
    pallas_call x1, Pallas kernels, first_blocks(): pl.pallas_call(first_kernel, in_specs=[SMEM, SMEM, ANY] + [VMEM] * 4, out...  4.88 us
    pallas_call x1, Pallas kernels, corner(): pl.pallas_call(functools.partial(corner_kernel, step), in_specs=[SMEM, AN...  3.32 us
    pallas_call x2, Pallas kernels, pick(): pl.pallas_call(functools.partial(pick_kernel, step, riding), in_specs=[AN...  2.18 us
    pallas_call x1, Pallas kernels, next_block(): pl.pallas_call(next_kernel, in_specs=[VMEM] * 5, out_specs=[VMEM] * 5, ou...  2.09 us
  transfers between devices with their start and end apart: 7, of which 4 were waited for; matrix products, arithmetic and copies ran while one was open for 1% of the time, Pallas kernels for 31%

profile of v8, /device:TPU:0, one launch (start us, length us, event | category | flops | bytes accessed | tf_op | source)
XLA Modules:
  0.0 48.0 jit_solution(13479811673448735614)
XLA Ops:
  0.6 0.0 copy-start
  0.6 0.0 copy-start.1
  0.7 0.0 copy-start.4
  0.7 1.1 %pick.2 = (bf16[1,64,4352]{2,1,0:T(8,128)(2,1)S(1)}, bf16[16,128]{1,0:T(8,128)(2,1)S(1)}) custom-call(bf16[4,64,4096]{2,1,0:T(8,128)(2,1)} %bitcast.22, bf16[32,512]{1,0:T(8,128)(2,1)} %coulomb.1), custom_call_target="tpu_custom_call" | custom-call | tf_op jit(solution)/shard_map/pick/pallas_call | solution.py:96
  1.8 3.0 %collective-permute-start = (bf16[1,64,4352]{2,1,0:T(8,128)(2,1)S(1)}, bf16[1,64,4352]{2,1,0:T(8,128)(2,1)S(1)}, u32[]{:S(2)}, u32[]{:S(2)}) collective-permute-start(bf16[1,64,4352]{2,1,0:T(8,128)(2,1)S(1)} %get-tuple-element.24), channel_id=1, source_target_pairs={{0,2},{1,3},{2,0},{3,1},{4,6},{5,7},{6,4},{7,5},{8,10},{9,11},{10,... | collective-permute-start | bytes 1671176 | tf_op jit(solution)/shard_map/ppermute | solution.py:411
  4.8 1.1 %pick.3 = (bf16[1,64,4096]{2,1,0:T(8,128)(2,1)S(1)}, bf16[16,128]{1,0:T(8,128)(2,1)S(1)}) custom-call(bf16[4,64,4096]{2,1,0:T(8,128)(2,1)} %bitcast.23, bf16[16,128]{1,0:T(8,128)(2,1)S(1)} %get-tuple-element.25.refs_1_), custom_call_target="tpu_custom_call" | custom-call | tf_op jit(solution)/shard_map/pick/pallas_call | solution.py:96
  5.9 0.1 collective-permute-start.1
  5.9 0.0 copy-done
  6.0 0.0 copy-start.2
  6.0 3.3 %corner.1 = (bf16[1,64,4224]{2,1,0:T(8,128)(2,1)S(1)}, bf16[16,128]{1,0:T(8,128)(2,1)S(1)}) custom-call(s32[4]{0:T(128)S(1)} %copy-done.4, bf16[4,64,4096]{2,1,0:T(8,128)(2,1)} %bitcast.24, bf16[4,64,64]{2,1,0:T(8,128)(2,1)S(1)} %copy-done, bf16[4,64,64]{2,1,0:T(8,128)(2,1)S(1)} %copy-done.1, bf16[16,128]{1,0:T(8,128)(2,1)S(1)} %get-tuple-element.27.hold), custom_call_target="tpu_custom_call" | custom-call | tf_op jit(solution)/shard_map/corner/pallas_call | solution.py:218
  9.3 0.2 collective-permute-start.4
  9.5 0.2 select_reduce_fusion
  9.7 0.0 collective-permute-done.1.other
  9.7 4.9 %first_blocks.1 = (bf16[256,256]{1,0:T(8,128)(2,1)S(1)}, bf16[512,512]{1,0:T(8,128)(2,1)S(1)}, bf16[512,512]{1,0:T(8,128)(2,1)S(1)}, bf16[512,256]{1,0:T(8,128)(...) custom-call(s32[4]{0:T(128)S(1)} %copy-done.4, ...), custom_call_target="tpu_custom_call" | custom-call | tf_op jit(solution)/shard_map/first_blocks/pallas_call | solution.py:258
  14.6 3.6 %collective-permute-done.block = bf16[1,64,4352]{2,1,0:T(8,128)(2,1)S(1)} collective-permute-done((bf16[1,64,4352]{2,1,0:T(8,128)(2,1)S(1)}, bf16[1,64,4352]{2,1,0:T(8,128)(2,1)S(1)}, u32[]{:S(2)}, u32[]{:S(2)}) %collective-permute-start) | collective-permute-done | bytes 557088 | tf_op jit(solution)/shard_map/ppermute | solution.py:411
  18.3 2.2 %collective-permute-start.2 = (bf16[1,64,640]{2,1,0:T(8,128)(2,1)S(1)}, bf16[1,64,640]{2,1,0:T(8,128)(2,1)S(1)}, u32[]{:S(2)}, u32[]{:S(2)}) collective-permute-start(bf16[1,64,640]{2,1,0:T(8,128)(2,1)S(1)} %rows_along_x.1.own), channel_id=1, source_target_pairs={{0,4},{4,0},{8,12},{12,8},{1,5},{5,1},{9,13},{13,9},{2,6},{6,2},{1... | collective-permute-start | bytes 245768 | tf_op jit(solution)/shard_map/ppermute | solution.py:411
  20.5 2.1 %next_block.1 = (bf16[64,4096]{1,0:T(8,128)(2,1)S(1)}, bf16[64,4096]{1,0:T(8,128)(2,1)S(1)}, bf16[64,4096]{1,0:T(8,128)(2,1)S(1)}, bf16[64,4096]{1,0:T(8,128)(2,1)S(1)}, bf16[16,128]{1,0:T(8,128)(2,1)}) custom-call(bf16[1,64,4352]{2,1,0:T(8,128)(2,1)S(1)} %collective-permute-done.block, bf16[256,256]{1,0:T(8,128)(2,1)S(1)} %get-tuple-element.32.occ, ...), custom_call_target="tpu_custom_call" | custom-call | tf_op jit(solution)/shard_map/next_block/pallas_call | solution.py:279
  22.6 0.9 %inner_chi.1 = (bf16[192,128]{1,0:T(8,128)(2,1)S(1)}, bf16[512,128]{1,0:T(8,128)(2,1)S(1)}, bf16[16,128]{1,0:T(8,128)(2,1)S(1)}) custom-call(bf16[512,256]{1,0:T(8,128)(2,1)S(1)} %get-tuple-element.30.place, bf16[128,4096]{1,0:T(8,128)(2,1)S(1)} %get-tuple-element.31.refs_0_, bf16[64,4096]{1,0:T(8,128)(2,1)S(1)} %get-tuple-element.35.refs_1_, ...), custom_call_target="tpu_custom_call" | custom-call | tf_op jit(solution)/shard_map/inner_chi/pallas_call | solution.py:302
  23.5 0.0 collective-permute-done.2.other
  23.5 3.0 %collective-permute-start.3 = (bf16[2,64,640]{2,1,0:T(8,128)(2,1)S(1)}, bf16[2,64,640]{2,1,0:T(8,128)(2,1)S(1)}, u32[]{:S(2)}, u32[]{:S(2)}) collective-permute-start(bf16[2,64,640]{2,1,0:T(8,128)(2,1)S(1)} %bitcast.20), channel_id=1, source_target_pairs={{0,8},{4,12},{8,0},{12,4},{1,9},{5,13},{9,1},{13,5},{2,10},{6,14},... | collective-permute-start | bytes 491528 | tf_op jit(solution)/shard_map/ppermute | solution.py:411
  26.6 1.7 %collective-permute-done.4.block = bf16[1,64,4224]{2,1,0:T(8,128)(2,1)S(1)} collective-permute-done((bf16[1,64,4224]{2,1,0:T(8,128)(2,1)S(1)}, bf16[1,64,4224]{2,1,0:T(8,128)(2,1)S(1)}, u32[]{:S(2)}, u32[]{:S(2)}) %collective-permute-start.4) | collective-permute-done | bytes 540704 | tf_op jit(solution)/shard_map/ppermute | solution.py:411
  28.3 1.9 %last_block.1 = bf16[512,256]{1,0:T(8,128)(2,1)} custom-call(bf16[1,64,4224]{2,1,0:T(8,128)(2,1)S(1)} %collective-permute-done.4.block, bf16[512,256]{1,0:T(8,128)(2,1)S(1)} %get-tuple-element.30.place, bf16[192,128]{1,0:T(8,128)(2,1)S(1)} %get-tuple-element.40.tail, bf16[512,128]{1,0:T(8,128)(2,1)S(1)} %get-tuple-element.41.head, ...), custom_call_target="tpu_custom_call" | custom-call | tf_op jit(solution)/shard_map/last_block/pallas_call | solution.py:329
  30.2 6.6 %all-to-all-start = ((bf16[16,32,256]{2,1,0:T(8,128)(2,1)}), bf16[16,32,256]{2,1,0:T(8,128)(2,1)S(1)}, u32[]{:S(2)}, u32[]{:S(2)}) async-start(bf16[16,32,256]{2,1,0:T(8,128)(2,1)} %bitcast.5), calls=%async_computation | async-start | bytes 524288 | tf_op jit(solution)/shard_map/all_to_all | solution.py:494
  36.8 0.0 collective-permute-done.3.other
  36.9 0.5 collective-permute-start.5
  37.4 0.1 eq.39
  37.5 0.1 copy.13
  37.6 0.1 compare_convert_fusion.hits
  37.7 0.4 placing.1.place
  38.0 0.5 %collective-permute-done.5.other = bf16[8,32,512]{2,1,0:T(8,128)(2,1)S(1)} collective-permute-done((bf16[8,32,512]{2,1,0:T(8,128)(2,1)S(1)}, bf16[8,32,512]{2,1,0:T(8,128)(2,1)S(1)}, u32[]{:S(2)}, u32[]{:S(2)}) %collective-permute-start.5) | collective-permute-done | bytes 262176 | tf_op jit(solution)/shard_map/ppermute | solution.py:411
  38.6 8.2 %all-to-all-done = bf16[16,32,256]{2,1,0:T(8,128)(2,1)S(1)} async-done(((bf16[16,32,256]{2,1,0:T(8,128)(2,1)}), bf16[16,32,256]{2,1,0:T(8,128)(2,1)S(1)}, u32[]{:S(2)}, u32[]{:S(2)}) %all-to-all-start) | async-done | bytes 262176 | tf_op jit(solution)/shard_map/all_to_all | solution.py:494
  46.9 1.1 %finish.1 = (f32[32,512]{1,0:T(8,128)}, f32[32,512]{1,0:T(8,128)}) custom-call(bf16[512,256]{1,0:T(8,128)(2,1)S(1)} %placing.1.place, bf16[512,256]{1,0:T(8,128)(2,1)S(1)} %bitcast.17, bf16[512,512]{1,0:T(8,128)(2,1)S(1)} %bitcast.13), custom_call_target="tpu_custom_call" | custom-call | tf_op jit(solution)/shard_map/finish/pallas_call | solution.py:377
  (17 shorter events, 0.2 us)
Async XLA Ops:
  0.6 5.3 %copy-start = (bf16[4,64,64]{2,1,0:T(8,128)(2,1)S(1)}, bf16[4,64,64]{2,1,0:T(8,128)(2,1)}, u32[]{:S(2)}) copy-start(bf16[4,64,64]{2,1,0:T(8,128)(2,1)} %occ.3) | copy-start | bytes 98308
  0.6 5.3 %copy-start.1 = (bf16[4,64,64]{2,1,0:T(8,128)(2,1)S(1)}, bf16[4,64,64]{2,1,0:T(8,128)(2,1)}, u32[]{:S(2)}) copy-start(bf16[4,64,64]{2,1,0:T(8,128)(2,1)} %virt.3) | copy-start | bytes 98308
  0.7 5.3 %copy-start.4 = (s32[4]{0:T(128)S(1)}, s32[4]{0:T(128)}, u32[]{:S(2)}) copy-start(s32[4]{0:T(128)} %sizes.3) | copy-start | bytes 52
  1.8 16.5 %collective-permute-start = (bf16[1,64,4352]{2,1,0:T(8,128)(2,1)S(1)}, bf16[1,64,4352]{2,1,0:T(8,128)(2,1)S(1)}, u32[]{:S(2)}, u32[]{:S(2)}) collective-permute-start(bf16[1,64,4352]{2,1,0:T(8,128)(2,1)S(1)} %get-tuple-element.24), channel_id=1, source_target_pairs={{0,2},{1,3},{2,0},{3,1},{4,6},{5,7},{6,4},{7,5},{8,10},{9,11},{10,... | collective-permute-start | bytes 1671176 | tf_op jit(solution)/shard_map/ppermute | solution.py:411
  4.8 4.7 %copy-start.3 = (s32[4,4]{1,0:T(4,128)S(1)}, s32[4,4]{1,0:T(4,128)}, u32[]{:S(2)}) copy-start(s32[4,4]{1,0:T(4,128)} %ids.1) | copy-start | bytes 196
  5.9 3.9 %collective-permute-start.1 = (bf16[1,64,4096]{2,1,0:T(8,128)(2,1)S(1)}, bf16[1,64,4096]{2,1,0:T(8,128)(2,1)S(1)}, u32[]{:S(2)}, u32[]{:S(2)}) collective-permute-start(bf16[1,64,4096]{2,1,0:T(8,128)(2,1)S(1)} %get-tuple-element.26), channel_id=1, source_target_pairs={{0,1},{1,0},{2,3},{3,2},{4,5},{5,4},{6,7},{7,6},{8,9},{9,8},{10,11... | collective-permute-start | bytes 1572872 | tf_op jit(solution)/shard_map/ppermute | solution.py:411
  6.0 12.3 %copy-start.2 = (bf16[32,512]{1,0:T(8,128)(2,1)S(1)}, bf16[32,512]{1,0:T(8,128)(2,1)}, u32[]{:S(2)}) copy-start(bf16[32,512]{1,0:T(8,128)(2,1)} %coulomb.1) | copy-start | bytes 98308
  9.3 18.9 %collective-permute-start.4 = (bf16[1,64,4224]{2,1,0:T(8,128)(2,1)S(1)}, bf16[1,64,4224]{2,1,0:T(8,128)(2,1)S(1)}, u32[]{:S(2)}, u32[]{:S(2)}) collective-permute-start(bf16[1,64,4224]{2,1,0:T(8,128)(2,1)S(1)} %get-tuple-element.39), channel_id=1, source_target_pairs={{0,3},{1,2},{2,1},{3,0},{4,7},{5,6},{6,5},{7,4},{8,11},{9,10},{10,... | collective-permute-start | bytes 1622024 | tf_op jit(solution)/shard_map/ppermute | solution.py:411
  18.3 5.2 %collective-permute-start.2 = (bf16[1,64,640]{2,1,0:T(8,128)(2,1)S(1)}, bf16[1,64,640]{2,1,0:T(8,128)(2,1)S(1)}, u32[]{:S(2)}, u32[]{:S(2)}) collective-permute-start(bf16[1,64,640]{2,1,0:T(8,128)(2,1)S(1)} %rows_along_x.1.own), channel_id=1, source_target_pairs={{0,4},{4,0},{8,12},{12,8},{1,5},{5,1},{9,13},{13,9},{2,6},{6,2},{1... | collective-permute-start | bytes 245768 | tf_op jit(solution)/shard_map/ppermute | solution.py:411
  23.5 13.3 %collective-permute-start.3 = (bf16[2,64,640]{2,1,0:T(8,128)(2,1)S(1)}, bf16[2,64,640]{2,1,0:T(8,128)(2,1)S(1)}, u32[]{:S(2)}, u32[]{:S(2)}) collective-permute-start(bf16[2,64,640]{2,1,0:T(8,128)(2,1)S(1)} %bitcast.20), channel_id=1, source_target_pairs={{0,8},{4,12},{8,0},{12,4},{1,9},{5,13},{9,1},{13,5},{2,10},{6,14},... | collective-permute-start | bytes 491528 | tf_op jit(solution)/shard_map/ppermute | solution.py:411
  30.2 16.7 %all-to-all-start = ((bf16[16,32,256]{2,1,0:T(8,128)(2,1)}), bf16[16,32,256]{2,1,0:T(8,128)(2,1)S(1)}, u32[]{:S(2)}, u32[]{:S(2)}) async-start(bf16[16,32,256]{2,1,0:T(8,128)(2,1)} %bitcast.5), calls=%async_computation | async-start | bytes 524288 | tf_op jit(solution)/shard_map/all_to_all | solution.py:494
  36.9 1.6 %collective-permute-start.5 = (bf16[8,32,512]{2,1,0:T(8,128)(2,1)S(1)}, bf16[8,32,512]{2,1,0:T(8,128)(2,1)S(1)}, u32[]{:S(2)}, u32[]{:S(2)}) collective-permute-start(bf16[8,32,512]{2,1,0:T(8,128)(2,1)S(1)} %bitcast.18), channel_id=1, source_target_pairs={{0,1},{1,0},{2,3},{3,2},{4,5},{5,4},{6,7},{7,6},{8,9},{9,8},{10,11... | collective-permute-start | bytes 786440 | tf_op jit(solution)/shard_map/ppermute | solution.py:411

commit v9 on v7

--- a/solution.py
+++ b/solution.py
@@ -342,13 +342,16 @@
         part = got[...]
         if group < rows:
             part = jnp.concatenate([part[d * rows + first : d * rows + first + group] for d in range(devices)], 0)
-        placed = dot(place[...], part)
+        step = 2 * blocks * group
+        placed = [
+            dot(place[h * step : (h + 1) * step, :], part[:, h * LANES : (h + 1) * LANES]) for h in range(kcount // 2)
+        ]
 
         def block(t):
             straight, turned = None, None
             for j in range(kcount):
-                at = (j * blocks + t) * group
-                piece = placed[at : at + group, j // 2 * LANES : (j // 2 + 1) * LANES]
+                at = (j % 2 * blocks + t) * group
+                piece = placed[j // 2][at : at + group]
                 if j % 2 == t % 2:
                     straight = piece if straight is None else straight + piece
                 else:

time: 48.3 us -> 48.3 us (level)
  no operation moved by 1% of the time
where the time goes in v9:
time: 48.3 us; the launch traced here: 48 us
  Pallas kernels  16.6 us (34%)
  starting transfers between devices  15.2 us (31%)
  waiting for transfers between devices  14.6 us (30%)
  between operations  0.84 us (2%)
    ppermute x6, starting transfers between devices, swap(): return lax.ppermute(array, axes, [(i, i ^ step) for i in range(count)])  8.62 us
    all_to_all x1, waiting for transfers between devices, shards(): lax.all_to_all(pieces.reshape(devices, out_rows, kcount * rows), everyone...  8.14 us
    all_to_all x1, starting transfers between devices, shards(): lax.all_to_all(pieces.reshape(devices, out_rows, kcount * rows), everyone...  6.61 us
    ppermute x6, waiting for transfers between devices, swap(): return lax.ppermute(array, axes, [(i, i ^ step) for i in range(count)])  6.43 us
    pallas_call x1, Pallas kernels, first_blocks(): pl.pallas_call(first_kernel, in_specs=[SMEM, SMEM, ANY] + [VMEM] * 4, out...  4.93 us
    pallas_call x1, Pallas kernels, corner(): pl.pallas_call(functools.partial(corner_kernel, step), in_specs=[SMEM, AN...  3.32 us
    pallas_call x2, Pallas kernels, pick(): pl.pallas_call(functools.partial(pick_kernel, step, riding), in_specs=[AN...  2.18 us
    pallas_call x1, Pallas kernels, next_block(): pl.pallas_call(next_kernel, in_specs=[VMEM] * 5, out_specs=[VMEM] * 5, ou...  2.09 us
  transfers between devices with their start and end apart: 7, of which 4 were waited for; matrix products, arithmetic and copies ran while one was open for 1% of the time, Pallas kernels for 30%

profile of v9, /device:TPU:0, one launch (start us, length us, event | category | flops | bytes accessed | tf_op | source)
XLA Modules:
  0.0 48.0 jit_solution(1530553662864739758)
XLA Ops:
  0.6 0.0 copy-start
  0.7 1.1 %pick.2 = (bf16[1,64,4352]{2,1,0:T(8,128)(2,1)S(1)}, bf16[16,128]{1,0:T(8,128)(2,1)S(1)}) custom-call(bf16[4,64,4096]{2,1,0:T(8,128)(2,1)} %bitcast.29, bf16[32,512]{1,0:T(8,128)(2,1)} %coulomb.1), custom_call_target="tpu_custom_call" | custom-call | tf_op jit(solution)/shard_map/pick/pallas_call | solution.py:96
  1.8 3.0 %collective-permute-start = (bf16[1,64,4352]{2,1,0:T(8,128)(2,1)S(1)}, bf16[1,64,4352]{2,1,0:T(8,128)(2,1)S(1)}, u32[]{:S(2)}, u32[]{:S(2)}) collective-permute-start(bf16[1,64,4352]{2,1,0:T(8,128)(2,1)S(1)} %get-tuple-element.23), channel_id=1, source_target_pairs={{0,2},{1,3},{2,0},{3,1},{4,6},{5,7},{6,4},{7,5},{8,10},{9,11},{10,... | collective-permute-start | bytes 1671176 | tf_op jit(solution)/shard_map/ppermute | solution.py:406
  4.8 1.1 %pick.3 = (bf16[1,64,4096]{2,1,0:T(8,128)(2,1)S(1)}, bf16[16,128]{1,0:T(8,128)(2,1)S(1)}) custom-call(bf16[4,64,4096]{2,1,0:T(8,128)(2,1)} %bitcast.30, bf16[16,128]{1,0:T(8,128)(2,1)S(1)} %get-tuple-element.24.refs_1_), custom_call_target="tpu_custom_call" | custom-call | tf_op jit(solution)/shard_map/pick/pallas_call | solution.py:96
  5.9 0.1 collective-permute-start.1
  6.0 0.0 copy-start.2
  6.0 3.3 %corner.1 = (bf16[1,64,4224]{2,1,0:T(8,128)(2,1)S(1)}, bf16[16,128]{1,0:T(8,128)(2,1)S(1)}) custom-call(s32[4]{0:T(128)S(1)} %copy-done.4, bf16[4,64,4096]{2,1,0:T(8,128)(2,1)} %bitcast.31, bf16[4,64,64]{2,1,0:T(8,128)(2,1)S(1)} %copy-done, bf16[4,64,64]{2,1,0:T(8,128)(2,1)S(1)} %copy-done.1, bf16[16,128]{1,0:T(8,128)(2,1)S(1)} %get-tuple-element.26.hold), custom_call_target="tpu_custom_call" | custom-call | tf_op jit(solution)/shard_map/corner/pallas_call | solution.py:218
  9.3 0.2 collective-permute-start.4
  9.5 0.0 copy-done.3
  9.5 0.2 select_reduce_fusion
  9.7 0.0 collective-permute-done.1.other
  9.7 4.9 %first_blocks.1 = (bf16[256,256]{1,0:T(8,128)(2,1)S(1)}, bf16[512,512]{1,0:T(8,128)(2,1)S(1)}, bf16[512,512]{1,0:T(8,128)(2,1)S(1)}, bf16[512,256]{1,0:T(8,128)(...) custom-call(s32[4]{0:T(128)S(1)} %copy-done.4, ...), custom_call_target="tpu_custom_call" | custom-call | tf_op jit(solution)/shard_map/first_blocks/pallas_call | solution.py:258
  14.7 3.6 %collective-permute-done.block = bf16[1,64,4352]{2,1,0:T(8,128)(2,1)S(1)} collective-permute-done((bf16[1,64,4352]{2,1,0:T(8,128)(2,1)S(1)}, bf16[1,64,4352]{2,1,0:T(8,128)(2,1)S(1)}, u32[]{:S(2)}, u32[]{:S(2)}) %collective-permute-start) | collective-permute-done | bytes 557088 | tf_op jit(solution)/shard_map/ppermute | solution.py:406
  18.2 0.0 copy-done.2
  18.3 3.2 %collective-permute-start.2 = (bf16[1,64,640]{2,1,0:T(8,128)(2,1)S(1)}, bf16[1,64,640]{2,1,0:T(8,128)(2,1)S(1)}, u32[]{:S(2)}, u32[]{:S(2)}) collective-permute-start(bf16[1,64,640]{2,1,0:T(8,128)(2,1)S(1)} %rows_along_x.1.own), channel_id=1, source_target_pairs={{0,8},{4,12},{8,0},{12,4},{1,9},{5,13},{9,1},{13,5},{2,10},{6,14},... | collective-permute-start | bytes 245768 | tf_op jit(solution)/shard_map/ppermute | solution.py:406
  21.5 2.1 %next_block.1 = (bf16[64,4096]{1,0:T(8,128)(2,1)S(1)}, bf16[64,4096]{1,0:T(8,128)(2,1)S(1)}, bf16[64,4096]{1,0:T(8,128)(2,1)S(1)}, bf16[64,4096]{1,0:T(8,128)(2,1)S(1)}, bf16[16,128]{1,0:T(8,128)(2,1)}) custom-call(bf16[1,64,4352]{2,1,0:T(8,128)(2,1)S(1)} %collective-permute-done.block, bf16[256,256]{1,0:T(8,128)(2,1)S(1)} %get-tuple-element.30.occ, ...), custom_call_target="tpu_custom_call" | custom-call | tf_op jit(solution)/shard_map/next_block/pallas_call | solution.py:279
  23.6 0.6 %inner_chi.1 = (bf16[192,256]{1,0:T(8,128)(2,1)S(1)}, bf16[16,128]{1,0:T(8,128)(2,1)S(1)}) custom-call(bf16[128,4096]{1,0:T(8,128)(2,1)S(1)} %get-tuple-element.29.refs_0_, bf16[64,4096]{1,0:T(8,128)(2,1)S(1)} %get-tuple-element.33.refs_1_, bf16[128,4096]{1,0:T(8,128)(2,1)S(1)} %get-tuple-element.34.refs_2_, bf16[64,4096]{1,0:T(8,128)(2,1)S(1)} %get-tuple-element.35.refs_3_), custom_call_target="tpu_custom_call" | custom-call | tf_op jit(solution)/shard_map/inner_chi/pallas_call | solution.py:298
  24.2 0.0 collective-permute-done.2.other
  24.2 1.7 %collective-permute-start.3 = (bf16[2,64,640]{2,1,0:T(8,128)(2,1)S(1)}, bf16[2,64,640]{2,1,0:T(8,128)(2,1)S(1)}, u32[]{:S(2)}, u32[]{:S(2)}) collective-permute-start(bf16[2,64,640]{2,1,0:T(8,128)(2,1)S(1)} %bitcast.27), channel_id=1, source_target_pairs={{0,4},{4,0},{8,12},{12,8},{1,5},{5,1},{9,13},{13,9},{2,6},{6,2},{1... | collective-permute-start | bytes 491528 | tf_op jit(solution)/shard_map/ppermute | solution.py:406
  25.9 2.4 %collective-permute-done.4.block = bf16[1,64,4224]{2,1,0:T(8,128)(2,1)S(1)} collective-permute-done((bf16[1,64,4224]{2,1,0:T(8,128)(2,1)S(1)}, bf16[1,64,4224]{2,1,0:T(8,128)(2,1)S(1)}, u32[]{:S(2)}, u32[]{:S(2)}) %collective-permute-start.4) | collective-permute-done | bytes 540704 | tf_op jit(solution)/shard_map/ppermute | solution.py:406
  28.3 1.9 %last_block.1 = bf16[512,256]{1,0:T(8,128)(2,1)} custom-call(bf16[1,64,4224]{2,1,0:T(8,128)(2,1)S(1)} %collective-permute-done.4.block, bf16[512,256]{1,0:T(8,128)(2,1)S(1)} %get-tuple-element.38.place, bf16[192,256]{1,0:T(8,128)(2,1)S(1)} %get-tuple-element.39.inner, bf16[128,4096]{1,0:T(8,128)(2,1)S(1)} %get-tuple-element.40.refs_0_, ...), custom_call_target="tpu_custom_call" | custom-call | tf_op jit(solution)/shard_map/last_block/pallas_call | solution.py:324
  30.2 6.6 %all-to-all-start = ((bf16[16,32,256]{2,1,0:T(8,128)(2,1)}), bf16[16,32,256]{2,1,0:T(8,128)(2,1)S(1)}, u32[]{:S(2)}, u32[]{:S(2)}) async-start(bf16[16,32,256]{2,1,0:T(8,128)(2,1)} %bitcast.7), calls=%async_computation | async-start | bytes 524288 | tf_op jit(solution)/shard_map/all_to_all | solution.py:494
  36.8 0.1 eq.39
  36.9 0.0 collective-permute-done.3.other
  37.0 0.5 collective-permute-start.5
  37.4 0.1 copy.10
  37.6 0.1 reshape.54
  37.7 0.1 compare_convert_fusion.hits
  37.7 0.4 placing.1.place
  38.1 0.5 %collective-permute-done.5.other = bf16[8,32,512]{2,1,0:T(8,128)(2,1)S(1)} collective-permute-done((bf16[8,32,512]{2,1,0:T(8,128)(2,1)S(1)}, bf16[8,32,512]{2,1,0:T(8,128)(2,1)S(1)}, u32[]{:S(2)}, u32[]{:S(2)}) %collective-permute-start.5) | collective-permute-done | bytes 262176 | tf_op jit(solution)/shard_map/ppermute | solution.py:406
  38.7 8.1 %all-to-all-done = bf16[16,32,256]{2,1,0:T(8,128)(2,1)S(1)} async-done(((bf16[16,32,256]{2,1,0:T(8,128)(2,1)}), bf16[16,32,256]{2,1,0:T(8,128)(2,1)S(1)}, u32[]{:S(2)}, u32[]{:S(2)}) %all-to-all-start) | async-done | bytes 262176 | tf_op jit(solution)/shard_map/all_to_all | solution.py:494
  46.8 1.1 %finish.1 = (f32[32,512]{1,0:T(8,128)}, f32[32,512]{1,0:T(8,128)}) custom-call(bf16[512,256]{1,0:T(8,128)(2,1)S(1)} %placing.1.place, bf16[512,256]{1,0:T(8,128)(2,1)S(1)} %bitcast.24, bf16[512,512]{1,0:T(8,128)(2,1)S(1)} %bitcast.20), custom_call_target="tpu_custom_call" | custom-call | tf_op jit(solution)/shard_map/finish/pallas_call | solution.py:372
  (18 shorter events, 0.2 us)
Async XLA Ops:
  0.6 5.3 %copy-start = (bf16[4,64,64]{2,1,0:T(8,128)(2,1)S(1)}, bf16[4,64,64]{2,1,0:T(8,128)(2,1)}, u32[]{:S(2)}) copy-start(bf16[4,64,64]{2,1,0:T(8,128)(2,1)} %occ.3) | copy-start | bytes 98308
  0.6 5.3 %copy-start.1 = (bf16[4,64,64]{2,1,0:T(8,128)(2,1)S(1)}, bf16[4,64,64]{2,1,0:T(8,128)(2,1)}, u32[]{:S(2)}) copy-start(bf16[4,64,64]{2,1,0:T(8,128)(2,1)} %virt.3) | copy-start | bytes 98308
  0.7 5.3 %copy-start.4 = (s32[4]{0:T(128)S(1)}, s32[4]{0:T(128)}, u32[]{:S(2)}) copy-start(s32[4]{0:T(128)} %sizes.3) | copy-start | bytes 52
  1.8 16.5 %collective-permute-start = (bf16[1,64,4352]{2,1,0:T(8,128)(2,1)S(1)}, bf16[1,64,4352]{2,1,0:T(8,128)(2,1)S(1)}, u32[]{:S(2)}, u32[]{:S(2)}) collective-permute-start(bf16[1,64,4352]{2,1,0:T(8,128)(2,1)S(1)} %get-tuple-element.23), channel_id=1, source_target_pairs={{0,2},{1,3},{2,0},{3,1},{4,6},{5,7},{6,4},{7,5},{8,10},{9,11},{10,... | collective-permute-start | bytes 1671176 | tf_op jit(solution)/shard_map/ppermute | solution.py:406
  4.8 4.7 %copy-start.3 = (s32[4,4]{1,0:T(4,128)S(1)}, s32[4,4]{1,0:T(4,128)}, u32[]{:S(2)}) copy-start(s32[4,4]{1,0:T(4,128)} %ids.1) | copy-start | bytes 196
  5.9 3.9 %collective-permute-start.1 = (bf16[1,64,4096]{2,1,0:T(8,128)(2,1)S(1)}, bf16[1,64,4096]{2,1,0:T(8,128)(2,1)S(1)}, u32[]{:S(2)}, u32[]{:S(2)}) collective-permute-start(bf16[1,64,4096]{2,1,0:T(8,128)(2,1)S(1)} %get-tuple-element.25), channel_id=1, source_target_pairs={{0,1},{1,0},{2,3},{3,2},{4,5},{5,4},{6,7},{7,6},{8,9},{9,8},{10,11... | collective-permute-start | bytes 1572872 | tf_op jit(solution)/shard_map/ppermute | solution.py:406
  6.0 12.3 %copy-start.2 = (bf16[32,512]{1,0:T(8,128)(2,1)S(1)}, bf16[32,512]{1,0:T(8,128)(2,1)}, u32[]{:S(2)}) copy-start(bf16[32,512]{1,0:T(8,128)(2,1)} %coulomb.1) | copy-start | bytes 98308
  9.3 18.9 %collective-permute-start.4 = (bf16[1,64,4224]{2,1,0:T(8,128)(2,1)S(1)}, bf16[1,64,4224]{2,1,0:T(8,128)(2,1)S(1)}, u32[]{:S(2)}, u32[]{:S(2)}) collective-permute-start(bf16[1,64,4224]{2,1,0:T(8,128)(2,1)S(1)} %get-tuple-element.37), channel_id=1, source_target_pairs={{0,3},{1,2},{2,1},{3,0},{4,7},{5,6},{6,5},{7,4},{8,11},{9,10},{10,... | collective-permute-start | bytes 1622024 | tf_op jit(solution)/shard_map/ppermute | solution.py:406
  18.3 5.9 %collective-permute-start.2 = (bf16[1,64,640]{2,1,0:T(8,128)(2,1)S(1)}, bf16[1,64,640]{2,1,0:T(8,128)(2,1)S(1)}, u32[]{:S(2)}, u32[]{:S(2)}) collective-permute-start(bf16[1,64,640]{2,1,0:T(8,128)(2,1)S(1)} %rows_along_x.1.own), channel_id=1, source_target_pairs={{0,8},{4,12},{8,0},{12,4},{1,9},{5,13},{9,1},{13,5},{2,10},{6,14},... | collective-permute-start | bytes 245768 | tf_op jit(solution)/shard_map/ppermute | solution.py:406
  24.2 12.7 %collective-permute-start.3 = (bf16[2,64,640]{2,1,0:T(8,128)(2,1)S(1)}, bf16[2,64,640]{2,1,0:T(8,128)(2,1)S(1)}, u32[]{:S(2)}, u32[]{:S(2)}) collective-permute-start(bf16[2,64,640]{2,1,0:T(8,128)(2,1)S(1)} %bitcast.27), channel_id=1, source_target_pairs={{0,4},{4,0},{8,12},{12,8},{1,5},{5,1},{9,13},{13,9},{2,6},{6,2},{1... | collective-permute-start | bytes 491528 | tf_op jit(solution)/shard_map/ppermute | solution.py:406
  30.2 16.7 %all-to-all-start = ((bf16[16,32,256]{2,1,0:T(8,128)(2,1)}), bf16[16,32,256]{2,1,0:T(8,128)(2,1)S(1)}, u32[]{:S(2)}, u32[]{:S(2)}) async-start(bf16[16,32,256]{2,1,0:T(8,128)(2,1)} %bitcast.7), calls=%async_computation | async-start | bytes 524288 | tf_op jit(solution)/shard_map/all_to_all | solution.py:494
  37.0 1.6 %collective-permute-start.5 = (bf16[8,32,512]{2,1,0:T(8,128)(2,1)S(1)}, bf16[8,32,512]{2,1,0:T(8,128)(2,1)S(1)}, u32[]{:S(2)}, u32[]{:S(2)}) collective-permute-start(bf16[8,32,512]{2,1,0:T(8,128)(2,1)S(1)} %bitcast.25), channel_id=1, source_target_pairs={{0,1},{1,0},{2,3},{3,2},{4,5},{5,4},{6,7},{7,6},{8,9},{9,8},{10,11... | collective-permute-start | bytes 786440 | tf_op jit(solution)/shard_map/ppermute | solution.py:406

commit v10 on v6

--- a/solution.py
+++ b/solution.py
@@ -357,8 +357,9 @@
 
         for t in range(0, blocks, 2):
             chi[first : first + group, t * width : (t + 2) * width] = jnp.where(low, block(t), block(t + 1))
+        ready = chi[first : first + group, :].astype(jnp.bfloat16)
+        screen[first : first + group, :] = dot(ready, metric[...])
     copies = started(sems, [(chi, chi_out)])
-    screen[...] = dot(chi[...].astype(jnp.bfloat16), metric[...])
     copies.append(pltpu.make_async_copy(screen, screen_out, sems.at[1]))
     copies[-1].start()
     finished(copies)

time: 48.3 us -> 48.5 us (level)
  no operation moved by 1% of the time
where the time goes in v10:
time: 48.5 us; the launch traced here: 48.2 us
  Pallas kernels  16.8 us (35%)
  starting transfers between devices  15.9 us (33%)
  waiting for transfers between devices  14 us (29%)
  between operations  0.83 us (2%)
    ppermute x6, starting transfers between devices, swap(): return lax.ppermute(array, axes, [(i, i ^ step) for i in range(count)])  9.27 us
    all_to_all x1, waiting for transfers between devices, shards(): lax.all_to_all(pieces.reshape(devices, out_rows, kcount * rows), everyone...  8.23 us
    all_to_all x1, starting transfers between devices, shards(): lax.all_to_all(pieces.reshape(devices, out_rows, kcount * rows), everyone...  6.61 us
    ppermute x6, waiting for transfers between devices, swap(): return lax.ppermute(array, axes, [(i, i ^ step) for i in range(count)])  5.79 us
    pallas_call x1, Pallas kernels, first_blocks(): pl.pallas_call(first_kernel, in_specs=[SMEM, SMEM, ANY] + [VMEM] * 4, out...  4.93 us
    pallas_call x1, Pallas kernels, corner(): pl.pallas_call(functools.partial(corner_kernel, step), in_specs=[SMEM, AN...  3.32 us
    pallas_call x2, Pallas kernels, pick(): pl.pallas_call(functools.partial(pick_kernel, step, riding), in_specs=[AN...  2.18 us
    pallas_call x1, Pallas kernels, next_block(): pl.pallas_call(next_kernel, in_specs=[VMEM] * 5, out_specs=[VMEM] * 5, ou...  2.09 us
  transfers between devices with their start and end apart: 7, of which 4 were waited for; matrix products, arithmetic and copies ran while one was open for 1% of the time, Pallas kernels for 30%

profile of v10, /device:TPU:0, one launch (start us, length us, event | category | flops | bytes accessed | tf_op | source)
XLA Modules:
  0.0 48.2 jit_solution(903844489194345589)
XLA Ops:
  0.6 0.0 copy-start
  0.6 0.0 copy-start.1
  0.7 0.0 copy-start.4
  0.7 1.1 %pick.2 = (bf16[1,64,4352]{2,1,0:T(8,128)(2,1)S(1)}, bf16[16,128]{1,0:T(8,128)(2,1)S(1)}) custom-call(bf16[4,64,4096]{2,1,0:T(8,128)(2,1)} %bitcast.22, bf16[32,512]{1,0:T(8,128)(2,1)} %coulomb.1), custom_call_target="tpu_custom_call" | custom-call | tf_op jit(solution)/shard_map/pick/pallas_call | solution.py:96
  1.8 3.0 %collective-permute-start = (bf16[1,64,4352]{2,1,0:T(8,128)(2,1)S(1)}, bf16[1,64,4352]{2,1,0:T(8,128)(2,1)S(1)}, u32[]{:S(2)}, u32[]{:S(2)}) collective-permute-start(bf16[1,64,4352]{2,1,0:T(8,128)(2,1)S(1)} %get-tuple-element.23), channel_id=1, source_target_pairs={{0,2},{1,3},{2,0},{3,1},{4,6},{5,7},{6,4},{7,5},{8,10},{9,11},{10,... | collective-permute-start | bytes 1671176 | tf_op jit(solution)/shard_map/ppermute | solution.py:404
  4.8 1.1 %pick.3 = (bf16[1,64,4096]{2,1,0:T(8,128)(2,1)S(1)}, bf16[16,128]{1,0:T(8,128)(2,1)S(1)}) custom-call(bf16[4,64,4096]{2,1,0:T(8,128)(2,1)} %bitcast.23, bf16[16,128]{1,0:T(8,128)(2,1)S(1)} %get-tuple-element.24.refs_1_), custom_call_target="tpu_custom_call" | custom-call | tf_op jit(solution)/shard_map/pick/pallas_call | solution.py:96
  5.9 0.1 collective-permute-start.1
  5.9 0.0 copy-done
  6.0 0.0 copy-start.2
  6.0 3.3 %corner.1 = (bf16[1,64,4224]{2,1,0:T(8,128)(2,1)S(1)}, bf16[16,128]{1,0:T(8,128)(2,1)S(1)}) custom-call(s32[4]{0:T(128)S(1)} %copy-done.4, bf16[4,64,4096]{2,1,0:T(8,128)(2,1)} %bitcast.24, bf16[4,64,64]{2,1,0:T(8,128)(2,1)S(1)} %copy-done, bf16[4,64,64]{2,1,0:T(8,128)(2,1)S(1)} %copy-done.1, bf16[16,128]{1,0:T(8,128)(2,1)S(1)} %get-tuple-element.26.hold), custom_call_target="tpu_custom_call" | custom-call | tf_op jit(solution)/shard_map/corner/pallas_call | solution.py:218
  9.3 0.2 collective-permute-start.4
  9.5 0.2 select_reduce_fusion
  9.7 0.0 collective-permute-done.1.other
  9.7 4.9 %first_blocks.1 = (bf16[256,256]{1,0:T(8,128)(2,1)S(1)}, bf16[512,512]{1,0:T(8,128)(2,1)S(1)}, bf16[512,512]{1,0:T(8,128)(2,1)S(1)}, bf16[512,256]{1,0:T(8,128)(...) custom-call(s32[4]{0:T(128)S(1)} %copy-done.4, ...), custom_call_target="tpu_custom_call" | custom-call | tf_op jit(solution)/shard_map/first_blocks/pallas_call | solution.py:258
  14.7 3.6 %collective-permute-done.block = bf16[1,64,4352]{2,1,0:T(8,128)(2,1)S(1)} collective-permute-done((bf16[1,64,4352]{2,1,0:T(8,128)(2,1)S(1)}, bf16[1,64,4352]{2,1,0:T(8,128)(2,1)S(1)}, u32[]{:S(2)}, u32[]{:S(2)}) %collective-permute-start) | collective-permute-done | bytes 557088 | tf_op jit(solution)/shard_map/ppermute | solution.py:404
  18.3 2.2 %collective-permute-start.2 = (bf16[1,64,640]{2,1,0:T(8,128)(2,1)S(1)}, bf16[1,64,640]{2,1,0:T(8,128)(2,1)S(1)}, u32[]{:S(2)}, u32[]{:S(2)}) collective-permute-start(bf16[1,64,640]{2,1,0:T(8,128)(2,1)S(1)} %rows_along_x.1.own), channel_id=1, source_target_pairs={{0,4},{4,0},{8,12},{12,8},{1,5},{5,1},{9,13},{13,9},{2,6},{6,2},{1... | collective-permute-start | bytes 245768 | tf_op jit(solution)/shard_map/ppermute | solution.py:404
  20.5 2.1 %next_block.1 = (bf16[64,4096]{1,0:T(8,128)(2,1)S(1)}, bf16[64,4096]{1,0:T(8,128)(2,1)S(1)}, bf16[64,4096]{1,0:T(8,128)(2,1)S(1)}, bf16[64,4096]{1,0:T(8,128)(2,1)S(1)}, bf16[16,128]{1,0:T(8,128)(2,1)}) custom-call(bf16[1,64,4352]{2,1,0:T(8,128)(2,1)S(1)} %collective-permute-done.block, bf16[256,256]{1,0:T(8,128)(2,1)S(1)} %get-tuple-element.30.occ, ...), custom_call_target="tpu_custom_call" | custom-call | tf_op jit(solution)/shard_map/next_block/pallas_call | solution.py:279
  22.6 0.6 %inner_chi.1 = (bf16[192,256]{1,0:T(8,128)(2,1)S(1)}, bf16[16,128]{1,0:T(8,128)(2,1)S(1)}) custom-call(bf16[128,4096]{1,0:T(8,128)(2,1)S(1)} %get-tuple-element.29.refs_0_, bf16[64,4096]{1,0:T(8,128)(2,1)S(1)} %get-tuple-element.33.refs_1_, bf16[128,4096]{1,0:T(8,128)(2,1)S(1)} %get-tuple-element.34.refs_2_, bf16[64,4096]{1,0:T(8,128)(2,1)S(1)} %get-tuple-element.35.refs_3_), custom_call_target="tpu_custom_call" | custom-call | tf_op jit(solution)/shard_map/inner_chi/pallas_call | solution.py:298
  23.2 0.0 collective-permute-done.2.other
  23.2 3.4 %collective-permute-start.3 = (bf16[2,64,640]{2,1,0:T(8,128)(2,1)S(1)}, bf16[2,64,640]{2,1,0:T(8,128)(2,1)S(1)}, u32[]{:S(2)}, u32[]{:S(2)}) collective-permute-start(bf16[2,64,640]{2,1,0:T(8,128)(2,1)S(1)} %bitcast.20), channel_id=1, source_target_pairs={{0,8},{4,12},{8,0},{12,4},{1,9},{5,13},{9,1},{13,5},{2,10},{6,14},... | collective-permute-start | bytes 491528 | tf_op jit(solution)/shard_map/ppermute | solution.py:404
  26.6 1.7 %collective-permute-done.4.block = bf16[1,64,4224]{2,1,0:T(8,128)(2,1)S(1)} collective-permute-done((bf16[1,64,4224]{2,1,0:T(8,128)(2,1)S(1)}, bf16[1,64,4224]{2,1,0:T(8,128)(2,1)S(1)}, u32[]{:S(2)}, u32[]{:S(2)}) %collective-permute-start.4) | collective-permute-done | bytes 540704 | tf_op jit(solution)/shard_map/ppermute | solution.py:404
  28.3 1.9 %last_block.1 = bf16[512,256]{1,0:T(8,128)(2,1)} custom-call(bf16[1,64,4224]{2,1,0:T(8,128)(2,1)S(1)} %collective-permute-done.4.block, bf16[512,256]{1,0:T(8,128)(2,1)S(1)} %get-tuple-element.38.place, bf16[192,256]{1,0:T(8,128)(2,1)S(1)} %get-tuple-element.39.inner, bf16[128,4096]{1,0:T(8,128)(2,1)S(1)} %get-tuple-element.40.refs_0_, ...), custom_call_target="tpu_custom_call" | custom-call | tf_op jit(solution)/shard_map/last_block/pallas_call | solution.py:324
  30.2 6.6 %all-to-all-start = ((bf16[16,32,256]{2,1,0:T(8,128)(2,1)}), bf16[16,32,256]{2,1,0:T(8,128)(2,1)S(1)}, u32[]{:S(2)}, u32[]{:S(2)}) async-start(bf16[16,32,256]{2,1,0:T(8,128)(2,1)} %bitcast.5), calls=%async_computation | async-start | bytes 524288 | tf_op jit(solution)/shard_map/all_to_all | solution.py:487
  36.8 0.0 collective-permute-done.3.other
  36.9 0.5 collective-permute-start.5
  37.4 0.1 eq.39
  37.5 0.1 copy.13
  37.5 0.1 compare_convert_fusion.hits
  37.6 0.4 placing.1.place
  38.0 0.5 %collective-permute-done.5.other = bf16[8,32,512]{2,1,0:T(8,128)(2,1)S(1)} collective-permute-done((bf16[8,32,512]{2,1,0:T(8,128)(2,1)S(1)}, bf16[8,32,512]{2,1,0:T(8,128)(2,1)S(1)}, u32[]{:S(2)}, u32[]{:S(2)}) %collective-permute-start.5) | collective-permute-done | bytes 262176 | tf_op jit(solution)/shard_map/ppermute | solution.py:404
  38.6 8.2 %all-to-all-done = bf16[16,32,256]{2,1,0:T(8,128)(2,1)S(1)} async-done(((bf16[16,32,256]{2,1,0:T(8,128)(2,1)}), bf16[16,32,256]{2,1,0:T(8,128)(2,1)S(1)}, u32[]{:S(2)}, u32[]{:S(2)}) %all-to-all-start) | async-done | bytes 262176 | tf_op jit(solution)/shard_map/all_to_all | solution.py:487
  46.8 1.3 %finish.1 = (f32[32,512]{1,0:T(8,128)}, f32[32,512]{1,0:T(8,128)}) custom-call(bf16[512,256]{1,0:T(8,128)(2,1)S(1)} %placing.1.place, bf16[512,256]{1,0:T(8,128)(2,1)S(1)} %bitcast.17, bf16[512,512]{1,0:T(8,128)(2,1)S(1)} %bitcast.13), custom_call_target="tpu_custom_call" | custom-call | tf_op jit(solution)/shard_map/finish/pallas_call | solution.py:370
  (17 shorter events, 0.2 us)
Async XLA Ops:
  0.6 5.3 %copy-start = (bf16[4,64,64]{2,1,0:T(8,128)(2,1)S(1)}, bf16[4,64,64]{2,1,0:T(8,128)(2,1)}, u32[]{:S(2)}) copy-start(bf16[4,64,64]{2,1,0:T(8,128)(2,1)} %occ.3) | copy-start | bytes 98308
  0.6 5.3 %copy-start.1 = (bf16[4,64,64]{2,1,0:T(8,128)(2,1)S(1)}, bf16[4,64,64]{2,1,0:T(8,128)(2,1)}, u32[]{:S(2)}) copy-start(bf16[4,64,64]{2,1,0:T(8,128)(2,1)} %virt.3) | copy-start | bytes 98308
  0.7 5.3 %copy-start.4 = (s32[4]{0:T(128)S(1)}, s32[4]{0:T(128)}, u32[]{:S(2)}) copy-start(s32[4]{0:T(128)} %sizes.3) | copy-start | bytes 52
  1.8 16.5 %collective-permute-start = (bf16[1,64,4352]{2,1,0:T(8,128)(2,1)S(1)}, bf16[1,64,4352]{2,1,0:T(8,128)(2,1)S(1)}, u32[]{:S(2)}, u32[]{:S(2)}) collective-permute-start(bf16[1,64,4352]{2,1,0:T(8,128)(2,1)S(1)} %get-tuple-element.23), channel_id=1, source_target_pairs={{0,2},{1,3},{2,0},{3,1},{4,6},{5,7},{6,4},{7,5},{8,10},{9,11},{10,... | collective-permute-start | bytes 1671176 | tf_op jit(solution)/shard_map/ppermute | solution.py:404
  4.8 4.7 %copy-start.3 = (s32[4,4]{1,0:T(4,128)S(1)}, s32[4,4]{1,0:T(4,128)}, u32[]{:S(2)}) copy-start(s32[4,4]{1,0:T(4,128)} %ids.1) | copy-start | bytes 196
  5.9 3.9 %collective-permute-start.1 = (bf16[1,64,4096]{2,1,0:T(8,128)(2,1)S(1)}, bf16[1,64,4096]{2,1,0:T(8,128)(2,1)S(1)}, u32[]{:S(2)}, u32[]{:S(2)}) collective-permute-start(bf16[1,64,4096]{2,1,0:T(8,128)(2,1)S(1)} %get-tuple-element.25), channel_id=1, source_target_pairs={{0,1},{1,0},{2,3},{3,2},{4,5},{5,4},{6,7},{7,6},{8,9},{9,8},{10,11... | collective-permute-start | bytes 1572872 | tf_op jit(solution)/shard_map/ppermute | solution.py:404
  6.0 12.3 %copy-start.2 = (bf16[32,512]{1,0:T(8,128)(2,1)S(1)}, bf16[32,512]{1,0:T(8,128)(2,1)}, u32[]{:S(2)}) copy-start(bf16[32,512]{1,0:T(8,128)(2,1)} %coulomb.1) | copy-start | bytes 98308
  9.3 18.9 %collective-permute-start.4 = (bf16[1,64,4224]{2,1,0:T(8,128)(2,1)S(1)}, bf16[1,64,4224]{2,1,0:T(8,128)(2,1)S(1)}, u32[]{:S(2)}, u32[]{:S(2)}) collective-permute-start(bf16[1,64,4224]{2,1,0:T(8,128)(2,1)S(1)} %get-tuple-element.37), channel_id=1, source_target_pairs={{0,3},{1,2},{2,1},{3,0},{4,7},{5,6},{6,5},{7,4},{8,11},{9,10},{10,... | collective-permute-start | bytes 1622024 | tf_op jit(solution)/shard_map/ppermute | solution.py:404
  18.3 4.9 %collective-permute-start.2 = (bf16[1,64,640]{2,1,0:T(8,128)(2,1)S(1)}, bf16[1,64,640]{2,1,0:T(8,128)(2,1)S(1)}, u32[]{:S(2)}, u32[]{:S(2)}) collective-permute-start(bf16[1,64,640]{2,1,0:T(8,128)(2,1)S(1)} %rows_along_x.1.own), channel_id=1, source_target_pairs={{0,4},{4,0},{8,12},{12,8},{1,5},{5,1},{9,13},{13,9},{2,6},{6,2},{1... | collective-permute-start | bytes 245768 | tf_op jit(solution)/shard_map/ppermute | solution.py:404
  23.2 13.6 %collective-permute-start.3 = (bf16[2,64,640]{2,1,0:T(8,128)(2,1)S(1)}, bf16[2,64,640]{2,1,0:T(8,128)(2,1)S(1)}, u32[]{:S(2)}, u32[]{:S(2)}) collective-permute-start(bf16[2,64,640]{2,1,0:T(8,128)(2,1)S(1)} %bitcast.20), channel_id=1, source_target_pairs={{0,8},{4,12},{8,0},{12,4},{1,9},{5,13},{9,1},{13,5},{2,10},{6,14},... | collective-permute-start | bytes 491528 | tf_op jit(solution)/shard_map/ppermute | solution.py:404
  30.2 16.7 %all-to-all-start = ((bf16[16,32,256]{2,1,0:T(8,128)(2,1)}), bf16[16,32,256]{2,1,0:T(8,128)(2,1)S(1)}, u32[]{:S(2)}, u32[]{:S(2)}) async-start(bf16[16,32,256]{2,1,0:T(8,128)(2,1)} %bitcast.5), calls=%async_computation | async-start | bytes 524288 | tf_op jit(solution)/shard_map/all_to_all | solution.py:487
  36.9 1.6 %collective-permute-start.5 = (bf16[8,32,512]{2,1,0:T(8,128)(2,1)S(1)}, bf16[8,32,512]{2,1,0:T(8,128)(2,1)S(1)}, u32[]{:S(2)}, u32[]{:S(2)}) collective-permute-start(bf16[8,32,512]{2,1,0:T(8,128)(2,1)S(1)} %bitcast.18), channel_id=1, source_target_pairs={{0,1},{1,0},{2,3},{3,2},{4,5},{5,4},{6,7},{7,6},{8,9},{9,8},{10,11... | collective-permute-start | bytes 786440 | tf_op jit(solution)/shard_map/ppermute | solution.py:404
